TPU v7x, 32 devices: a whole 2x2x4 slice. The times are simulated.
32 devices in a mesh: groups: 2 (over x), leaf: 16 (over z, y, core).
Axes of the slice: x: 2, y: 2, z: 4, core: 2. Of those that a mesh axis runs over, the one named last changes fastest.
Arguments:
- vectors: float32 [256, 32, 128], P(('groups', 'leaf')), parts along dimension 0, may hold values from -6 to 6
- near_index: int32 [256, 6], P(('groups', 'leaf')), parts along dimension 0, may hold values from 0 to 127, as said below
- near_block: float32 [256, 6, 128, 128], P(('groups', 'leaf')), parts along dimension 0, may hold values from -0.21875 to 0.21875
- basis: float32 [256, 128, 64], P(('groups', 'leaf')), parts along dimension 0, may hold values from -0.5 to 0.5
- far_index: int32 [256, 8], P(('groups', 'leaf')), parts along dimension 0, may hold values from 0 to 127, as said below
- far_coupling: float32 [256, 8, 64, 64], P(('groups', 'leaf')), parts along dimension 0, may hold values from -0.25 to 0.25
- transfer: float32 [256, 64, 64], P(('groups', 'leaf')), parts along dimension 0, may hold values from -0.25 to 0.25
- up_index: int32 [32, 8], P(('groups', 'leaf')), parts along dimension 0, may hold values from 0 to 15, as said below
- up_coupling: float32 [32, 8, 64, 64], P(('groups', 'leaf')), parts along dimension 0, may hold values from -0.25 to 0.25
Outputs:
- product: float32 [256, 32, 128], P(('groups', 'leaf')), parts along dimension 0
There are 2 independent parts, one for each index of `groups`. A program takes and returns all parts, laid end to end along the dimension named above; each array names one. Nothing has to cross between parts.
Inputs may be any that keep to these rules, and one draw needn't show every extreme that they name: near_index[l, 0] = l, and every leaf's list differs from l by at most 8; slot 1 differs by exactly 8. `far_index`: slot 2 of leaf l is (l + 64) mod 128; every other entry differs from l by 8 + 1 to 24; slot 0 by exactly 24, slot 1 by exactly 9. `up_index`: slot 2 of parent q is (q + 8) mod 16; every other entry differs from q by 1 + 1 to 3; slot 0 by exactly 3, slot 1 by exactly 2.
All inputs are finite; a program needn't handle non-finite values.
Results may differ from a plain program's by a relative error of at most 0.000057.
Values sent between devices are 32-bit elements; how exact they have to be, the bound alone decides.
No kernel may reach another device: no remote copies, remote signals or barrier semaphores. Data moves between devices by JAX's collectives and lax.ppermute only.
A program may use at most 64 MiB of HBM per device.

v0:
```python
import jax
import jax.numpy as jnp
from jax import lax
from jax.sharding import PartitionSpec as P

CHILD = 8


highest = lax.Precision.HIGHEST


def with_halo(x, sides, width):
    for axis, dim in sides:
        count, length = (lax.axis_size(axis), x.shape[dim])
        up = [(i, (i + 1) % count) for i in range(count - 1)]
        down = [(j, i) for i, j in up]
        last = lax.slice_in_dim(x, length - width, length, axis=dim)
        first = lax.slice_in_dim(x, 0, width, axis=dim)
        before = lax.ppermute(last, axis, up)
        after = lax.ppermute(first, axis, down)
        x = jnp.concatenate([before, x, after], axis=dim)
    return x


def per_device(
    vectors, near_index, near_block, basis, far_index, far_coupling, transfer, up_index, up_coupling
):
    leaf_dev = vectors.shape[0]
    offset_leaf = lax.axis_index("leaf") * leaf_dev
    leaf_coeffs = jnp.einsum("lvp,lpk->lvk", vectors, basis, precision=highest)
    blank_carry = jnp.zeros(far_index.shape + leaf_coeffs.shape[1:], jnp.float32)
    shard_piece = lax.all_gather(leaf_coeffs, "leaf", axis=0, tiled=True)
    inside = (far_index >= 0) & (far_index < shard_piece.shape[0])
    chosen_rows = jnp.take(shard_piece, jnp.clip(far_index, 0, shard_piece.shape[0] - 1), axis=0)
    selected = jnp.where(inside[:, :, None, None], chosen_rows, blank_carry)
    leaf_far = jnp.einsum("lsvk,lskm->lvm", selected, far_coupling, precision=highest)
    parents_here = leaf_dev // CHILD
    child_coeffs = leaf_coeffs.reshape(
        parents_here, CHILD, leaf_coeffs.shape[1], leaf_coeffs.shape[2]
    )
    child_transfer = transfer.reshape(parents_here, CHILD, transfer.shape[1], transfer.shape[2])
    parent_coeffs = jnp.einsum("pcvk,pckm->pvm", child_coeffs, child_transfer, precision=highest)
    parent_all = lax.all_gather(parent_coeffs, "leaf", axis=0, tiled=True)
    parent_rows = jnp.take(parent_all, up_index, axis=0)
    parent_far = jnp.einsum("psvk,pskm->pvm", parent_rows, up_coupling, precision=highest)
    downward = jnp.einsum("pvm,pckm->pcvk", parent_far, child_transfer, precision=highest).reshape(
        leaf_coeffs.shape
    )
    leaf_far = leaf_far + downward
    padded = with_halo(vectors, (("leaf", 0),), leaf_dev)
    near_inputs = jnp.take(padded, near_index - offset_leaf + leaf_dev, axis=0)
    near_field = jnp.einsum("lsvq,lspq->lvp", near_inputs, near_block, precision=highest)
    return near_field + jnp.einsum("lvk,lpk->lvp", leaf_far, basis, precision=highest)


def solution(mesh):
    placed = (
        P(("groups", "leaf"), None, None),
        P(("groups", "leaf"), None),
        P(("groups", "leaf"), None, None, None),
        P(("groups", "leaf"), None, None),
        P(("groups", "leaf"), None),
        P(("groups", "leaf"), None, None, None),
        P(("groups", "leaf"), None, None),
        P(("groups", "leaf"), None),
        P(("groups", "leaf"), None, None, None),
    )
    return jax.shard_map(
        per_device,
        mesh=mesh,
        in_specs=placed,
        out_specs=P(("groups", "leaf"), None, None),
        check_vma=False,
    )
```

profile of v0, /device:TPU:0, one launch (start us, length us, event | category | flops | bytes accessed | tf_op | source)
XLA Modules:
  0.0 73.6 jit_solution(16939762691682293150)
XLA Ops:
  6.5 0.0 copy-start
  6.5 0.0 all-gather.3.cloned.1.call-start
  6.5 3.3 %collective-permute-start = (f32[8,32,128]{2,1,0:T(8,128)}, f32[8,32,128]{2,1,0:T(8,128)}, u32[]{:S(2)}, u32[]{:S(2)}) collective-permute-start(f32[8,32,128]{2,1,0:T(8,128)} %param.9), channel_id=1, source_target_pairs={{0,1},{1,2},{2,3},{3,4},{4,5},{5,6},{6,7},{7,8},{8,9},{9,10},{10,1... | collective-permute-start | bytes 393224 | tf_op jit(solution)/shard_map/ppermute | solution.py:19
  9.8 1.3 %collective-permute-start.1 = (f32[8,32,128]{2,1,0:T(8,128)}, f32[8,32,128]{2,1,0:T(8,128)}, u32[]{:S(2)}, u32[]{:S(2)}) collective-permute-start(f32[8,32,128]{2,1,0:T(8,128)} %param.9), channel_id=1, source_target_pairs={{1,0},{2,1},{3,2},{4,3},{5,4},{6,5},{7,6},{8,7},{9,8},{10,9},{11,1... | collective-permute-start | bytes 393224 | tf_op jit(solution)/shard_map/ppermute | solution.py:20
  11.1 2.2 %fusion.20 = f32[8,32,64]{2,1,0:T(8,128)} fusion(f32[8,32,128]{2,1,0:T(8,128)} %param.9, f32[8,128,64]{1,2,0:T(8,128)} %param.12), kind=kOutput, calls=%fused_computation.39 | convolution fusion | flops 25165824 | bytes 458752 | tf_op jit(solution)/shard_map/lvp,lpk->lvk/dot_general | solution.py:30
  13.3 0.0 all-gather.3.cloned.1.call-update
  13.3 0.7 compare_select_fusion
  14.0 0.7 fusion.19
  14.7 1.3 %convolution_bitcast_fusion.3 = f32[32,64]{1,0:T(8,128)S(1)} fusion(f32[8,32,64]{2,1,0:T(8,128)} %fusion.20, f32[8,64,64]{2,1,0:T(8,128)} %param.15), kind=kOutput, calls=%fused_computation.8 | convolution fusion | flops 12582912 | bytes 204800 | tf_op jit(solution)/shard_map/pcvk,pckm->pvm/dot_general | solution.py:42
  16.0 0.6 reshape.55
  16.6 26.8 %all-gather = f32[512,64]{1,0:T(8,128)} all-gather(f32[32,64]{1,0:T(8,128)S(1)} %convolution_bitcast_fusion.3), channel_id=2, replica_groups=mesh['groups'=2,'leaf'=16] {'leaf'}, dimensions={0}, use_global_device_ids=true | all-gather | bytes 139264 | tf_op jit(solution)/shard_map/all_gather | solution.py:43
  43.4 1.5 %gather_fusion.2 = f32[8,32,64]{2,1,0:T(8,128)S(1)} fusion(f32[16,32,64]{2,1,0:T(8,128)} %bitcast.41, s32[1024]{0:T(1024)S(1)} %pad_clamp_fusion), kind=kCustom, calls=%fused_computation.2 | custom fusion | bytes 131104 | tf_op jit(solution)/shard_map/jit(_take)/gather | solution.py:44
  44.9 0.7 and_bitcast_fusion
  45.6 1.3 %compare_and_fusion.1 = (pred[8,8]{1,0:T(8,128)(4,1)S(1)}, pred[8,8]{1,0:T(8,128)(4,1)}) fusion(s32[8,8]{1,0:T(8,128)} %param.13), kind=kLoop, calls=%fused_computation.30 | loop fusion | flops 640 | bytes 384 | tf_op jit(solution)/shard_map/and | solution.py:33
  46.9 0.7 compare_and_fusion.2
  47.6 1.3 %fusion.10 = f32[32,64,1]{1,0,2:T(8,128)S(1)} fusion(f32[1,8,64,64]{3,2,1,0:T(8,128)} %param.17, f32[8,32,64]{2,1,0:T(8,128)S(1)} %gather_fusion.2, pred[8]{0:T(512)(128)(4,1)S(1)} %and_bitcast_fusion), kind=kOutput, calls=%fused_computation.19 | convolution fusion | flops 12599296 | bytes 204808 | tf_op jit(solution)/shard_map/psvk,pskm->pvm/dot_general | solution.py:45
  48.9 0.0 copy-done.1
  48.9 1.5 %convolution_bitcast_fusion = f32[8,32,64]{2,1,0:T(8,128)} fusion(f32[32,64,1]{1,0,2:T(8,128)S(1)} %fusion.10, f32[8,64,64]{2,1,0:T(8,128)S(1)} %copy-done.1), kind=kOutput, calls=%fused_computation.4 | convolution fusion | flops 12582912 | bytes 204800 | tf_op jit(solution)/shard_map/pvm,pckm->pcvk/dot_general | solution.py:46
  50.4 0.6 pad_clamp_fusion.1
  51.0 0.1 reshape.47
  51.1 0.0 collective-permute-done
  51.1 0.0 collective-permute-done.1
  51.1 1.1 %pad_maximum_fusion = f32[24,32,128]{2,1,0:T(8,128)S(1)} fusion(f32[8,32,128]{2,1,0:T(8,128)} %collective-permute-done.1, f32[8,32,128]{2,1,0:T(8,128)} %param.9, f32[8,32,128]{2,1,0:T(8,128)} %collective-permute-done), kind=kLoop, calls=%fused_computation.16 | loop fusion | flops 196608 | bytes 786432 | tf_op jit(solution)/shard_map/concatenate | solution.py:21
  52.2 1.5 %gather_fusion = f32[48,32,128]{2,1,0:T(8,128)} fusion(f32[24,32,128]{2,1,0:T(8,128)S(1)} %pad_maximum_fusion, s32[1024]{0:T(1024)S(1)} %pad_clamp_fusion.2), kind=kCustom, calls=%fused_computation | custom fusion | bytes 1573056 | tf_op jit(solution)/shard_map/jit(_take)/gather | solution.py:51
  53.7 0.0 copy-done
  53.7 4.5 %convolution_bitcast_fusion.2 = f32[8,32,128]{2,1,0:T(8,128)S(1)} fusion(f32[8,6,128,128]{3,2,1,0:T(8,128)S(1)} %copy-done, f32[8,6,32,128]{3,2,1,0:T(8,128)} %bitcast.40, pred[8,6]{1,0:T(8,128)(4,1)S(1)} %get-tuple-element.5), kind=kOutput, calls=%fused_computation.7 | convolution fusion | flops 302186496 | bytes 4063280 | tf_op jit(solution)/shard_map/lsvq,lspq->lvp/dot_general | solution.py:52
  58.1 0.9 %all-gather.3.cloned.1.call-done = f32[128,32,64]{2,1,0:T(8,128)} async-done(((f32[8,32,64]{2,1,0:T(8,128)}), f32[128,32,64]{2,1,0:T(8,128)}) %all-gather.3.cloned.1.call-update) | async-done | bytes 1048592 | tf_op jit(solution)/shard_map/all_gather | solution.py:32
  59.1 3.2 %gather_fusion.1 = f32[64,32,64]{2,1,0:T(8,128)} fusion(f32[128,32,64]{2,1,0:T(8,128)} %all-gather.3.cloned.1.call-done, s32[1024]{0:T(1024)S(1)} %pad_clamp_fusion.1), kind=kCustom, calls=%fused_computation.1 | custom fusion | bytes 1048832 | tf_op jit(solution)/shard_map/jit(_take)/gather | solution.py:34
  62.3 0.0 copy-done.3
  62.3 0.0 copy-done.4
  62.3 3.5 %fusion = f32[8,32,64]{2,1,0:T(8,128)S(1)} fusion(f32[8,32,64]{2,1,0:T(8,128)S(1)} %copy-done.3, f32[8,8,64,64]{3,2,1,0:T(8,128)} %param.14, f32[8,8,32,64]{3,2,1,0:T(8,128)} %bitcast.39, pred[8,8]{1,0:T(8,128)(4,1)S(1)} %copy-done.4, pred[8,8]{1,0:T(8,128)(4,1)S(1)} %get-tuple-element.7), kind=kOutput, calls=%fused_computation.6 | convolution fusion | flops 100941824 | bytes 1704064 | tf_op jit(solution)/shard_map/lsvk,lskm->lvm/dot_general | solution.py:36
  65.7 1.0 %convolution_add_fusion = f32[8,32,128]{2,1,0:T(8,128)} fusion(f32[8,32,128]{2,1,0:T(8,128)S(1)} %convolution_bitcast_fusion.2, f32[8,32,64]{2,1,0:T(8,128)S(1)} %fusion, f32[8,128,64]{1,2,0:T(8,128)S(1)} %copy-done.2), kind=kOutput, calls=%fused_computation.3 | convolution fusion | flops 25198592 | bytes 589824 | tf_op jit(solution)/shard_map/lvk,lpk->lvp/dot_general | solution.py:53
  (7 shorter events, 0.0 us)
Async XLA Ops:
  6.5 47.1 %copy-start = (f32[8,6,128,128]{3,2,1,0:T(8,128)S(1)}, f32[8,6,128,128]{3,2,1,0:T(8,128)}, u32[]{:S(2)}) copy-start(f32[8,6,128,128]{3,2,1,0:T(8,128)} %param.11) | copy-start | bytes 9437188
  6.5 42.4 %copy-start.1 = (f32[8,64,64]{2,1,0:T(8,128)S(1)}, f32[8,64,64]{2,1,0:T(8,128)}, u32[]{:S(2)}) copy-start(f32[8,64,64]{2,1,0:T(8,128)} %param.15) | copy-start | bytes 393220
  6.5 52.5 %all-gather.3.cloned.1.call-start = ((), (), s32[]{:S(2)}) async-start(), calls=%async_computation | async-start | bytes 2228224 | tf_op jit(solution)/shard_map/all_gather | solution.py:32
  6.5 44.6 %collective-permute-start = (f32[8,32,128]{2,1,0:T(8,128)}, f32[8,32,128]{2,1,0:T(8,128)}, u32[]{:S(2)}, u32[]{:S(2)}) collective-permute-start(f32[8,32,128]{2,1,0:T(8,128)} %param.9), channel_id=1, source_target_pairs={{0,1},{1,2},{2,3},{3,4},{4,5},{5,6},{6,7},{7,8},{8,9},{9,10},{10,1... | collective-permute-start | bytes 393224 | tf_op jit(solution)/shard_map/ppermute | solution.py:19
  9.8 41.3 %collective-permute-start.1 = (f32[8,32,128]{2,1,0:T(8,128)}, f32[8,32,128]{2,1,0:T(8,128)}, u32[]{:S(2)}, u32[]{:S(2)}) collective-permute-start(f32[8,32,128]{2,1,0:T(8,128)} %param.9), channel_id=1, source_target_pairs={{1,0},{2,1},{3,2},{4,3},{5,4},{6,5},{7,6},{8,7},{9,8},{10,9},{11,1... | collective-permute-start | bytes 393224 | tf_op jit(solution)/shard_map/ppermute | solution.py:20
  53.7 8.6 %copy-start.3 = (f32[8,32,64]{2,1,0:T(8,128)S(1)}, f32[8,32,64]{2,1,0:T(8,128)}, u32[]{:S(2)}) copy-start(f32[8,32,64]{2,1,0:T(8,128)} %convolution_bitcast_fusion) | copy-start | bytes 196612
  53.7 8.6 %copy-start.4 = (pred[8,8]{1,0:T(8,128)(4,1)S(1)}, pred[8,8]{1,0:T(8,128)(4,1)}, u32[]{:S(2)}) copy-start(pred[8,8]{1,0:T(8,128)(4,1)} %get-tuple-element.8) | copy-start | bytes 196
  62.3 3.5 %copy-start.2 = (f32[8,128,64]{1,2,0:T(8,128)S(1)}, f32[8,128,64]{1,2,0:T(8,128)}, u32[]{:S(2)}) copy-start(f32[8,128,64]{1,2,0:T(8,128)} %param.12) | copy-start | bytes 786436
Sparse Core Ops, SparseCore 0:
  13.4 45.5 all-gather.2
where the time goes:
time: 74.1 us; the launch traced here: 73.6 us
  blocking collectives  26.8 us (36%)
  matrix products  15.2 us (21%)
  between operations  13.5 us (18%)
  local copies, waits for them, and re-layouts  6.91 us (9%)
  other arithmetic  5.72 us (8%)
  starting transfers between devices  4.54 us (6%)
  waiting for transfers between devices  0.94 us (1%)
    all_gather x1, blocking collectives, per_device(): parent_all = lax.all_gather(parent_coeffs, 'leaf', axis=0, tiled=True)  26.8 us
    dot_general x1, matrix products, per_device(): jnp.einsum('lsvq,lspq->lvp', near_inputs, near_block, precision=highest)  4.46 us
    dot_general x1, matrix products, per_device(): jnp.einsum('lsvk,lskm->lvm', selected, far_coupling, precision=highest)  3.47 us
    ppermute x1, starting transfers between devices, with_halo(): before = lax.ppermute(last, axis, up)  3.26 us
    gather x1, local copies, waits for them, and re-layouts, per_device(): jnp.take(shard_piece, jnp.clip(far_index, 0, shard_piece.shape[0] - 1), a...  3.19 us
    dot_general x1, matrix products, per_device(): leaf_coeffs = jnp.einsum('lvp,lpk->lvk', vectors, basis, precision=highest)  2.2 us
    gather x1, local copies, waits for them, and re-layouts, per_device(): parent_rows = jnp.take(parent_all, up_index, axis=0)  1.5 us
    gather x1, local copies, waits for them, and re-layouts, per_device(): near_inputs = jnp.take(padded, near_index - offset_leaf + leaf_dev, axis=0)  1.49 us
  transfers between devices with their start and end apart: 3, of which 1 were waited for; matrix products, arithmetic and copies ran while one was open for 27% of the time, Pallas kernels for 0%

commit v1 on v0

v1 whole, which is shorter than its diff:
```python
import functools

import jax
import jax.numpy as jnp
from jax import lax
from jax.experimental import pallas as pl
from jax.experimental.pallas import tpu as pltpu
from jax.sharding import PartitionSpec as P

REACH = 3
F32 = jnp.float32
NN = (((1,), (0,)), ((), ()))
NT = (((1,), (1,)), ((), ()))
VMEM = pl.BlockSpec(memory_space=pltpu.VMEM)
SMEM = pl.BlockSpec(memory_space=pltpu.SMEM)


def split(x):
    high = x.astype(jnp.bfloat16)
    return high, (x - high.astype(F32)).astype(jnp.bfloat16)


def dot(x, y, dims):
    xh, xl = split(x)
    yh, yl = split(y)
    mul = functools.partial(lax.dot_general, dimension_numbers=dims, preferred_element_type=F32)
    return mul(xh, yh) + (mul(xl, yh) + mul(xh, yl))


def pack(x):
    half = x.shape[0] // 2
    return jnp.concatenate([x[:half], x[half:]], axis=1)


def coeffs_kernel(vectors, basis, transfer, sent, coeffs):
    leaves, rows, points = vectors.shape
    rank = basis.shape[2]
    half = rows // 2
    base = leaves * rows
    parts = []
    for l in range(leaves):
        own = vectors[l]
        sent[l * rows : (l + 1) * rows] = own
        parts.append(dot(own, basis[l], NN))
    whole = jnp.concatenate(parts, axis=1)
    parts.append(dot(whole, transfer[...].reshape(leaves * rank, rank), NN))
    for i, part in enumerate(parts):
        packed = pack(part)
        coeffs[i * half : (i + 1) * half] = packed
        sent[base + i * half : base + (i + 1) * half] = packed


def place(index, here, side):
    away = (index - here) * side
    return jnp.where(jnp.abs(away) <= REACH, away + REACH, 2 * REACH + 1)


def near_kernel(near_index, vectors, near_block, beside, across, near, held):
    leaves, slots = near_index.shape
    rows = vectors.shape[1]
    here = lax.axis_index("leaf")
    side = 1 - 2 * lax.rem(here, 2)
    for l in range(leaves):
        held[l] = across[l * rows : (l + 1) * rows]
        held[leaves + l] = vectors[l]
        held[2 * leaves + l] = beside[l * rows : (l + 1) * rows]
    for l in range(leaves):
        chosen = []
        for s in range(slots):
            index = near_index[l, s]
            device = lax.div(index, leaves)
            away = (device - here) * side
            chosen.append(held[(away + 1) * leaves + (index - device * leaves)])
        inputs = jnp.concatenate(chosen, axis=1)
        blocks = jnp.concatenate([near_block[l, s] for s in range(slots)], axis=1)
        near[l] = dot(inputs, blocks, NT)


def far_kernel(
    far_index, up_index, near, own, beside, across, second, third, opposite, second_beside, third_beside,
    far_coupling, up_coupling, transfer, basis, product, held,
):
    leaves, rows, points = near.shape
    rank = basis.shape[2]
    half = rows // 2
    slots = far_index.shape[1]
    here = lax.axis_index("leaf")
    side = 1 - 2 * lax.rem(here, 2)
    left = lax.broadcasted_iota(jnp.int32, (half, 2 * rank), 1) < rank
    left_all = lax.broadcasted_iota(jnp.int32, (rows, 2 * rank), 1) < rank
    base = leaves * rows
    sources = (third, second, across, own, beside, second_beside, third_beside, opposite)
    for k, source in enumerate(sources):
        skip = source.shape[0] - (leaves + 1) * half
        for i in range(leaves + 1):
            x = source[skip + i * half : skip + (i + 1) * half]
            turned = pltpu.roll(x, rank, 1)
            held[k * (leaves + 1) + i, :half] = jnp.where(left, x, turned)
            held[k * (leaves + 1) + i, half:] = jnp.where(left, turned, x)

    def chosen(u, s):
        if u < leaves:
            index = far_index[u, s]
            device = lax.div(index, leaves)
            return held[place(device, here, side) * (leaves + 1) + (index - device * leaves)]
        return held[place(up_index[0, s], here, side) * (leaves + 1) + leaves]

    def far(u, coupling):
        inputs = [jnp.where(left_all, chosen(u, s), chosen(u, s + 1)) for s in range(0, slots, 2)]
        return dot(jnp.concatenate(inputs, axis=1), coupling.reshape(slots * rank, rank), NN)

    parent_far = far(leaves, up_coupling[0])
    down = dot(parent_far, transfer[...].reshape(leaves * rank, rank), NT)
    for l in range(leaves):
        leaf_far = far(l, far_coupling[l]) + down[:, l * rank : (l + 1) * rank]
        product[l] = near[l] + dot(leaf_far, basis[l], NT)


def routes(groups, count):
    last = count - 1

    def mirrored(step):
        wanted = [(i - step, i) if i % 2 == 0 else (i + step, i) for i in range(count)]
        return [(j, i) for j, i in wanted if 0 <= j <= last]

    def everywhere(pairs):
        return [(g * count + j, g * count + i) for g in range(groups) for j, i in pairs]

    beside = everywhere([(i, i ^ 1) for i in range(count)])
    across = everywhere(mirrored(1))
    if groups > 1:
        across += [(g * count + i, (g + 1) % groups * count + i) for g in range(groups) for i in (0, last)]
    second = everywhere(mirrored(2) + [(1, 0), (last - 1, last)])
    third = everywhere(mirrored(3) + [(0, 2), (2, 0), (last, last - 2), (last - 2, last)])
    opposite = everywhere([(i, (i + count // 2) % count) for i in range(count)])
    return beside, across, second, third, opposite


def per_device(
    groups, vectors, near_index, near_block, basis, far_index, far_coupling, transfer, up_index, up_coupling
):
    leaves, rows, points = vectors.shape
    rank = basis.shape[2]
    packed = (leaves + 1) * rows // 2
    beside_to, across_to, second_to, third_to, opposite_to = routes(groups, lax.axis_size("leaf"))

    def send(x, to):
        return lax.ppermute(x, ("groups", "leaf"), to)

    sent, own = pl.pallas_call(
        coeffs_kernel,
        out_shape=(
            jax.ShapeDtypeStruct((leaves * rows + packed, points), F32),
            jax.ShapeDtypeStruct((packed, points), F32),
        ),
        in_specs=[VMEM] * 3,
        out_specs=(VMEM, VMEM),
    )(vectors, basis, transfer)
    across = send(sent, across_to)
    beside = send(sent, beside_to)
    opposite = send(own, opposite_to)
    third = send(own, third_to)
    second = send(own, second_to)
    second_beside = send(across, beside_to)
    third_beside = send(second, beside_to)
    near = pl.pallas_call(
        near_kernel,
        out_shape=jax.ShapeDtypeStruct(vectors.shape, F32),
        in_specs=[SMEM] + [VMEM] * 4,
        out_specs=VMEM,
        scratch_shapes=[pltpu.VMEM((3 * leaves, rows, points), F32)],
    )(near_index, vectors, near_block, beside, across)
    return pl.pallas_call(
        far_kernel,
        out_shape=jax.ShapeDtypeStruct(vectors.shape, F32),
        in_specs=[SMEM] * 2 + [VMEM] * 13,
        out_specs=VMEM,
        scratch_shapes=[pltpu.VMEM(((2 * REACH + 2) * (leaves + 1), rows, points), F32)],
    )(
        far_index, up_index, near, own, beside, across, second, third, opposite, second_beside, third_beside,
        far_coupling, up_coupling, transfer, basis,
    )


def solution(mesh):
    placed = (
        P(("groups", "leaf"), None, None),
        P(("groups", "leaf"), None),
        P(("groups", "leaf"), None, None, None),
        P(("groups", "leaf"), None, None),
        P(("groups", "leaf"), None),
        P(("groups", "leaf"), None, None, None),
        P(("groups", "leaf"), None, None),
        P(("groups", "leaf"), None),
        P(("groups", "leaf"), None, None, None),
    )
    return jax.shard_map(
        functools.partial(per_device, mesh.shape["groups"]),
        mesh=mesh,
        in_specs=placed,
        out_specs=P(("groups", "leaf"), None, None),
        check_vma=False,
    )
```

time: 74.1 us -> 30.3 us (0.41)
  blocking collectives: 26.8 us -> 0 us
  matrix products: 15.2 us -> 0 us
  between operations: 13.5 us -> 0.08 us
  Pallas kernels: 0 us -> 11.3 us
  starting transfers between devices: 4.54 us -> 10.8 us
  other arithmetic: 5.72 us -> 0 us
  local copies, waits for them, and re-layouts: 6.91 us -> 3.93 us
  waiting for transfers between devices: 0.94 us -> 3.82 us
    all_gather x1 -> x0, blocking collectives: 26.8 us -> none  [per_device(): parent_all = lax.all_gather(parent_coeffs, 'leaf', axis=0, tiled=True)]
    dot_general x7 -> x0, matrix products: 15.2 us -> none  [the longest x1 4.46 us: per_device(): jnp.einsum('lsvq,lspq->lvp', near_inputs, near_block, precision=highest)]
    pallas_call x0 -> x3, Pallas kernels: none -> 11.3 us  [the longest x1 4.55 us: per_device(): pl.pallas_call(far_kernel, out_shape=jax.ShapeDtypeStruct(vectors.shape,...]
    ppermute x2 -> x7, starting transfers between devices: 4.54 us -> 10.8 us  [send(): return lax.ppermute(x, ('groups', 'leaf'), to)]
    gather x3 -> x0, local copies, waits for them, and re-layouts: 6.19 us -> none  [the longest x1 3.19 us: per_device(): jnp.take(shard_piece, jnp.clip(far_index, 0, shard_piece.shape[0] - 1), a...]
    unnamed x10 -> x15, local copies, waits for them, and re-layouts: 0.02 us -> 3.93 us
    ppermute x2 -> x7, waiting for transfers between devices: 0.01 us -> 3.82 us  [send(): return lax.ppermute(x, ('groups', 'leaf'), to)]
    and x2 -> x0, other arithmetic: 1.98 us -> none  [the longest x1 1.28 us: per_device(): inside = (far_index >= 0) & (far_index < shard_piece.shape[0])]
  transfers between devices with their start and end apart: 3 -> 7, of which waited for: 1 -> 1; matrix products, arithmetic and copies ran while one was open for 27% -> 0% of each run, Pallas kernels for 0% -> 14%
where the time goes in v1:
time: 30.3 us; the launch traced here: 29.9 us
  Pallas kernels  11.3 us (37%)
  starting transfers between devices  10.8 us (36%)
  local copies, waits for them, and re-layouts  3.93 us (13%)
  waiting for transfers between devices  3.82 us (13%)
    ppermute x7, starting transfers between devices, send(): return lax.ppermute(x, ('groups', 'leaf'), to)  10.8 us
    pallas_call x1, Pallas kernels, per_device(): pl.pallas_call(far_kernel, out_shape=jax.ShapeDtypeStruct(vectors.shape,...  4.55 us
    pallas_call x1, Pallas kernels, per_device(): pl.pallas_call(near_kernel, out_shape=jax.ShapeDtypeStruct(vectors.shape,...  4.3 us
    unnamed x15, local copies, waits for them, and re-layouts  3.93 us
    ppermute x7, waiting for transfers between devices, send(): return lax.ppermute(x, ('groups', 'leaf'), to)  3.82 us
    pallas_call x1, Pallas kernels, per_device(): pl.pallas_call(coeffs_kernel, out_shape=(jax.ShapeDtypeStruct((leaves * r...  2.47 us
  transfers between devices with their start and end apart: 7, of which 1 were waited for; matrix products, arithmetic and copies ran while one was open for 0% of the time, Pallas kernels for 14%

profile of v1, /device:TPU:0, one launch (start us, length us, event | category | flops | bytes accessed | tf_op | source)
XLA Modules:
  0.0 29.9 jit_solution(788615112832243273)
XLA Ops:
  0.0 1.9 %copy.10.basis = f32[8,128,64]{2,1,0:T(8,128)} copy(f32[8,128,64]{1,2,0:T(8,128)} %param.12) | data formatting | bytes 524288 | tf_op args[3]
  1.9 2.5 %shard_map.91 = (f32[400,128]{1,0:T(8,128)}, f32[144,128]{1,0:T(8,128)}) custom-call(f32[8,32,128]{2,1,0:T(8,128)} %vectors.3, f32[8,128,64]{2,1,0:T(8,128)} %copy.10.basis, f32[8,64,64]{2,1,0:T(8,128)} %transfer.3), custom_call_target="tpu_custom_call" | custom-call | tf_op jit(solution)/shard_map/pallas_call | solution.py:150
  4.4 2.9 %collective-permute-start.1 = (f32[400,128]{1,0:T(8,128)}, f32[400,128]{1,0:T(8,128)S(1)}, u32[]{:S(2)}, u32[]{:S(2)}) collective-permute-start(f32[400,128]{1,0:T(8,128)} %get-tuple-element.7), channel_id=1, source_target_pairs={{2,1},{1,2},{4,3},{3,4},{6,5},{5,6},{8,7},{7,8},{10,9},{9,10},{12,... | collective-permute-start | bytes 614408 | tf_op jit(solution)/shard_map/ppermute | solution.py:148
  7.4 0.1 collective-permute-start
  7.5 3.8 %collective-permute-done.1.across = f32[400,128]{1,0:T(8,128)S(1)} collective-permute-done((f32[400,128]{1,0:T(8,128)}, f32[400,128]{1,0:T(8,128)S(1)}, u32[]{:S(2)}, u32[]{:S(2)}) %collective-permute-start.1) | collective-permute-done | bytes 204832 | tf_op jit(solution)/shard_map/ppermute | solution.py:148
  11.3 0.0 copy-start
  11.3 1.4 %collective-permute-start.5 = (f32[400,128]{1,0:T(8,128)S(1)}, f32[400,128]{1,0:T(8,128)S(1)}, u32[]{:S(2)}, u32[]{:S(2)}) collective-permute-start(f32[400,128]{1,0:T(8,128)S(1)} %collective-permute-done.1.across), channel_id=1, source_target_pairs={{0,1},{1,0},{2,3},{3,2},{4,5},{5,4},{6,7},{7,6},{8,9},{9,8},{10,11... | collective-permute-start | bytes 614408 | tf_op jit(solution)/shard_map/ppermute | solution.py:148
  12.7 2.3 %collective-permute-start.2 = (f32[144,128]{1,0:T(8,128)}, f32[144,128]{1,0:T(8,128)S(1)}, u32[]{:S(2)}, u32[]{:S(2)}) collective-permute-start(f32[144,128]{1,0:T(8,128)} %get-tuple-element.8.own), channel_id=1, source_target_pairs={{3,1},{0,2},{5,3},{2,4},{7,5},{4,6},{9,7},{6,8},{11,9},{8,10},{13,... | collective-permute-start | bytes 221192 | tf_op jit(solution)/shard_map/ppermute | solution.py:148
  15.0 2.6 %collective-permute-start.4 = (f32[144,128]{1,0:T(8,128)}, f32[144,128]{1,0:T(8,128)S(1)}, u32[]{:S(2)}, u32[]{:S(2)}) collective-permute-start(f32[144,128]{1,0:T(8,128)} %get-tuple-element.8.own), channel_id=1, source_target_pairs={{0,8},{1,9},{2,10},{3,11},{4,12},{5,13},{6,14},{7,15},{8,0},{9,1},... | collective-permute-start | bytes 221192 | tf_op jit(solution)/shard_map/ppermute | solution.py:148
  17.6 1.4 %collective-permute-start.3 = (f32[144,128]{1,0:T(8,128)}, f32[144,128]{1,0:T(8,128)S(1)}, u32[]{:S(2)}, u32[]{:S(2)}) collective-permute-start(f32[144,128]{1,0:T(8,128)} %get-tuple-element.8.own), channel_id=1, source_target_pairs={{4,1},{6,3},{1,4},{8,5},{3,6},{10,7},{5,8},{12,9},{7,10},{14,11},{... | collective-permute-start | bytes 221192 | tf_op jit(solution)/shard_map/ppermute | solution.py:148
  19.0 0.0 collective-permute-done.2.second
  19.0 0.0 copy-start.3
  19.0 0.0 collective-permute-start.6
  19.0 0.0 collective-permute-done.beside
  19.0 0.0 copy-done
  19.0 0.0 copy-start.1
  19.0 0.7 %copy-done.1 = f32[400,128]{1,0:T(8,128)} copy-done((f32[400,128]{1,0:T(8,128)}, f32[400,128]{1,0:T(8,128)S(1)}, u32[]{:S(2)}) %copy-start.1) | copy-done | bytes 204824
  19.7 4.3 %shard_map.92.near = f32[8,32,128]{2,1,0:T(8,128)} custom-call(s32[8,6]{1,0:T(8,128)} %near_index.1, f32[8,32,128]{2,1,0:T(8,128)} %vectors.3, f32[8,6,128,128]{3,2,1,0:T(8,128)} %near_block.1, f32[400,128]{1,0:T(8,128)} %copy-done.1, f32[400,128]{1,0:T(8,128)} %copy-done), custom_call_target="tpu_custom_call" | custom-call | tf_op jit(solution)/shard_map/pallas_call | solution.py:166
  24.0 0.0 collective-permute-done.4.opposite
  24.0 0.0 copy-start.4
  24.0 0.0 collective-permute-done.3.third
  24.0 0.0 copy-start.5
  24.0 0.0 collective-permute-done.6.third_beside
  24.0 0.0 copy-start.6
  24.0 0.0 collective-permute-done.5.second_beside
  24.0 0.0 copy-done.3
  24.1 0.6 %copy-done.4 = f32[144,128]{1,0:T(8,128)} copy-done((f32[144,128]{1,0:T(8,128)}, f32[144,128]{1,0:T(8,128)S(1)}, u32[]{:S(2)}) %copy-start.4) | copy-done | bytes 73752
  24.6 0.0 copy-done.5
  24.7 0.0 copy-done.6
  24.7 0.0 copy-start.2
  24.7 0.7 %copy-done.2 = f32[400,128]{1,0:T(8,128)} copy-done((f32[400,128]{1,0:T(8,128)}, f32[400,128]{1,0:T(8,128)S(1)}, u32[]{:S(2)}) %copy-start.2) | copy-done | bytes 204824
  25.4 4.6 %shard_map.93 = f32[8,32,128]{2,1,0:T(8,128)} custom-call(s32[8,8]{1,0:T(8,128)} %far_index.1, s32[1,8]{1,0:T(1,128)} %up_index.1, f32[8,32,128]{2,1,0:T(8,128)} %shard_map.92.near, f32[144,128]{1,0:T(8,128)} %get-tuple-element.8.own, f32[400,128]{1,0:T(8,128)} %copy-done.1, f32[400,128]{1,0:T(8,128)} %copy-done, f32[144,128]{1,0:T(8,128)} %copy-done.3, ...), custom_call_target="tpu_custom_call" | custom-call | tf_op jit(solution)/shard_map/pallas_call | solution.py:173
Async XLA Ops:
  4.4 6.9 %collective-permute-start.1 = (f32[400,128]{1,0:T(8,128)}, f32[400,128]{1,0:T(8,128)S(1)}, u32[]{:S(2)}, u32[]{:S(2)}) collective-permute-start(f32[400,128]{1,0:T(8,128)} %get-tuple-element.7), channel_id=1, source_target_pairs={{2,1},{1,2},{4,3},{3,4},{6,5},{5,6},{8,7},{7,8},{10,9},{9,10},{12,... | collective-permute-start | bytes 614408 | tf_op jit(solution)/shard_map/ppermute | solution.py:148
  7.4 11.6 %collective-permute-start = (f32[400,128]{1,0:T(8,128)}, f32[400,128]{1,0:T(8,128)S(1)}, u32[]{:S(2)}, u32[]{:S(2)}) collective-permute-start(f32[400,128]{1,0:T(8,128)} %get-tuple-element.7), channel_id=1, source_target_pairs={{0,1},{1,0},{2,3},{3,2},{4,5},{5,4},{6,7},{7,6},{8,9},{9,8},{10,11... | collective-permute-start | bytes 614408 | tf_op jit(solution)/shard_map/ppermute | solution.py:148
  11.3 7.7 %copy-start = (f32[400,128]{1,0:T(8,128)}, f32[400,128]{1,0:T(8,128)S(1)}, u32[]{:S(2)}) copy-start(f32[400,128]{1,0:T(8,128)S(1)} %collective-permute-done.1.across) | copy-start | bytes 614404
  11.3 12.7 %collective-permute-start.5 = (f32[400,128]{1,0:T(8,128)S(1)}, f32[400,128]{1,0:T(8,128)S(1)}, u32[]{:S(2)}, u32[]{:S(2)}) collective-permute-start(f32[400,128]{1,0:T(8,128)S(1)} %collective-permute-done.1.across), channel_id=1, source_target_pairs={{0,1},{1,0},{2,3},{3,2},{4,5},{5,4},{6,7},{7,6},{8,9},{9,8},{10,11... | collective-permute-start | bytes 614408 | tf_op jit(solution)/shard_map/ppermute | solution.py:148
  12.7 6.3 %collective-permute-start.2 = (f32[144,128]{1,0:T(8,128)}, f32[144,128]{1,0:T(8,128)S(1)}, u32[]{:S(2)}, u32[]{:S(2)}) collective-permute-start(f32[144,128]{1,0:T(8,128)} %get-tuple-element.8.own), channel_id=1, source_target_pairs={{3,1},{0,2},{5,3},{2,4},{7,5},{4,6},{9,7},{6,8},{11,9},{8,10},{13,... | collective-permute-start | bytes 221192 | tf_op jit(solution)/shard_map/ppermute | solution.py:148
  15.0 9.0 %collective-permute-start.4 = (f32[144,128]{1,0:T(8,128)}, f32[144,128]{1,0:T(8,128)S(1)}, u32[]{:S(2)}, u32[]{:S(2)}) collective-permute-start(f32[144,128]{1,0:T(8,128)} %get-tuple-element.8.own), channel_id=1, source_target_pairs={{0,8},{1,9},{2,10},{3,11},{4,12},{5,13},{6,14},{7,15},{8,0},{9,1},... | collective-permute-start | bytes 221192 | tf_op jit(solution)/shard_map/ppermute | solution.py:148
  17.6 6.4 %collective-permute-start.3 = (f32[144,128]{1,0:T(8,128)}, f32[144,128]{1,0:T(8,128)S(1)}, u32[]{:S(2)}, u32[]{:S(2)}) collective-permute-start(f32[144,128]{1,0:T(8,128)} %get-tuple-element.8.own), channel_id=1, source_target_pairs={{4,1},{6,3},{1,4},{8,5},{3,6},{10,7},{5,8},{12,9},{7,10},{14,11},{... | collective-permute-start | bytes 221192 | tf_op jit(solution)/shard_map/ppermute | solution.py:148
  19.0 5.1 %copy-start.3 = (f32[144,128]{1,0:T(8,128)}, f32[144,128]{1,0:T(8,128)S(1)}, u32[]{:S(2)}) copy-start(f32[144,128]{1,0:T(8,128)S(1)} %collective-permute-done.2.second) | copy-start | bytes 221188
  19.0 5.0 %collective-permute-start.6 = (f32[144,128]{1,0:T(8,128)S(1)}, f32[144,128]{1,0:T(8,128)S(1)}, u32[]{:S(2)}, u32[]{:S(2)}) collective-permute-start(f32[144,128]{1,0:T(8,128)S(1)} %collective-permute-done.2.second), channel_id=1, source_target_pairs={{0,1},{1,0},{2,3},{3,2},{4,5},{5,4},{6,7},{7,6},{8,9},{9,8},{10,11... | collective-permute-start | bytes 221192 | tf_op jit(solution)/shard_map/ppermute | solution.py:148
  19.0 0.7 %copy-start.1 = (f32[400,128]{1,0:T(8,128)}, f32[400,128]{1,0:T(8,128)S(1)}, u32[]{:S(2)}) copy-start(f32[400,128]{1,0:T(8,128)S(1)} %collective-permute-done.beside) | copy-start | bytes 614404
  24.0 0.6 %copy-start.4 = (f32[144,128]{1,0:T(8,128)}, f32[144,128]{1,0:T(8,128)S(1)}, u32[]{:S(2)}) copy-start(f32[144,128]{1,0:T(8,128)S(1)} %collective-permute-done.4.opposite) | copy-start | bytes 221188
  24.0 0.7 %copy-start.5 = (f32[144,128]{1,0:T(8,128)}, f32[144,128]{1,0:T(8,128)S(1)}, u32[]{:S(2)}) copy-start(f32[144,128]{1,0:T(8,128)S(1)} %collective-permute-done.3.third) | copy-start | bytes 221188
  24.0 0.6 %copy-start.6 = (f32[144,128]{1,0:T(8,128)}, f32[144,128]{1,0:T(8,128)S(1)}, u32[]{:S(2)}) copy-start(f32[144,128]{1,0:T(8,128)S(1)} %collective-permute-done.6.third_beside) | copy-start | bytes 221188
  24.7 0.7 %copy-start.2 = (f32[400,128]{1,0:T(8,128)}, f32[400,128]{1,0:T(8,128)S(1)}, u32[]{:S(2)}) copy-start(f32[400,128]{1,0:T(8,128)S(1)} %collective-permute-done.5.second_beside) | copy-start | bytes 614404

commit v2 on v1

--- a/solution.py
+++ b/solution.py
@@ -11,8 +11,17 @@
 F32 = jnp.float32
 NN = (((1,), (0,)), ((), ()))
 NT = (((1,), (1,)), ((), ()))
+HBM = pl.BlockSpec(memory_space=pltpu.HBM)
 VMEM = pl.BlockSpec(memory_space=pltpu.VMEM)
 SMEM = pl.BlockSpec(memory_space=pltpu.SMEM)
+
+
+def cost(us):
+    return pl.CostEstimate(flops=us * 500_000_000, bytes_accessed=0, transcendentals=0)
+
+
+def room(mib):
+    return pltpu.CompilerParams(vmem_limit_bytes=mib << 20)
 
 
 def split(x):
@@ -27,27 +36,40 @@
     return mul(xh, yh) + (mul(xl, yh) + mul(xh, yl))
 
 
+def streamed(blocks, inputs):
+    rows = inputs.shape[0]
+    bh, bl = split(blocks)
+    xh, xl = split(inputs)
+    mul = functools.partial(lax.dot_general, dimension_numbers=NT, preferred_element_type=F32)
+    both = mul(bh, jnp.concatenate([xh, xl], axis=0))
+    return (both[:, :rows] + (both[:, rows:] + mul(bl, xh))).T
+
+
 def pack(x):
     half = x.shape[0] // 2
     return jnp.concatenate([x[:half], x[half:]], axis=1)
 
 
-def coeffs_kernel(vectors, basis, transfer, sent, coeffs):
+def coeffs_kernel(vectors_in, basis_in, transfer_in, coeffs, vectors, basis, transfer, arrived):
     leaves, rows, points = vectors.shape
-    rank = basis.shape[2]
+    copies = [
+        pltpu.make_async_copy(there, here, arrived.at[i])
+        for i, (there, here) in enumerate(((vectors_in, vectors), (basis_in, basis), (transfer_in, transfer)))
+    ]
+    for copy in copies:
+        copy.start()
+    copies[0].wait()
+    copies[1].wait()
+    rank = basis.shape[1]
     half = rows // 2
-    base = leaves * rows
     parts = []
     for l in range(leaves):
-        own = vectors[l]
-        sent[l * rows : (l + 1) * rows] = own
-        parts.append(dot(own, basis[l], NN))
+        parts.append(dot(vectors[l], basis[l], NT))
     whole = jnp.concatenate(parts, axis=1)
+    copies[2].wait()
     parts.append(dot(whole, transfer[...].reshape(leaves * rank, rank), NN))
     for i, part in enumerate(parts):
-        packed = pack(part)
-        coeffs[i * half : (i + 1) * half] = packed
-        sent[base + i * half : base + (i + 1) * half] = packed
+        coeffs[i * half : (i + 1) * half] = pack(part)
 
 
 def place(index, here, side):
@@ -55,15 +77,15 @@
     return jnp.where(jnp.abs(away) <= REACH, away + REACH, 2 * REACH + 1)
 
 
-def near_kernel(near_index, vectors, near_block, beside, across, near, held):
+def near_kernel(near_index, near_block, own, beside, across, near, held):
     leaves, slots = near_index.shape
-    rows = vectors.shape[1]
+    rows = near.shape[1]
     here = lax.axis_index("leaf")
     side = 1 - 2 * lax.rem(here, 2)
     for l in range(leaves):
-        held[l] = across[l * rows : (l + 1) * rows]
-        held[leaves + l] = vectors[l]
-        held[2 * leaves + l] = beside[l * rows : (l + 1) * rows]
+        held[l] = across[l]
+        held[leaves + l] = own[l]
+        held[2 * leaves + l] = beside[l]
     for l in range(leaves):
         chosen = []
         for s in range(slots):
@@ -73,7 +95,7 @@
             chosen.append(held[(away + 1) * leaves + (index - device * leaves)])
         inputs = jnp.concatenate(chosen, axis=1)
         blocks = jnp.concatenate([near_block[l, s] for s in range(slots)], axis=1)
-        near[l] = dot(inputs, blocks, NT)
+        near[l] = streamed(blocks, inputs)
 
 
 def far_kernel(
@@ -81,7 +103,7 @@
     far_coupling, up_coupling, transfer, basis, product, held,
 ):
     leaves, rows, points = near.shape
-    rank = basis.shape[2]
+    rank = basis.shape[1]
     half = rows // 2
     slots = far_index.shape[1]
     here = lax.axis_index("leaf")
@@ -91,9 +113,8 @@
     base = leaves * rows
     sources = (third, second, across, own, beside, second_beside, third_beside, opposite)
     for k, source in enumerate(sources):
-        skip = source.shape[0] - (leaves + 1) * half
         for i in range(leaves + 1):
-            x = source[skip + i * half : skip + (i + 1) * half]
+            x = source[i * half : (i + 1) * half]
             turned = pltpu.roll(x, rank, 1)
             held[k * (leaves + 1) + i, :half] = jnp.where(left, x, turned)
             held[k * (leaves + 1) + i, half:] = jnp.where(left, turned, x)
@@ -111,9 +132,10 @@
 
     parent_far = far(leaves, up_coupling[0])
     down = dot(parent_far, transfer[...].reshape(leaves * rank, rank), NT)
-    for l in range(leaves):
-        leaf_far = far(l, far_coupling[l]) + down[:, l * rank : (l + 1) * rank]
-        product[l] = near[l] + dot(leaf_far, basis[l], NT)
+    leaf_fars = [far(l, far_coupling[l]) for l in range(leaves)]
+    for l in range(leaves):
+        leaf_far = leaf_fars[l] + down[:, l * rank : (l + 1) * rank]
+        product[l] = near[l] + dot(leaf_far, basis[l], NN)
 
 
 def routes(groups, count):
@@ -142,38 +164,51 @@
     leaves, rows, points = vectors.shape
     rank = basis.shape[2]
     packed = (leaves + 1) * rows // 2
+    basis = jnp.swapaxes(basis, 1, 2)
     beside_to, across_to, second_to, third_to, opposite_to = routes(groups, lax.axis_size("leaf"))
 
     def send(x, to):
         return lax.ppermute(x, ("groups", "leaf"), to)
 
-    sent, own = pl.pallas_call(
+    vectors_across = send(vectors, across_to)
+    vectors_beside = send(vectors, beside_to)
+    own = pl.pallas_call(
         coeffs_kernel,
-        out_shape=(
-            jax.ShapeDtypeStruct((leaves * rows + packed, points), F32),
-            jax.ShapeDtypeStruct((packed, points), F32),
-        ),
-        in_specs=[VMEM] * 3,
-        out_specs=(VMEM, VMEM),
-    )(vectors, basis, transfer)
-    across = send(sent, across_to)
-    beside = send(sent, beside_to)
+        out_shape=jax.ShapeDtypeStruct((packed, points), F32),
+        in_specs=[HBM] * 3,
+        out_specs=VMEM,
+        scratch_shapes=[
+            pltpu.VMEM(vectors.shape, F32),
+            pltpu.VMEM(basis.shape, F32),
+            pltpu.VMEM(transfer.shape, F32),
+            pltpu.SemaphoreType.DMA((3,)),
+        ],
+        compiler_params=room(4),
+        cost_estimate=cost(5),
+    )(*(pltpu.with_memory_space_constraint(x, pltpu.HBM) for x in (vectors, basis, transfer)))
     opposite = send(own, opposite_to)
+    across = send(own, across_to)
+    second = send(own, second_to)
     third = send(own, third_to)
-    second = send(own, second_to)
-    second_beside = send(across, beside_to)
-    third_beside = send(second, beside_to)
+    beside = send(own, beside_to)
     near = pl.pallas_call(
         near_kernel,
         out_shape=jax.ShapeDtypeStruct(vectors.shape, F32),
         in_specs=[SMEM] + [VMEM] * 4,
+        compiler_params=room(8),
+        cost_estimate=cost(3),
         out_specs=VMEM,
         scratch_shapes=[pltpu.VMEM((3 * leaves, rows, points), F32)],
-    )(near_index, vectors, near_block, beside, across)
+    )(near_index, near_block, vectors, vectors_beside, vectors_across)
+    across, second, near = lax.optimization_barrier((across, second, near))
+    second_beside = send(across, beside_to)
+    third_beside = send(second, beside_to)
     return pl.pallas_call(
         far_kernel,
         out_shape=jax.ShapeDtypeStruct(vectors.shape, F32),
         in_specs=[SMEM] * 2 + [VMEM] * 13,
+        compiler_params=room(10),
+        cost_estimate=cost(3),
         out_specs=VMEM,
         scratch_shapes=[pltpu.VMEM(((2 * REACH + 2) * (leaves + 1), rows, points), F32)],
     )(

time: 30.3 us -> 18.3 us (0.60)
  Pallas kernels: 11.3 us -> 6.11 us
  local copies, waits for them, and re-layouts: 3.93 us -> 0.05 us
  waiting for transfers between devices: 3.82 us -> 1.98 us
  starting transfers between devices: 10.8 us -> 9.93 us
    unnamed x15 -> x18, local copies, waits for them, and re-layouts: 3.93 us -> 0.05 us
    pallas_call x1, Pallas kernels: 4.3 us -> 1.78 us  [per_device(): pl.pallas_call(near_kernel, out_shape=jax.ShapeDtypeStruct(vectors.shape,...]
    pallas_call x1, Pallas kernels: 4.55 us -> 2.47 us  [per_device(): pl.pallas_call(far_kernel, out_shape=jax.ShapeDtypeStruct(vectors.shape,...]
    ppermute x7 -> x9, waiting for transfers between devices: 3.82 us -> 1.98 us  [send(): return lax.ppermute(x, ('groups', 'leaf'), to)]
    ppermute x7 -> x9, starting transfers between devices: 10.8 us -> 9.93 us  [send(): return lax.ppermute(x, ('groups', 'leaf'), to)]
    pallas_call x1, Pallas kernels: 2.47 us -> 1.85 us  [per_device(): pl.pallas_call(coeffs_kernel, out_shape=jax.ShapeDtypeStruct((packed, poi...]
  transfers between devices with their start and end apart: 7 -> 9, of which waited for: 1 -> 4; matrix products, arithmetic and copies ran while one was open for 0% -> 0% of each run, Pallas kernels for 14% -> 20%
where the time goes in v2:
time: 18.3 us; the launch traced here: 18.2 us
  starting transfers between devices  9.93 us (54%)
  Pallas kernels  6.11 us (33%)
  waiting for transfers between devices  1.98 us (11%)
    ppermute x9, starting transfers between devices, send(): return lax.ppermute(x, ('groups', 'leaf'), to)  9.93 us
    pallas_call x1, Pallas kernels, per_device(): pl.pallas_call(far_kernel, out_shape=jax.ShapeDtypeStruct(vectors.shape,...  2.47 us
    ppermute x9, waiting for transfers between devices, send(): return lax.ppermute(x, ('groups', 'leaf'), to)  1.98 us
    pallas_call x1, Pallas kernels, per_device(): pl.pallas_call(coeffs_kernel, out_shape=jax.ShapeDtypeStruct((packed, poi...  1.85 us
    pallas_call x1, Pallas kernels, per_device(): pl.pallas_call(near_kernel, out_shape=jax.ShapeDtypeStruct(vectors.shape,...  1.78 us
  transfers between devices with their start and end apart: 9, of which 4 were waited for; matrix products, arithmetic and copies ran while one was open for 0% of the time, Pallas kernels for 20%

profile of v2, /device:TPU:0, one launch (start us, length us, event | category | flops | bytes accessed | tf_op | source)
XLA Modules:
  0.0 18.2 jit_solution(17254277014146947494)
XLA Ops:
  0.0 0.5 %collective-permute-start.2 = (f32[8,32,128]{2,1,0:T(8,128)}, f32[8,32,128]{2,1,0:T(8,128)S(1)}, u32[]{:S(2)}, u32[]{:S(2)}) collective-permute-start(f32[8,32,128]{2,1,0:T(8,128)} %own.1), channel_id=1, source_target_pairs={{0,1},{1,0},{2,3},{3,2},{4,5},{5,4},{6,7},{7,6},{8,9},{9,8},{10,11... | collective-permute-start | bytes 393224 | tf_op jit(solution)/shard_map/ppermute | solution.py:171
  0.5 2.5 %collective-permute-start.3 = (f32[8,32,128]{2,1,0:T(8,128)}, f32[8,32,128]{2,1,0:T(8,128)S(1)}, u32[]{:S(2)}, u32[]{:S(2)}) collective-permute-start(f32[8,32,128]{2,1,0:T(8,128)} %own.1), channel_id=1, source_target_pairs={{2,1},{1,2},{4,3},{3,4},{6,5},{5,6},{8,7},{7,8},{10,9},{9,10},{12,... | collective-permute-start | bytes 393224 | tf_op jit(solution)/shard_map/ppermute | solution.py:171
  2.9 1.9 %shard_map.91.own = f32[144,128]{1,0:T(8,128)S(1)} custom-call(f32[8,32,128]{2,1,0:T(8,128)} %own.1, f32[8,64,128]{2,1,0:T(8,128)} %bitcast.1, f32[8,64,64]{2,1,0:T(8,128)} %transfer.1), custom_call_target="tpu_custom_call" | custom-call | flops 2500000000 | tf_op jit(solution)/shard_map/pallas_call | solution.py:175
  4.8 0.0 copy-start.1
  4.8 0.0 copy-start.2
  4.8 0.0 copy-start.3
  4.8 0.0 copy-start.4
  4.9 0.0 copy-start.7
  4.9 0.0 copy-start.8
  4.9 2.7 %collective-permute-start.6 = (f32[144,128]{1,0:T(8,128)S(1)}, f32[144,128]{1,0:T(8,128)S(1)}, u32[]{:S(2)}, u32[]{:S(2)}) collective-permute-start(f32[144,128]{1,0:T(8,128)S(1)} %shard_map.91.own), channel_id=1, source_target_pairs={{0,8},{1,9},{2,10},{3,11},{4,12},{5,13},{6,14},{7,15},{8,0},{9,1},... | collective-permute-start | bytes 221192 | tf_op jit(solution)/shard_map/ppermute | solution.py:171
  7.6 0.6 %collective-permute-start.5 = (f32[144,128]{1,0:T(8,128)S(1)}, f32[144,128]{1,0:T(8,128)S(1)}, u32[]{:S(2)}, u32[]{:S(2)}) collective-permute-start(f32[144,128]{1,0:T(8,128)S(1)} %shard_map.91.own), channel_id=1, source_target_pairs={{4,1},{6,3},{1,4},{8,5},{3,6},{10,7},{5,8},{12,9},{7,10},{14,11},{... | collective-permute-start | bytes 221192 | tf_op jit(solution)/shard_map/ppermute | solution.py:171
  8.2 1.1 %collective-permute-start.4 = (f32[144,128]{1,0:T(8,128)S(1)}, f32[144,128]{1,0:T(8,128)S(1)}, u32[]{:S(2)}, u32[]{:S(2)}) collective-permute-start(f32[144,128]{1,0:T(8,128)S(1)} %shard_map.91.own), channel_id=1, source_target_pairs={{0,1},{1,0},{2,3},{3,2},{4,5},{5,4},{6,7},{7,6},{8,9},{9,8},{10,11... | collective-permute-start | bytes 221192 | tf_op jit(solution)/shard_map/ppermute | solution.py:171
  9.3 0.0 collective-permute-done.2.beside
  9.3 0.6 %collective-permute-start.1 = (f32[144,128]{1,0:T(8,128)S(1)}, f32[144,128]{1,0:T(8,128)S(1)}, u32[]{:S(2)}, u32[]{:S(2)}) collective-permute-start(f32[144,128]{1,0:T(8,128)S(1)} %shard_map.91.own), channel_id=1, source_target_pairs={{3,1},{0,2},{5,3},{2,4},{7,5},{4,6},{9,7},{6,8},{11,9},{8,10},{13,... | collective-permute-start | bytes 221192 | tf_op jit(solution)/shard_map/ppermute | solution.py:171
  9.9 0.0 collective-permute-done.3.across
  9.9 1.5 %collective-permute-start = (f32[144,128]{1,0:T(8,128)S(1)}, f32[144,128]{1,0:T(8,128)S(1)}, u32[]{:S(2)}, u32[]{:S(2)}) collective-permute-start(f32[144,128]{1,0:T(8,128)S(1)} %shard_map.91.own), channel_id=1, source_target_pairs={{2,1},{1,2},{4,3},{3,4},{6,5},{5,6},{8,7},{7,8},{10,9},{9,10},{12,... | collective-permute-start | bytes 221192 | tf_op jit(solution)/shard_map/ppermute | solution.py:171
  11.4 0.0 copy-done
  11.4 0.0 copy-done.5
  11.4 1.8 %shard_map.92.near = f32[8,32,128]{2,1,0:T(8,128)S(1)} custom-call(s32[8,6]{1,0:T(8,128)S(1)} %copy-done.6, f32[8,6,128,128]{3,2,1,0:T(8,128)S(1)} %copy-done, f32[8,32,128]{2,1,0:T(8,128)S(1)} %copy-done.5, f32[8,32,128]{2,1,0:T(8,128)S(1)} %collective-permute-done.2.beside, f32[8,32,128]{2,1,0:T(8,128)S(1)} %collective-permute-done.3.across), custom_call_target="tpu_custom_call" | custom-call | flops 1500000000 | tf_op jit(solution)/shard_map/pallas_call | solution.py:194
  13.2 0.6 %collective-permute-done.1.second = f32[144,128]{1,0:T(8,128)S(1)} collective-permute-done((f32[144,128]{1,0:T(8,128)S(1)}, f32[144,128]{1,0:T(8,128)S(1)}, u32[]{:S(2)}, u32[]{:S(2)}) %collective-permute-start.1) | collective-permute-done | bytes 73760 | tf_op jit(solution)/shard_map/ppermute | solution.py:171
  13.8 0.5 %collective-permute-done.across = f32[144,128]{1,0:T(8,128)S(1)} collective-permute-done((f32[144,128]{1,0:T(8,128)S(1)}, f32[144,128]{1,0:T(8,128)S(1)}, u32[]{:S(2)}, u32[]{:S(2)}) %collective-permute-start) | collective-permute-done | bytes 73760 | tf_op jit(solution)/shard_map/ppermute | solution.py:171
  14.2 0.0 collective-permute-start.7
  14.2 0.5 %collective-permute-start.8 = (f32[144,128]{1,0:T(8,128)S(1)}, f32[144,128]{1,0:T(8,128)S(1)}, u32[]{:S(2)}, u32[]{:S(2)}) collective-permute-start(f32[144,128]{1,0:T(8,128)S(1)} %collective-permute-done.1.second), channel_id=1, source_target_pairs={{0,1},{1,0},{2,3},{3,2},{4,5},{5,4},{6,7},{7,6},{8,9},{9,8},{10,11... | collective-permute-start | bytes 221192 | tf_op jit(solution)/shard_map/ppermute | solution.py:171
  14.7 0.0 collective-permute-done.6.opposite
  14.8 0.0 collective-permute-done.5.third
  14.8 0.0 collective-permute-done.4.beside
  14.8 0.7 %collective-permute-done.7.second_beside = f32[144,128]{1,0:T(8,128)S(1)} collective-permute-done((f32[144,128]{1,0:T(8,128)S(1)}, f32[144,128]{1,0:T(8,128)S(1)}, u32[]{:S(2)}, u32[]{:S(2)}) %collective-permute-start.7) | collective-permute-done | bytes 73760 | tf_op jit(solution)/shard_map/ppermute | solution.py:171
  15.5 0.2 collective-permute-done.8.third_beside
  15.7 0.0 copy-done.1
  15.7 0.0 copy-done.7
  15.7 0.0 copy-done.8
  15.7 2.5 %shard_map.93 = f32[8,32,128]{2,1,0:T(8,128)} custom-call(s32[8,8]{1,0:T(8,128)S(1)} %copy-done.7, s32[1,8]{1,0:T(1,128)S(1)} %copy-done.8, f32[8,32,128]{2,1,0:T(8,128)S(1)} %shard_map.92.near, f32[144,128]{1,0:T(8,128)S(1)} %shard_map.91.own, f32[144,128]{1,0:T(8,128)S(1)} %collective-permute-done.4.beside, f32[144,128]{1,0:T(8,128)S(1)} %collective-permute-done.across, ...), custom_call_target="tpu_custom_call" | custom-call | flops 1500000000 | tf_op jit(solution)/shard_map/pallas_call | solution.py:206
  (7 shorter events, 0.0 us)
Async XLA Ops:
  0.0 9.3 %collective-permute-start.2 = (f32[8,32,128]{2,1,0:T(8,128)}, f32[8,32,128]{2,1,0:T(8,128)S(1)}, u32[]{:S(2)}, u32[]{:S(2)}) collective-permute-start(f32[8,32,128]{2,1,0:T(8,128)} %own.1), channel_id=1, source_target_pairs={{0,1},{1,0},{2,3},{3,2},{4,5},{5,4},{6,7},{7,6},{8,9},{9,8},{10,11... | collective-permute-start | bytes 393224 | tf_op jit(solution)/shard_map/ppermute | solution.py:171
  0.5 9.4 %collective-permute-start.3 = (f32[8,32,128]{2,1,0:T(8,128)}, f32[8,32,128]{2,1,0:T(8,128)S(1)}, u32[]{:S(2)}, u32[]{:S(2)}) collective-permute-start(f32[8,32,128]{2,1,0:T(8,128)} %own.1), channel_id=1, source_target_pairs={{2,1},{1,2},{4,3},{3,4},{6,5},{5,6},{8,7},{7,8},{10,9},{9,10},{12,... | collective-permute-start | bytes 393224 | tf_op jit(solution)/shard_map/ppermute | solution.py:171
  2.9 8.4 %copy-start = (f32[8,6,128,128]{3,2,1,0:T(8,128)S(1)}, f32[8,6,128,128]{3,2,1,0:T(8,128)}, u32[]{:S(2)}) copy-start(f32[8,6,128,128]{3,2,1,0:T(8,128)} %near_block.1) | copy-start | bytes 9437188
  2.9 8.4 %copy-start.5 = (f32[8,32,128]{2,1,0:T(8,128)S(1)}, f32[8,32,128]{2,1,0:T(8,128)}, u32[]{:S(2)}) copy-start(f32[8,32,128]{2,1,0:T(8,128)} %own.1) | copy-start | bytes 393220
  2.9 8.4 %copy-start.6 = (s32[8,6]{1,0:T(8,128)S(1)}, s32[8,6]{1,0:T(8,128)}, u32[]{:S(2)}) copy-start(s32[8,6]{1,0:T(8,128)} %near_index.1) | copy-start | bytes 580
  4.8 10.9 %copy-start.1 = (f32[8,8,64,64]{3,2,1,0:T(8,128)S(1)}, f32[8,8,64,64]{3,2,1,0:T(8,128)}, u32[]{:S(2)}) copy-start(f32[8,8,64,64]{3,2,1,0:T(8,128)} %far_coupling.1) | copy-start | bytes 3145732
  4.8 10.8 %copy-start.2 = (f32[8,128,64]{1,2,0:T(8,128)S(1)}, f32[8,128,64]{1,2,0:T(8,128)}, u32[]{:S(2)}) copy-start(f32[8,128,64]{1,2,0:T(8,128)} %param.12) | copy-start | bytes 786436
  4.8 10.8 %copy-start.3 = (f32[8,64,64]{2,1,0:T(8,128)S(1)}, f32[8,64,64]{2,1,0:T(8,128)}, u32[]{:S(2)}) copy-start(f32[8,64,64]{2,1,0:T(8,128)} %transfer.1) | copy-start | bytes 393220
  4.8 10.8 %copy-start.4 = (f32[1,8,64,64]{3,2,1,0:T(8,128)S(1)}, f32[1,8,64,64]{3,2,1,0:T(8,128)}, u32[]{:S(2)}) copy-start(f32[1,8,64,64]{3,2,1,0:T(8,128)} %up_coupling.1) | copy-start | bytes 393220
  4.9 10.8 %copy-start.7 = (s32[8,8]{1,0:T(8,128)S(1)}, s32[8,8]{1,0:T(8,128)}, u32[]{:S(2)}) copy-start(s32[8,8]{1,0:T(8,128)} %far_index.1) | copy-start | bytes 772
  4.9 10.8 %copy-start.8 = (s32[1,8]{1,0:T(1,128)S(1)}, s32[1,8]{1,0:T(1,128)}, u32[]{:S(2)}) copy-start(s32[1,8]{1,0:T(1,128)} %up_index.1) | copy-start | bytes 100
  4.9 9.9 %collective-permute-start.6 = (f32[144,128]{1,0:T(8,128)S(1)}, f32[144,128]{1,0:T(8,128)S(1)}, u32[]{:S(2)}, u32[]{:S(2)}) collective-permute-start(f32[144,128]{1,0:T(8,128)S(1)} %shard_map.91.own), channel_id=1, source_target_pairs={{0,8},{1,9},{2,10},{3,11},{4,12},{5,13},{6,14},{7,15},{8,0},{9,1},... | collective-permute-start | bytes 221192 | tf_op jit(solution)/shard_map/ppermute | solution.py:171
  7.6 7.2 %collective-permute-start.5 = (f32[144,128]{1,0:T(8,128)S(1)}, f32[144,128]{1,0:T(8,128)S(1)}, u32[]{:S(2)}, u32[]{:S(2)}) collective-permute-start(f32[144,128]{1,0:T(8,128)S(1)} %shard_map.91.own), channel_id=1, source_target_pairs={{4,1},{6,3},{1,4},{8,5},{3,6},{10,7},{5,8},{12,9},{7,10},{14,11},{... | collective-permute-start | bytes 221192 | tf_op jit(solution)/shard_map/ppermute | solution.py:171
  8.2 6.6 %collective-permute-start.4 = (f32[144,128]{1,0:T(8,128)S(1)}, f32[144,128]{1,0:T(8,128)S(1)}, u32[]{:S(2)}, u32[]{:S(2)}) collective-permute-start(f32[144,128]{1,0:T(8,128)S(1)} %shard_map.91.own), channel_id=1, source_target_pairs={{0,1},{1,0},{2,3},{3,2},{4,5},{5,4},{6,7},{7,6},{8,9},{9,8},{10,11... | collective-permute-start | bytes 221192 | tf_op jit(solution)/shard_map/ppermute | solution.py:171
  9.3 4.5 %collective-permute-start.1 = (f32[144,128]{1,0:T(8,128)S(1)}, f32[144,128]{1,0:T(8,128)S(1)}, u32[]{:S(2)}, u32[]{:S(2)}) collective-permute-start(f32[144,128]{1,0:T(8,128)S(1)} %shard_map.91.own), channel_id=1, source_target_pairs={{3,1},{0,2},{5,3},{2,4},{7,5},{4,6},{9,7},{6,8},{11,9},{8,10},{13,... | collective-permute-start | bytes 221192 | tf_op jit(solution)/shard_map/ppermute | solution.py:171
  9.9 4.4 %collective-permute-start = (f32[144,128]{1,0:T(8,128)S(1)}, f32[144,128]{1,0:T(8,128)S(1)}, u32[]{:S(2)}, u32[]{:S(2)}) collective-permute-start(f32[144,128]{1,0:T(8,128)S(1)} %shard_map.91.own), channel_id=1, source_target_pairs={{2,1},{1,2},{4,3},{3,4},{6,5},{5,6},{8,7},{7,8},{10,9},{9,10},{12,... | collective-permute-start | bytes 221192 | tf_op jit(solution)/shard_map/ppermute | solution.py:171
  14.2 1.3 %collective-permute-start.7 = (f32[144,128]{1,0:T(8,128)S(1)}, f32[144,128]{1,0:T(8,128)S(1)}, u32[]{:S(2)}, u32[]{:S(2)}) collective-permute-start(f32[144,128]{1,0:T(8,128)S(1)} %collective-permute-done.across), channel_id=1, source_target_pairs={{0,1},{1,0},{2,3},{3,2},{4,5},{5,4},{6,7},{7,6},{8,9},{9,8},{10,11... | collective-permute-start | bytes 221192 | tf_op jit(solution)/shard_map/ppermute | solution.py:171
  14.2 1.4 %collective-permute-start.8 = (f32[144,128]{1,0:T(8,128)S(1)}, f32[144,128]{1,0:T(8,128)S(1)}, u32[]{:S(2)}, u32[]{:S(2)}) collective-permute-start(f32[144,128]{1,0:T(8,128)S(1)} %collective-permute-done.1.second), channel_id=1, source_target_pairs={{0,1},{1,0},{2,3},{3,2},{4,5},{5,4},{6,7},{7,6},{8,9},{9,8},{10,11... | collective-permute-start | bytes 221192 | tf_op jit(solution)/shard_map/ppermute | solution.py:171

commit v3 on v2

--- a/solution.py
+++ b/solution.py
@@ -13,7 +13,6 @@
 NT = (((1,), (1,)), ((), ()))
 HBM = pl.BlockSpec(memory_space=pltpu.HBM)
 VMEM = pl.BlockSpec(memory_space=pltpu.VMEM)
-SMEM = pl.BlockSpec(memory_space=pltpu.SMEM)
 
 
 def cost(us):
@@ -29,20 +28,24 @@
     return high, (x - high.astype(F32)).astype(jnp.bfloat16)
 
 
+def mul(x, y, dims):
+    return lax.dot_general(x, y, dims, preferred_element_type=F32)
+
+
 def dot(x, y, dims):
+    rows = x.shape[0]
     xh, xl = split(x)
     yh, yl = split(y)
-    mul = functools.partial(lax.dot_general, dimension_numbers=dims, preferred_element_type=F32)
-    return mul(xh, yh) + (mul(xl, yh) + mul(xh, yl))
+    both = mul(jnp.concatenate([xh, xl], axis=0), yh, dims)
+    return both[:rows] + (both[rows:] + mul(xh, yl, dims))
 
 
 def streamed(blocks, inputs):
     rows = inputs.shape[0]
     bh, bl = split(blocks)
     xh, xl = split(inputs)
-    mul = functools.partial(lax.dot_general, dimension_numbers=NT, preferred_element_type=F32)
-    both = mul(bh, jnp.concatenate([xh, xl], axis=0))
-    return (both[:, :rows] + (both[:, rows:] + mul(bl, xh))).T
+    both = mul(bh, jnp.concatenate([xh, xl], axis=0), NT)
+    return (both[:, :rows] + (both[:, rows:] + mul(bl, xh, NT))).T
 
 
 def pack(x):
@@ -72,9 +75,14 @@
         coeffs[i * half : (i + 1) * half] = pack(part)
 
 
-def place(index, here, side):
-    away = (index - here) * side
-    return jnp.where(jnp.abs(away) <= REACH, away + REACH, 2 * REACH + 1)
+def place(index, here):
+    differ = index ^ here
+    elsewhere = jnp.where(jnp.abs(index - here) <= REACH, 6, 7)
+    return jnp.where(differ < 4, differ, jnp.where((index ^ other_side_of(here)) & -2 == 0, 4 + (differ & 1), elsewhere))
+
+
+def other_side_of(core):
+    return core - 2 + 2 * (core & 2)
 
 
 def near_kernel(near_index, near_block, own, beside, across, near, held):
@@ -86,20 +94,18 @@
         held[l] = across[l]
         held[leaves + l] = own[l]
         held[2 * leaves + l] = beside[l]
-    for l in range(leaves):
-        chosen = []
-        for s in range(slots):
-            index = near_index[l, s]
-            device = lax.div(index, leaves)
-            away = (device - here) * side
-            chosen.append(held[(away + 1) * leaves + (index - device * leaves)])
+    index = near_index[...]
+    device = lax.div(index, leaves)
+    places = ((device - here) * side + 1) * leaves + (index - device * leaves)
+    for l in range(leaves):
+        chosen = [held[places[l, s]] for s in range(slots)]
         inputs = jnp.concatenate(chosen, axis=1)
         blocks = jnp.concatenate([near_block[l, s] for s in range(slots)], axis=1)
         near[l] = streamed(blocks, inputs)
 
 
 def far_kernel(
-    far_index, up_index, near, own, beside, across, second, third, opposite, second_beside, third_beside,
+    far_index, up_index, near, own, beside, pair, pair_beside, side, side_beside, third, opposite,
     far_coupling, up_coupling, transfer, basis, product, held,
 ):
     leaves, rows, points = near.shape
@@ -107,11 +113,10 @@
     half = rows // 2
     slots = far_index.shape[1]
     here = lax.axis_index("leaf")
-    side = 1 - 2 * lax.rem(here, 2)
     left = lax.broadcasted_iota(jnp.int32, (half, 2 * rank), 1) < rank
     left_all = lax.broadcasted_iota(jnp.int32, (rows, 2 * rank), 1) < rank
     base = leaves * rows
-    sources = (third, second, across, own, beside, second_beside, third_beside, opposite)
+    sources = (own, beside, pair, pair_beside, side, side_beside, third, opposite)
     for k, source in enumerate(sources):
         for i in range(leaves + 1):
             x = source[i * half : (i + 1) * half]
@@ -119,12 +124,13 @@
             held[k * (leaves + 1) + i, :half] = jnp.where(left, x, turned)
             held[k * (leaves + 1) + i, half:] = jnp.where(left, turned, x)
 
+    index = far_index[...]
+    device = lax.div(index, leaves)
+    places = place(device, here) * (leaves + 1) + (index - device * leaves)
+    up_places = place(up_index[...], here) * (leaves + 1) + leaves
+
     def chosen(u, s):
-        if u < leaves:
-            index = far_index[u, s]
-            device = lax.div(index, leaves)
-            return held[place(device, here, side) * (leaves + 1) + (index - device * leaves)]
-        return held[place(up_index[0, s], here, side) * (leaves + 1) + leaves]
+        return held[places[u, s] if u < leaves else up_places[0, s]]
 
     def far(u, coupling):
         inputs = [jnp.where(left_all, chosen(u, s), chosen(u, s + 1)) for s in range(0, slots, 2)]
@@ -138,24 +144,31 @@
         product[l] = near[l] + dot(leaf_far, basis[l], NN)
 
 
+def other_side(core):
+    return core + 2 if core & 2 else core - 2
+
+
 def routes(groups, count):
     last = count - 1
+    ends = (0, 1, last - 1, last)
+
+    def everywhere(pairs):
+        return [(g * count + j, g * count + i) for g in range(groups) for j, i in pairs]
 
     def mirrored(step):
         wanted = [(i - step, i) if i % 2 == 0 else (i + step, i) for i in range(count)]
         return [(j, i) for j, i in wanted if 0 <= j <= last]
 
-    def everywhere(pairs):
-        return [(g * count + j, g * count + i) for g in range(groups) for j, i in pairs]
-
-    beside = everywhere([(i, i ^ 1) for i in range(count)])
+    beside = everywhere([(i ^ 1, i) for i in range(count)])
+    pair = everywhere([(i ^ 2, i) for i in range(count)])
+    opposite = everywhere([((i + count // 2) % count, i) for i in range(count)])
+    third = everywhere(mirrored(3) + [(0, 2), (2, 0), (last, last - 2), (last - 2, last)])
     across = everywhere(mirrored(1))
+    side = everywhere([(other_side(i), i) for i in range(count) if i not in ends])
     if groups > 1:
         across += [(g * count + i, (g + 1) % groups * count + i) for g in range(groups) for i in (0, last)]
-    second = everywhere(mirrored(2) + [(1, 0), (last - 1, last)])
-    third = everywhere(mirrored(3) + [(0, 2), (2, 0), (last, last - 2), (last - 2, last)])
-    opposite = everywhere([(i, (i + count // 2) % count) for i in range(count)])
-    return beside, across, second, third, opposite
+        side += [(g * count + i, (g + 1) % groups * count + i) for g in range(groups) for i in ends]
+    return beside, across, pair, side, third, opposite
 
 
 def per_device(
@@ -165,7 +178,7 @@
     rank = basis.shape[2]
     packed = (leaves + 1) * rows // 2
     basis = jnp.swapaxes(basis, 1, 2)
-    beside_to, across_to, second_to, third_to, opposite_to = routes(groups, lax.axis_size("leaf"))
+    beside_to, across_to, pair_to, side_to, third_to, opposite_to = routes(groups, lax.axis_size("leaf"))
 
     def send(x, to):
         return lax.ppermute(x, ("groups", "leaf"), to)
@@ -186,33 +199,33 @@
         compiler_params=room(4),
         cost_estimate=cost(5),
     )(*(pltpu.with_memory_space_constraint(x, pltpu.HBM) for x in (vectors, basis, transfer)))
+    pair = send(own, pair_to)
+    side = send(own, side_to)
     opposite = send(own, opposite_to)
-    across = send(own, across_to)
-    second = send(own, second_to)
     third = send(own, third_to)
     beside = send(own, beside_to)
+    vectors_across, vectors_beside, side, pair = lax.optimization_barrier((vectors_across, vectors_beside, side, pair))
+    pair_beside = send(pair, beside_to)
+    side_beside = send(side, beside_to)
     near = pl.pallas_call(
         near_kernel,
         out_shape=jax.ShapeDtypeStruct(vectors.shape, F32),
-        in_specs=[SMEM] + [VMEM] * 4,
+        in_specs=[VMEM] * 5,
         compiler_params=room(8),
         cost_estimate=cost(3),
         out_specs=VMEM,
         scratch_shapes=[pltpu.VMEM((3 * leaves, rows, points), F32)],
     )(near_index, near_block, vectors, vectors_beside, vectors_across)
-    across, second, near = lax.optimization_barrier((across, second, near))
-    second_beside = send(across, beside_to)
-    third_beside = send(second, beside_to)
     return pl.pallas_call(
         far_kernel,
         out_shape=jax.ShapeDtypeStruct(vectors.shape, F32),
-        in_specs=[SMEM] * 2 + [VMEM] * 13,
+        in_specs=[VMEM] * 15,
         compiler_params=room(10),
         cost_estimate=cost(3),
         out_specs=VMEM,
-        scratch_shapes=[pltpu.VMEM(((2 * REACH + 2) * (leaves + 1), rows, points), F32)],
+        scratch_shapes=[pltpu.VMEM((8 * (leaves + 1), rows, points), F32)],
     )(
-        far_index, up_index, near, own, beside, across, second, third, opposite, second_beside, third_beside,
+        far_index, up_index, near, own, beside, pair, pair_beside, side, side_beside, third, opposite,
         far_coupling, up_coupling, transfer, basis,
     )
 

time: 18.3 us -> 16.9 us (0.923)
  waiting for transfers between devices: 1.98 us -> 0.72 us
  Pallas kernels: 6.11 us -> 4.88 us
  starting transfers between devices: 9.93 us -> 11 us
    ppermute x9, waiting for transfers between devices: 1.98 us -> 0.72 us  [send(): return lax.ppermute(x, ('groups', 'leaf'), to)]
    ppermute x9, starting transfers between devices: 9.93 us -> 11 us  [send(): return lax.ppermute(x, ('groups', 'leaf'), to)]
    pallas_call x1, Pallas kernels: 2.47 us -> 1.82 us  [per_device(): pl.pallas_call(far_kernel, out_shape=jax.ShapeDtypeStruct(vectors.shape,...]
    pallas_call x1, Pallas kernels: 1.78 us -> 1.3 us  [per_device(): pl.pallas_call(near_kernel, out_shape=jax.ShapeDtypeStruct(vectors.shape,...]
  transfers between devices with their start and end apart: 9 -> 9, of which waited for: 4 -> 1; matrix products, arithmetic and copies ran while one was open for 0% -> 0% of each run, Pallas kernels for 20% -> 18%
where the time goes in v3:
time: 16.9 us; the launch traced here: 16.8 us
  starting transfers between devices  11 us (65%)
  Pallas kernels  4.88 us (29%)
  waiting for transfers between devices  0.72 us (4%)
    ppermute x9, starting transfers between devices, send(): return lax.ppermute(x, ('groups', 'leaf'), to)  11 us
    pallas_call x1, Pallas kernels, per_device(): pl.pallas_call(far_kernel, out_shape=jax.ShapeDtypeStruct(vectors.shape,...  1.82 us
    pallas_call x1, Pallas kernels, per_device(): pl.pallas_call(coeffs_kernel, out_shape=jax.ShapeDtypeStruct((packed, poi...  1.76 us
    pallas_call x1, Pallas kernels, per_device(): pl.pallas_call(near_kernel, out_shape=jax.ShapeDtypeStruct(vectors.shape,...  1.3 us
    ppermute x9, waiting for transfers between devices, send(): return lax.ppermute(x, ('groups', 'leaf'), to)  0.72 us
  transfers between devices with their start and end apart: 9, of which 1 were waited for; matrix products, arithmetic and copies ran while one was open for 0% of the time, Pallas kernels for 18%

profile of v3, /device:TPU:0, one launch (start us, length us, event | category | flops | bytes accessed | tf_op | source)
XLA Modules:
  0.0 16.8 jit_solution(13700052788681935877)
XLA Ops:
  0.0 0.5 %collective-permute-start.1 = (f32[8,32,128]{2,1,0:T(8,128)}, f32[8,32,128]{2,1,0:T(8,128)S(1)}, u32[]{:S(2)}, u32[]{:S(2)}) collective-permute-start(f32[8,32,128]{2,1,0:T(8,128)} %own.1), channel_id=1, source_target_pairs={{1,0},{0,1},{3,2},{2,3},{5,4},{4,5},{7,6},{6,7},{9,8},{8,9},{11,10... | collective-permute-start | bytes 393224 | tf_op jit(solution)/shard_map/ppermute | solution.py:184
  0.5 2.5 %collective-permute-start = (f32[8,32,128]{2,1,0:T(8,128)}, f32[8,32,128]{2,1,0:T(8,128)S(1)}, u32[]{:S(2)}, u32[]{:S(2)}) collective-permute-start(f32[8,32,128]{2,1,0:T(8,128)} %own.1), channel_id=1, source_target_pairs={{2,1},{1,2},{4,3},{3,4},{6,5},{5,6},{8,7},{7,8},{10,9},{9,10},{12,... | collective-permute-start | bytes 393224 | tf_op jit(solution)/shard_map/ppermute | solution.py:184
  2.9 1.8 %shard_map.91.own = f32[144,128]{1,0:T(8,128)S(1)} custom-call(f32[8,32,128]{2,1,0:T(8,128)} %own.1, f32[8,64,128]{2,1,0:T(8,128)} %bitcast.1, f32[8,64,64]{2,1,0:T(8,128)} %transfer.1), custom_call_target="tpu_custom_call" | custom-call | flops 2500000000 | tf_op jit(solution)/shard_map/pallas_call | solution.py:188
  4.7 0.0 copy-start.1
  4.7 0.0 copy-start.2
  4.7 0.0 copy-start.3
  4.8 0.0 copy-start.4
  4.8 0.0 copy-start.7
  4.8 0.0 copy-start.8
  4.8 0.1 collective-permute-start.3
  4.9 2.1 %collective-permute-start.2 = (f32[144,128]{1,0:T(8,128)S(1)}, f32[144,128]{1,0:T(8,128)S(1)}, u32[]{:S(2)}, u32[]{:S(2)}) collective-permute-start(f32[144,128]{1,0:T(8,128)S(1)} %shard_map.91.own), channel_id=1, source_target_pairs={{4,2},{5,3},{2,4},{3,5},{8,6},{9,7},{6,8},{7,9},{12,10},{13,11},{1... | collective-permute-start | bytes 221192 | tf_op jit(solution)/shard_map/ppermute | solution.py:184
  7.0 2.4 %collective-permute-start.8 = (f32[144,128]{1,0:T(8,128)S(1)}, f32[144,128]{1,0:T(8,128)S(1)}, u32[]{:S(2)}, u32[]{:S(2)}) collective-permute-start(f32[144,128]{1,0:T(8,128)S(1)} %shard_map.91.own), channel_id=1, source_target_pairs={{8,0},{9,1},{10,2},{11,3},{12,4},{13,5},{14,6},{15,7},{0,8},{1,9},... | collective-permute-start | bytes 221192 | tf_op jit(solution)/shard_map/ppermute | solution.py:184
  9.4 0.0 collective-permute-done.3.pair
  9.4 2.9 %collective-permute-start.7 = (f32[144,128]{1,0:T(8,128)S(1)}, f32[144,128]{1,0:T(8,128)S(1)}, u32[]{:S(2)}, u32[]{:S(2)}) collective-permute-start(f32[144,128]{1,0:T(8,128)S(1)} %shard_map.91.own), channel_id=1, source_target_pairs={{4,1},{6,3},{1,4},{8,5},{3,6},{10,7},{5,8},{12,9},{7,10},{14,11},{... | collective-permute-start | bytes 221192 | tf_op jit(solution)/shard_map/ppermute | solution.py:184
  12.3 0.0 collective-permute-done.2.side
  12.3 0.0 collective-permute-start.4
  12.3 0.0 collective-permute-done.1.beside
  12.3 0.0 collective-permute-done.across
  12.3 0.5 %collective-permute-start.5 = (f32[144,128]{1,0:T(8,128)S(1)}, f32[144,128]{1,0:T(8,128)S(1)}, u32[]{:S(2)}, u32[]{:S(2)}) collective-permute-start(f32[144,128]{1,0:T(8,128)S(1)} %collective-permute-done.3.pair), channel_id=1, source_target_pairs={{1,0},{0,1},{3,2},{2,3},{5,4},{4,5},{7,6},{6,7},{9,8},{8,9},{11,10... | collective-permute-start | bytes 221192 | tf_op jit(solution)/shard_map/ppermute | solution.py:184
  12.8 0.1 collective-permute-start.6
  12.9 0.0 copy-done.5
  12.9 1.3 %shard_map.92.near = f32[8,32,128]{2,1,0:T(8,128)S(1)} custom-call(s32[8,6]{1,0:T(8,128)S(1)} %copy-done.6, f32[8,6,128,128]{3,2,1,0:T(8,128)S(1)} %copy-done, f32[8,32,128]{2,1,0:T(8,128)S(1)} %copy-done.5, f32[8,32,128]{2,1,0:T(8,128)S(1)} %collective-permute-done.1.beside, f32[8,32,128]{2,1,0:T(8,128)S(1)} %collective-permute-done.across), custom_call_target="tpu_custom_call" | custom-call | flops 1500000000 | tf_op jit(solution)/shard_map/pallas_call | solution.py:210
  14.2 0.7 %collective-permute-done.8.opposite = f32[144,128]{1,0:T(8,128)S(1)} collective-permute-done((f32[144,128]{1,0:T(8,128)S(1)}, f32[144,128]{1,0:T(8,128)S(1)}, u32[]{:S(2)}, u32[]{:S(2)}) %collective-permute-start.8) | collective-permute-done | bytes 73760 | tf_op jit(solution)/shard_map/ppermute | solution.py:184
  14.9 0.0 collective-permute-done.7.third
  14.9 0.0 collective-permute-done.4.beside
  14.9 0.0 collective-permute-done.5.pair_beside
  14.9 0.0 collective-permute-done.6.side_beside
  14.9 0.0 copy-done.1
  14.9 0.0 copy-done.2
  14.9 0.0 copy-done.3
  14.9 0.0 copy-done.4
  15.0 1.8 %shard_map.93 = f32[8,32,128]{2,1,0:T(8,128)} custom-call(s32[8,8]{1,0:T(8,128)S(1)} %copy-done.7, s32[1,8]{1,0:T(1,128)S(1)} %copy-done.8, f32[8,32,128]{2,1,0:T(8,128)S(1)} %shard_map.92.near, f32[144,128]{1,0:T(8,128)S(1)} %shard_map.91.own, f32[144,128]{1,0:T(8,128)S(1)} %collective-permute-done.4.beside, f32[144,128]{1,0:T(8,128)S(1)} %collective-permute-done.3.pair, ...), custom_call_target="tpu_custom_call" | custom-call | flops 1500000000 | tf_op jit(solution)/shard_map/pallas_call | solution.py:219
  (7 shorter events, 0.0 us)
Async XLA Ops:
  0.0 12.3 %collective-permute-start.1 = (f32[8,32,128]{2,1,0:T(8,128)}, f32[8,32,128]{2,1,0:T(8,128)S(1)}, u32[]{:S(2)}, u32[]{:S(2)}) collective-permute-start(f32[8,32,128]{2,1,0:T(8,128)} %own.1), channel_id=1, source_target_pairs={{1,0},{0,1},{3,2},{2,3},{5,4},{4,5},{7,6},{6,7},{9,8},{8,9},{11,10... | collective-permute-start | bytes 393224 | tf_op jit(solution)/shard_map/ppermute | solution.py:184
  0.5 11.8 %collective-permute-start = (f32[8,32,128]{2,1,0:T(8,128)}, f32[8,32,128]{2,1,0:T(8,128)S(1)}, u32[]{:S(2)}, u32[]{:S(2)}) collective-permute-start(f32[8,32,128]{2,1,0:T(8,128)} %own.1), channel_id=1, source_target_pairs={{2,1},{1,2},{4,3},{3,4},{6,5},{5,6},{8,7},{7,8},{10,9},{9,10},{12,... | collective-permute-start | bytes 393224 | tf_op jit(solution)/shard_map/ppermute | solution.py:184
  2.9 9.9 %copy-start = (f32[8,6,128,128]{3,2,1,0:T(8,128)S(1)}, f32[8,6,128,128]{3,2,1,0:T(8,128)}, u32[]{:S(2)}) copy-start(f32[8,6,128,128]{3,2,1,0:T(8,128)} %near_block.1) | copy-start | bytes 9437188
  2.9 9.9 %copy-start.5 = (f32[8,32,128]{2,1,0:T(8,128)S(1)}, f32[8,32,128]{2,1,0:T(8,128)}, u32[]{:S(2)}) copy-start(f32[8,32,128]{2,1,0:T(8,128)} %own.1) | copy-start | bytes 393220
  2.9 9.9 %copy-start.6 = (s32[8,6]{1,0:T(8,128)S(1)}, s32[8,6]{1,0:T(8,128)}, u32[]{:S(2)}) copy-start(s32[8,6]{1,0:T(8,128)} %near_index.1) | copy-start | bytes 580
  4.7 10.2 %copy-start.1 = (f32[8,8,64,64]{3,2,1,0:T(8,128)S(1)}, f32[8,8,64,64]{3,2,1,0:T(8,128)}, u32[]{:S(2)}) copy-start(f32[8,8,64,64]{3,2,1,0:T(8,128)} %far_coupling.1) | copy-start | bytes 3145732
  4.7 10.2 %copy-start.2 = (f32[8,128,64]{1,2,0:T(8,128)S(1)}, f32[8,128,64]{1,2,0:T(8,128)}, u32[]{:S(2)}) copy-start(f32[8,128,64]{1,2,0:T(8,128)} %param.12) | copy-start | bytes 786436
  4.7 10.2 %copy-start.3 = (f32[8,64,64]{2,1,0:T(8,128)S(1)}, f32[8,64,64]{2,1,0:T(8,128)}, u32[]{:S(2)}) copy-start(f32[8,64,64]{2,1,0:T(8,128)} %transfer.1) | copy-start | bytes 393220
  4.8 10.2 %copy-start.4 = (f32[1,8,64,64]{3,2,1,0:T(8,128)S(1)}, f32[1,8,64,64]{3,2,1,0:T(8,128)}, u32[]{:S(2)}) copy-start(f32[1,8,64,64]{3,2,1,0:T(8,128)} %up_coupling.1) | copy-start | bytes 393220
  4.8 10.2 %copy-start.7 = (s32[8,8]{1,0:T(8,128)S(1)}, s32[8,8]{1,0:T(8,128)}, u32[]{:S(2)}) copy-start(s32[8,8]{1,0:T(8,128)} %far_index.1) | copy-start | bytes 772
  4.8 10.2 %copy-start.8 = (s32[1,8]{1,0:T(1,128)S(1)}, s32[1,8]{1,0:T(1,128)}, u32[]{:S(2)}) copy-start(s32[1,8]{1,0:T(1,128)} %up_index.1) | copy-start | bytes 100
  4.8 4.6 %collective-permute-start.3 = (f32[144,128]{1,0:T(8,128)S(1)}, f32[144,128]{1,0:T(8,128)S(1)}, u32[]{:S(2)}, u32[]{:S(2)}) collective-permute-start(f32[144,128]{1,0:T(8,128)S(1)} %shard_map.91.own), channel_id=1, source_target_pairs={{2,0},{3,1},{0,2},{1,3},{6,4},{7,5},{4,6},{5,7},{10,8},{11,9},{8,1... | collective-permute-start | bytes 221192 | tf_op jit(solution)/shard_map/ppermute | solution.py:184
  4.9 7.3 %collective-permute-start.2 = (f32[144,128]{1,0:T(8,128)S(1)}, f32[144,128]{1,0:T(8,128)S(1)}, u32[]{:S(2)}, u32[]{:S(2)}) collective-permute-start(f32[144,128]{1,0:T(8,128)S(1)} %shard_map.91.own), channel_id=1, source_target_pairs={{4,2},{5,3},{2,4},{3,5},{8,6},{9,7},{6,8},{7,9},{12,10},{13,11},{1... | collective-permute-start | bytes 221192 | tf_op jit(solution)/shard_map/ppermute | solution.py:184
  7.0 7.9 %collective-permute-start.8 = (f32[144,128]{1,0:T(8,128)S(1)}, f32[144,128]{1,0:T(8,128)S(1)}, u32[]{:S(2)}, u32[]{:S(2)}) collective-permute-start(f32[144,128]{1,0:T(8,128)S(1)} %shard_map.91.own), channel_id=1, source_target_pairs={{8,0},{9,1},{10,2},{11,3},{12,4},{13,5},{14,6},{15,7},{0,8},{1,9},... | collective-permute-start | bytes 221192 | tf_op jit(solution)/shard_map/ppermute | solution.py:184
  9.4 5.5 %collective-permute-start.7 = (f32[144,128]{1,0:T(8,128)S(1)}, f32[144,128]{1,0:T(8,128)S(1)}, u32[]{:S(2)}, u32[]{:S(2)}) collective-permute-start(f32[144,128]{1,0:T(8,128)S(1)} %shard_map.91.own), channel_id=1, source_target_pairs={{4,1},{6,3},{1,4},{8,5},{3,6},{10,7},{5,8},{12,9},{7,10},{14,11},{... | collective-permute-start | bytes 221192 | tf_op jit(solution)/shard_map/ppermute | solution.py:184
  12.3 2.6 %collective-permute-start.4 = (f32[144,128]{1,0:T(8,128)S(1)}, f32[144,128]{1,0:T(8,128)S(1)}, u32[]{:S(2)}, u32[]{:S(2)}) collective-permute-start(f32[144,128]{1,0:T(8,128)S(1)} %shard_map.91.own), channel_id=1, source_target_pairs={{1,0},{0,1},{3,2},{2,3},{5,4},{4,5},{7,6},{6,7},{9,8},{8,9},{11,10... | collective-permute-start | bytes 221192 | tf_op jit(solution)/shard_map/ppermute | solution.py:184
  12.3 2.6 %collective-permute-start.5 = (f32[144,128]{1,0:T(8,128)S(1)}, f32[144,128]{1,0:T(8,128)S(1)}, u32[]{:S(2)}, u32[]{:S(2)}) collective-permute-start(f32[144,128]{1,0:T(8,128)S(1)} %collective-permute-done.3.pair), channel_id=1, source_target_pairs={{1,0},{0,1},{3,2},{2,3},{5,4},{4,5},{7,6},{6,7},{9,8},{8,9},{11,10... | collective-permute-start | bytes 221192 | tf_op jit(solution)/shard_map/ppermute | solution.py:184
  12.8 2.1 %collective-permute-start.6 = (f32[144,128]{1,0:T(8,128)S(1)}, f32[144,128]{1,0:T(8,128)S(1)}, u32[]{:S(2)}, u32[]{:S(2)}) collective-permute-start(f32[144,128]{1,0:T(8,128)S(1)} %collective-permute-done.2.side), channel_id=1, source_target_pairs={{1,0},{0,1},{3,2},{2,3},{5,4},{4,5},{7,6},{6,7},{9,8},{8,9},{11,10... | collective-permute-start | bytes 221192 | tf_op jit(solution)/shard_map/ppermute | solution.py:184

commit v4 on v3

--- a/solution.py
+++ b/solution.py
@@ -7,7 +7,7 @@
 from jax.experimental.pallas import tpu as pltpu
 from jax.sharding import PartitionSpec as P
 
-REACH = 3
+PARTNER = 2
 F32 = jnp.float32
 NN = (((1,), (0,)), ((), ()))
 NT = (((1,), (1,)), ((), ()))
@@ -53,7 +53,7 @@
     return jnp.concatenate([x[:half], x[half:]], axis=1)
 
 
-def coeffs_kernel(vectors_in, basis_in, transfer_in, coeffs, vectors, basis, transfer, arrived):
+def coeffs_kernel(vectors_in, basis_in, transfer_in, coeffs, longer, vectors, basis, transfer, arrived):
     leaves, rows, points = vectors.shape
     copies = [
         pltpu.make_async_copy(there, here, arrived.at[i])
@@ -72,13 +72,16 @@
     copies[2].wait()
     parts.append(dot(whole, transfer[...].reshape(leaves * rank, rank), NN))
     for i, part in enumerate(parts):
-        coeffs[i * half : (i + 1) * half] = pack(part)
+        packed = pack(part)
+        coeffs[i * half : (i + 1) * half] = packed
+        longer[i * half : (i + 1) * half] = packed
+    longer[len(parts) * half :] = jnp.zeros_like(longer[len(parts) * half :])
 
 
 def place(index, here):
     differ = index ^ here
-    elsewhere = jnp.where(jnp.abs(index - here) <= REACH, 6, 7)
-    return jnp.where(differ < 4, differ, jnp.where((index ^ other_side_of(here)) & -2 == 0, 4 + (differ & 1), elsewhere))
+    side = (index ^ other_side_of(here)) & -2 == 0
+    return jnp.where(differ & -4 == 0, differ, jnp.where(side, 4 + (differ & 1), 6))
 
 
 def other_side_of(core):
@@ -104,26 +107,35 @@
         near[l] = streamed(blocks, inputs)
 
 
+def partner_matrices_kernel(far_coupling, up_coupling, transfer, basis, high, low):
+    leaves, rank, points = basis.shape
+    through = dot(up_coupling[0, PARTNER], transfer[...].reshape(leaves * rank, rank), NT)
+    for l in range(leaves):
+        two = jnp.concatenate([far_coupling[l, PARTNER], through[:, l * rank : (l + 1) * rank]], axis=0)
+        high[l], low[l] = split(dot(two, basis[l], NN))
+
+
+def doubled(x, left):
+    turned = pltpu.roll(x, x.shape[1] // 2, 1)
+    return jnp.where(left, x, turned), jnp.where(left, turned, x)
+
+
 def far_kernel(
-    far_index, up_index, near, own, beside, pair, pair_beside, side, side_beside, third, opposite,
-    far_coupling, up_coupling, transfer, basis, product, held,
+    far_index, up_index, near, own, beside, pair, pair_beside, side, side_beside, third,
+    far_coupling, up_coupling, transfer, basis, base, held,
 ):
     leaves, rows, points = near.shape
     rank = basis.shape[1]
     half = rows // 2
-    slots = far_index.shape[1]
+    slots = [s for s in range(far_index.shape[1]) if s != PARTNER]
     here = lax.axis_index("leaf")
     left = lax.broadcasted_iota(jnp.int32, (half, 2 * rank), 1) < rank
     left_all = lax.broadcasted_iota(jnp.int32, (rows, 2 * rank), 1) < rank
-    base = leaves * rows
-    sources = (own, beside, pair, pair_beside, side, side_beside, third, opposite)
+    sources = (own, beside, pair, pair_beside, side, side_beside, third)
     for k, source in enumerate(sources):
         for i in range(leaves + 1):
-            x = source[i * half : (i + 1) * half]
-            turned = pltpu.roll(x, rank, 1)
-            held[k * (leaves + 1) + i, :half] = jnp.where(left, x, turned)
-            held[k * (leaves + 1) + i, half:] = jnp.where(left, turned, x)
-
+            block = k * (leaves + 1) + i
+            held[block, :half], held[block, half:] = doubled(source[i * half : (i + 1) * half], left)
     index = far_index[...]
     device = lax.div(index, leaves)
     places = place(device, here) * (leaves + 1) + (index - device * leaves)
@@ -133,15 +145,30 @@
         return held[places[u, s] if u < leaves else up_places[0, s]]
 
     def far(u, coupling):
-        inputs = [jnp.where(left_all, chosen(u, s), chosen(u, s + 1)) for s in range(0, slots, 2)]
-        return dot(jnp.concatenate(inputs, axis=1), coupling.reshape(slots * rank, rank), NN)
+        inputs = [jnp.where(left_all, chosen(u, s), chosen(u, t)) for s, t in zip(slots[0:-1:2], slots[1::2])]
+        if len(slots) % 2:
+            inputs.append(chosen(u, slots[-1])[:, :rank])
+        return dot(jnp.concatenate(inputs, axis=1), jnp.concatenate([coupling[s] for s in slots], axis=0), NN)
 
     parent_far = far(leaves, up_coupling[0])
     down = dot(parent_far, transfer[...].reshape(leaves * rank, rank), NT)
     leaf_fars = [far(l, far_coupling[l]) for l in range(leaves)]
     for l in range(leaves):
         leaf_far = leaf_fars[l] + down[:, l * rank : (l + 1) * rank]
-        product[l] = near[l] + dot(leaf_far, basis[l], NN)
+        base[l] = near[l] + dot(leaf_far, basis[l], NN)
+
+
+def partner_kernel(base, opposite, high, low, product):
+    leaves, rows, points = base.shape
+    half = rows // 2
+    left = lax.broadcasted_iota(jnp.int32, (half, points), 1) < points // 2
+    blocks = [doubled(opposite[i * half : (i + 1) * half], left) for i in range(leaves + 1)]
+    parent = blocks[leaves]
+    for l in range(leaves):
+        inputs = jnp.concatenate([jnp.where(left, blocks[l][i], parent[i]) for i in range(2)], axis=0)
+        xh, xl = split(inputs)
+        both = mul(jnp.concatenate([xh, xl], axis=0), high[l], NN)
+        product[l] = base[l] + (both[:rows] + (both[rows:] + mul(xh, low[l], NN)))
 
 
 def other_side(core):
@@ -162,11 +189,12 @@
     beside = everywhere([(i ^ 1, i) for i in range(count)])
     pair = everywhere([(i ^ 2, i) for i in range(count)])
     opposite = everywhere([((i + count // 2) % count, i) for i in range(count)])
-    third = everywhere(mirrored(3) + [(0, 2), (2, 0), (last, last - 2), (last - 2, last)])
+    third = everywhere(mirrored(3))
     across = everywhere(mirrored(1))
     side = everywhere([(other_side(i), i) for i in range(count) if i not in ends])
     if groups > 1:
         across += [(g * count + i, (g + 1) % groups * count + i) for g in range(groups) for i in (0, last)]
+        third += [(g * count + i, (g + 1) % groups * count + i) for g in range(groups) for i in (0, 2, last - 2, last)]
         side += [(g * count + i, (g + 1) % groups * count + i) for g in range(groups) for i in ends]
     return beside, across, pair, side, third, opposite
 
@@ -185,11 +213,11 @@
 
     vectors_across = send(vectors, across_to)
     vectors_beside = send(vectors, beside_to)
-    own = pl.pallas_call(
+    own, own_longer = pl.pallas_call(
         coeffs_kernel,
-        out_shape=jax.ShapeDtypeStruct((packed, points), F32),
+        out_shape=tuple(jax.ShapeDtypeStruct((packed + extra, points), F32) for extra in (0, 8)),
         in_specs=[HBM] * 3,
-        out_specs=VMEM,
+        out_specs=(VMEM, VMEM),
         scratch_shapes=[
             pltpu.VMEM(vectors.shape, F32),
             pltpu.VMEM(basis.shape, F32),
@@ -199,35 +227,54 @@
         compiler_params=room(4),
         cost_estimate=cost(5),
     )(*(pltpu.with_memory_space_constraint(x, pltpu.HBM) for x in (vectors, basis, transfer)))
+    own, vectors_beside = lax.optimization_barrier((own, vectors_beside))
     pair = send(own, pair_to)
     side = send(own, side_to)
-    opposite = send(own, opposite_to)
+    opposite = send(own_longer, opposite_to)
     third = send(own, third_to)
     beside = send(own, beside_to)
-    vectors_across, vectors_beside, side, pair = lax.optimization_barrier((vectors_across, vectors_beside, side, pair))
+    whole = jax.ShapeDtypeStruct(vectors.shape, F32)
+    parts = jax.ShapeDtypeStruct((leaves, 2 * rank, points), jnp.bfloat16)
+    near = pl.pallas_call(
+        near_kernel,
+        out_shape=whole,
+        in_specs=[VMEM] * 5,
+        out_specs=VMEM,
+        scratch_shapes=[pltpu.VMEM((3 * leaves, rows, points), F32)],
+        compiler_params=room(8),
+        cost_estimate=cost(0),
+    )(near_index, near_block, vectors, vectors_beside, vectors_across)
+    near, side, pair = lax.optimization_barrier((near, side, pair))
     pair_beside = send(pair, beside_to)
     side_beside = send(side, beside_to)
-    near = pl.pallas_call(
-        near_kernel,
-        out_shape=jax.ShapeDtypeStruct(vectors.shape, F32),
-        in_specs=[VMEM] * 5,
-        compiler_params=room(8),
+    high, low = pl.pallas_call(
+        partner_matrices_kernel,
+        out_shape=(parts, parts),
+        in_specs=[VMEM] * 4,
+        out_specs=(VMEM, VMEM),
+        compiler_params=room(4),
         cost_estimate=cost(3),
+    )(far_coupling, up_coupling, transfer, basis)
+    base = pl.pallas_call(
+        far_kernel,
+        out_shape=whole,
+        in_specs=[VMEM] * 14,
         out_specs=VMEM,
-        scratch_shapes=[pltpu.VMEM((3 * leaves, rows, points), F32)],
-    )(near_index, near_block, vectors, vectors_beside, vectors_across)
-    return pl.pallas_call(
-        far_kernel,
-        out_shape=jax.ShapeDtypeStruct(vectors.shape, F32),
-        in_specs=[VMEM] * 15,
+        scratch_shapes=[pltpu.VMEM((7 * (leaves + 1), rows, points), F32)],
         compiler_params=room(10),
-        cost_estimate=cost(3),
-        out_specs=VMEM,
-        scratch_shapes=[pltpu.VMEM((8 * (leaves + 1), rows, points), F32)],
+        cost_estimate=cost(0),
     )(
-        far_index, up_index, near, own, beside, pair, pair_beside, side, side_beside, third, opposite,
+        far_index, up_index, near, own, beside, pair, pair_beside, side, side_beside, third,
         far_coupling, up_coupling, transfer, basis,
     )
+    return pl.pallas_call(
+        partner_kernel,
+        out_shape=whole,
+        in_specs=[VMEM] * 4,
+        out_specs=VMEM,
+        compiler_params=room(4),
+        cost_estimate=cost(0),
+    )(base, opposite, high, low)
 
 
 def solution(mesh):

time: 16.9 us -> 16.2 us (0.959)
  starting transfers between devices: 11 us -> 9.8 us
  Pallas kernels: 4.88 us -> 5.7 us
  waiting for transfers between devices: 0.72 us -> 0.47 us
    ppermute x9, starting transfers between devices: 11 us -> 9.8 us  [send(): return lax.ppermute(x, ('groups', 'leaf'), to)]
    pallas_call x3 -> x5, Pallas kernels: 4.88 us -> 5.7 us  [the longest x1 1.76 us: per_device(): pl.pallas_call(coeffs_kernel, out_shape=tuple((jax.ShapeDtypeStruct((pack...]
    ppermute x9, waiting for transfers between devices: 0.72 us -> 0.47 us  [send(): return lax.ppermute(x, ('groups', 'leaf'), to)]
  transfers between devices with their start and end apart: 9 -> 9, of which waited for: 1 -> 2; matrix products, arithmetic and copies ran while one was open for 0% -> 0% of each run, Pallas kernels for 18% -> 29%
where the time goes in v4:
time: 16.2 us; the launch traced here: 16.1 us
  starting transfers between devices  9.8 us (60%)
  Pallas kernels  5.7 us (35%)
  waiting for transfers between devices  0.47 us (3%)
    ppermute x9, starting transfers between devices, send(): return lax.ppermute(x, ('groups', 'leaf'), to)  9.8 us
    pallas_call x1, Pallas kernels, per_device(): pl.pallas_call(coeffs_kernel, out_shape=tuple((jax.ShapeDtypeStruct((pack...  1.76 us
    pallas_call x1, Pallas kernels, per_device(): pl.pallas_call(near_kernel, out_shape=whole, in_specs=[VMEM] * 5, out_spe...  1.29 us
    pallas_call x1, Pallas kernels, per_device(): pl.pallas_call(far_kernel, out_shape=whole, in_specs=[VMEM] * 14, out_spe...  1.07 us
    pallas_call x1, Pallas kernels, per_device(): pl.pallas_call(partner_kernel, out_shape=whole, in_specs=[VMEM] * 4, out_...  0.98 us
    pallas_call x1, Pallas kernels, per_device(): pl.pallas_call(partner_matrices_kernel, out_shape=(parts, parts), in_spec...  0.59 us
    ppermute x9, waiting for transfers between devices, send(): return lax.ppermute(x, ('groups', 'leaf'), to)  0.47 us
  transfers between devices with their start and end apart: 9, of which 2 were waited for; matrix products, arithmetic and copies ran while one was open for 0% of the time, Pallas kernels for 29%

profile of v4, /device:TPU:0, one launch (start us, length us, event | category | flops | bytes accessed | tf_op | source)
XLA Modules:
  0.0 16.1 jit_solution(7631610408149364969)
XLA Ops:
  0.0 0.5 %collective-permute-start = (f32[8,32,128]{2,1,0:T(8,128)}, f32[8,32,128]{2,1,0:T(8,128)S(1)}, u32[]{:S(2)}, u32[]{:S(2)}) collective-permute-start(f32[8,32,128]{2,1,0:T(8,128)} %own.1), channel_id=1, source_target_pairs={{1,0},{0,1},{3,2},{2,3},{5,4},{4,5},{7,6},{6,7},{9,8},{8,9},{11,10... | collective-permute-start | bytes 393224 | tf_op jit(solution)/shard_map/ppermute | solution.py:212
  0.5 2.5 %collective-permute-start.1 = (f32[8,32,128]{2,1,0:T(8,128)}, f32[8,32,128]{2,1,0:T(8,128)S(1)}, u32[]{:S(2)}, u32[]{:S(2)}) collective-permute-start(f32[8,32,128]{2,1,0:T(8,128)} %own.1), channel_id=1, source_target_pairs={{2,1},{1,2},{4,3},{3,4},{6,5},{5,6},{8,7},{7,8},{10,9},{9,10},{12,... | collective-permute-start | bytes 393224 | tf_op jit(solution)/shard_map/ppermute | solution.py:212
  2.9 1.8 %shard_map.91 = (f32[144,128]{1,0:T(8,128)S(1)}, f32[152,128]{1,0:T(8,128)S(1)}) custom-call(f32[8,32,128]{2,1,0:T(8,128)} %own.1, f32[8,64,128]{2,1,0:T(8,128)} %bitcast.1, f32[8,64,64]{2,1,0:T(8,128)} %transfer.3), custom_call_target="tpu_custom_call" | custom-call | flops 2500000000 | tf_op jit(solution)/shard_map/pallas_call | solution.py:216
  4.7 0.0 copy-start.1
  4.7 0.0 copy-start.2
  4.7 0.0 copy-start.3
  4.8 0.0 copy-start.4
  4.8 0.0 collective-permute-done.beside
  4.8 0.1 collective-permute-start.3
  4.9 2.1 %collective-permute-start.2 = (f32[144,128]{1,0:T(8,128)S(1)}, f32[144,128]{1,0:T(8,128)S(1)}, u32[]{:S(2)}, u32[]{:S(2)}) collective-permute-start(f32[144,128]{1,0:T(8,128)S(1)} %get-tuple-element.16.own), channel_id=1, source_target_pairs={{4,2},{5,3},{2,4},{3,5},{8,6},{9,7},{6,8},{7,9},{12,10},{13,11},{1... | collective-permute-start | bytes 221192 | tf_op jit(solution)/shard_map/ppermute | solution.py:212
  7.0 2.4 %collective-permute-start.8 = (f32[152,128]{1,0:T(8,128)S(1)}, f32[152,128]{1,0:T(8,128)S(1)}, u32[]{:S(2)}, u32[]{:S(2)}) collective-permute-start(f32[152,128]{1,0:T(8,128)S(1)} %get-tuple-element.20), channel_id=1, source_target_pairs={{8,0},{9,1},{10,2},{11,3},{12,4},{13,5},{14,6},{15,7},{0,8},{1,9},... | collective-permute-start | bytes 233480 | tf_op jit(solution)/shard_map/ppermute | solution.py:212
  9.4 1.5 %collective-permute-start.7 = (f32[144,128]{1,0:T(8,128)S(1)}, f32[144,128]{1,0:T(8,128)S(1)}, u32[]{:S(2)}, u32[]{:S(2)}) collective-permute-start(f32[144,128]{1,0:T(8,128)S(1)} %get-tuple-element.16.own), channel_id=1, source_target_pairs={{4,1},{6,3},{1,4},{8,5},{3,6},{10,7},{5,8},{12,9},{7,10},{14,11},{... | collective-permute-start | bytes 221192 | tf_op jit(solution)/shard_map/ppermute | solution.py:212
  10.9 0.0 collective-permute-done.1.across
  10.9 0.2 %collective-permute-start.4 = (f32[144,128]{1,0:T(8,128)S(1)}, f32[144,128]{1,0:T(8,128)S(1)}, u32[]{:S(2)}, u32[]{:S(2)}) collective-permute-start(f32[144,128]{1,0:T(8,128)S(1)} %get-tuple-element.16.own), channel_id=1, source_target_pairs={{1,0},{0,1},{3,2},{2,3},{5,4},{4,5},{7,6},{6,7},{9,8},{8,9},{11,10... | collective-permute-start | bytes 221192 | tf_op jit(solution)/shard_map/ppermute | solution.py:212
  11.1 0.0 copy-done
  11.1 0.0 copy-done.5
  11.1 0.0 copy-done.7
  11.1 1.3 %shard_map.92.near = f32[8,32,128]{2,1,0:T(8,128)S(1)} custom-call(s32[8,6]{1,0:T(8,128)S(1)} %copy-done.7, f32[8,6,128,128]{3,2,1,0:T(8,128)S(1)} %copy-done, f32[8,32,128]{2,1,0:T(8,128)S(1)} %copy-done.5, f32[8,32,128]{2,1,0:T(8,128)S(1)} %collective-permute-done.beside, f32[8,32,128]{2,1,0:T(8,128)S(1)} %collective-permute-done.1.across), custom_call_target="tpu_custom_call" | custom-call | tf_op jit(solution)/shard_map/pallas_call | solution.py:238
  12.4 0.0 collective-permute-done.3.pair
  12.4 0.0 collective-permute-done.2.side
  12.4 0.4 %collective-permute-start.5 = (f32[144,128]{1,0:T(8,128)S(1)}, f32[144,128]{1,0:T(8,128)S(1)}, u32[]{:S(2)}, u32[]{:S(2)}) collective-permute-start(f32[144,128]{1,0:T(8,128)S(1)} %collective-permute-done.3.pair), channel_id=1, source_target_pairs={{1,0},{0,1},{3,2},{2,3},{5,4},{4,5},{7,6},{6,7},{9,8},{8,9},{11,10... | collective-permute-start | bytes 221192 | tf_op jit(solution)/shard_map/ppermute | solution.py:212
  12.8 0.2 %collective-permute-start.6 = (f32[144,128]{1,0:T(8,128)S(1)}, f32[144,128]{1,0:T(8,128)S(1)}, u32[]{:S(2)}, u32[]{:S(2)}) collective-permute-start(f32[144,128]{1,0:T(8,128)S(1)} %collective-permute-done.2.side), channel_id=1, source_target_pairs={{1,0},{0,1},{3,2},{2,3},{5,4},{4,5},{7,6},{6,7},{9,8},{8,9},{11,10... | collective-permute-start | bytes 221192 | tf_op jit(solution)/shard_map/ppermute | solution.py:212
  13.0 0.0 copy-done.1
  13.0 0.0 copy-done.2
  13.0 0.6 %shard_map.94 = (bf16[8,128,128]{2,1,0:T(8,128)(2,1)S(1)}, bf16[8,128,128]{2,1,0:T(8,128)(2,1)S(1)}) custom-call(f32[8,8,64,64]{3,2,1,0:T(8,128)S(1)} %copy-done.1, f32[1,8,64,64]{3,2,1,0:T(8,128)S(1)} %copy-done.4, f32[8,64,64]{2,1,0:T(8,128)S(1)} %copy-done.3, f32[8,64,128]{2,1,0:T(8,128)S(1)} %bitcast.2), custom_call_target="tpu_custom_call" | custom-call | flops 1500000000 | tf_op jit(solution)/shard_map/pallas_call | solution.py:250
  13.6 0.1 collective-permute-done.7.third
  13.7 0.0 collective-permute-done.4.beside
  13.7 0.0 collective-permute-done.5.pair_beside
  13.7 0.3 %collective-permute-done.6.side_beside = f32[144,128]{1,0:T(8,128)S(1)} collective-permute-done((f32[144,128]{1,0:T(8,128)S(1)}, f32[144,128]{1,0:T(8,128)S(1)}, u32[]{:S(2)}, u32[]{:S(2)}) %collective-permute-start.6) | collective-permute-done | bytes 73760 | tf_op jit(solution)/shard_map/ppermute | solution.py:212
  14.0 1.1 %shard_map.93.base = f32[8,32,128]{2,1,0:T(8,128)S(1)} custom-call(s32[8,8]{1,0:T(8,128)S(1)} %copy-done.6, s32[1,8]{1,0:T(1,128)S(1)} %copy-done.8, f32[8,32,128]{2,1,0:T(8,128)S(1)} %shard_map.92.near, f32[144,128]{1,0:T(8,128)S(1)} %get-tuple-element.16.own, f32[144,128]{1,0:T(8,128)S(1)} %collective-permute-done.4.beside, ...), custom_call_target="tpu_custom_call" | custom-call | tf_op jit(solution)/shard_map/pallas_call | solution.py:258
  15.1 0.0 collective-permute-done.8.opposite
  15.1 1.0 %shard_map.95 = f32[8,32,128]{2,1,0:T(8,128)} custom-call(f32[8,32,128]{2,1,0:T(8,128)S(1)} %shard_map.93.base, f32[152,128]{1,0:T(8,128)S(1)} %collective-permute-done.8.opposite, bf16[8,128,128]{2,1,0:T(8,128)(2,1)S(1)} %get-tuple-element.21.high, bf16[8,128,128]{2,1,0:T(8,128)(2,1)S(1)} %get-tuple-element.22.low), custom_call_target="tpu_custom_call" | custom-call | tf_op jit(solution)/shard_map/pallas_call | solution.py:270
  (9 shorter events, 0.0 us)
Async XLA Ops:
  0.0 4.8 %collective-permute-start = (f32[8,32,128]{2,1,0:T(8,128)}, f32[8,32,128]{2,1,0:T(8,128)S(1)}, u32[]{:S(2)}, u32[]{:S(2)}) collective-permute-start(f32[8,32,128]{2,1,0:T(8,128)} %own.1), channel_id=1, source_target_pairs={{1,0},{0,1},{3,2},{2,3},{5,4},{4,5},{7,6},{6,7},{9,8},{8,9},{11,10... | collective-permute-start | bytes 393224 | tf_op jit(solution)/shard_map/ppermute | solution.py:212
  0.5 10.4 %collective-permute-start.1 = (f32[8,32,128]{2,1,0:T(8,128)}, f32[8,32,128]{2,1,0:T(8,128)S(1)}, u32[]{:S(2)}, u32[]{:S(2)}) collective-permute-start(f32[8,32,128]{2,1,0:T(8,128)} %own.1), channel_id=1, source_target_pairs={{2,1},{1,2},{4,3},{3,4},{6,5},{5,6},{8,7},{7,8},{10,9},{9,10},{12,... | collective-permute-start | bytes 393224 | tf_op jit(solution)/shard_map/ppermute | solution.py:212
  2.9 8.1 %copy-start = (f32[8,6,128,128]{3,2,1,0:T(8,128)S(1)}, f32[8,6,128,128]{3,2,1,0:T(8,128)}, u32[]{:S(2)}) copy-start(f32[8,6,128,128]{3,2,1,0:T(8,128)} %near_block.1) | copy-start | bytes 9437188
  2.9 8.1 %copy-start.5 = (f32[8,32,128]{2,1,0:T(8,128)S(1)}, f32[8,32,128]{2,1,0:T(8,128)}, u32[]{:S(2)}) copy-start(f32[8,32,128]{2,1,0:T(8,128)} %own.1) | copy-start | bytes 393220
  2.9 8.1 %copy-start.7 = (s32[8,6]{1,0:T(8,128)S(1)}, s32[8,6]{1,0:T(8,128)}, u32[]{:S(2)}) copy-start(s32[8,6]{1,0:T(8,128)} %near_index.1) | copy-start | bytes 580
  4.7 8.3 %copy-start.1 = (f32[8,8,64,64]{3,2,1,0:T(8,128)S(1)}, f32[8,8,64,64]{3,2,1,0:T(8,128)}, u32[]{:S(2)}) copy-start(f32[8,8,64,64]{3,2,1,0:T(8,128)} %far_coupling.3) | copy-start | bytes 3145732
  4.7 8.2 %copy-start.2 = (f32[8,128,64]{1,2,0:T(8,128)S(1)}, f32[8,128,64]{1,2,0:T(8,128)}, u32[]{:S(2)}) copy-start(f32[8,128,64]{1,2,0:T(8,128)} %param.12) | copy-start | bytes 786436
  4.7 8.2 %copy-start.3 = (f32[8,64,64]{2,1,0:T(8,128)S(1)}, f32[8,64,64]{2,1,0:T(8,128)}, u32[]{:S(2)}) copy-start(f32[8,64,64]{2,1,0:T(8,128)} %transfer.3) | copy-start | bytes 393220
  4.8 8.2 %copy-start.4 = (f32[1,8,64,64]{3,2,1,0:T(8,128)S(1)}, f32[1,8,64,64]{3,2,1,0:T(8,128)}, u32[]{:S(2)}) copy-start(f32[1,8,64,64]{3,2,1,0:T(8,128)} %up_coupling.3) | copy-start | bytes 393220
  4.8 7.6 %collective-permute-start.3 = (f32[144,128]{1,0:T(8,128)S(1)}, f32[144,128]{1,0:T(8,128)S(1)}, u32[]{:S(2)}, u32[]{:S(2)}) collective-permute-start(f32[144,128]{1,0:T(8,128)S(1)} %get-tuple-element.16.own), channel_id=1, source_target_pairs={{2,0},{3,1},{0,2},{1,3},{6,4},{7,5},{4,6},{5,7},{10,8},{11,9},{8,1... | collective-permute-start | bytes 221192 | tf_op jit(solution)/shard_map/ppermute | solution.py:212
  4.9 7.5 %collective-permute-start.2 = (f32[144,128]{1,0:T(8,128)S(1)}, f32[144,128]{1,0:T(8,128)S(1)}, u32[]{:S(2)}, u32[]{:S(2)}) collective-permute-start(f32[144,128]{1,0:T(8,128)S(1)} %get-tuple-element.16.own), channel_id=1, source_target_pairs={{4,2},{5,3},{2,4},{3,5},{8,6},{9,7},{6,8},{7,9},{12,10},{13,11},{1... | collective-permute-start | bytes 221192 | tf_op jit(solution)/shard_map/ppermute | solution.py:212
  7.0 8.1 %collective-permute-start.8 = (f32[152,128]{1,0:T(8,128)S(1)}, f32[152,128]{1,0:T(8,128)S(1)}, u32[]{:S(2)}, u32[]{:S(2)}) collective-permute-start(f32[152,128]{1,0:T(8,128)S(1)} %get-tuple-element.20), channel_id=1, source_target_pairs={{8,0},{9,1},{10,2},{11,3},{12,4},{13,5},{14,6},{15,7},{0,8},{1,9},... | collective-permute-start | bytes 233480 | tf_op jit(solution)/shard_map/ppermute | solution.py:212
  9.4 4.4 %collective-permute-start.7 = (f32[144,128]{1,0:T(8,128)S(1)}, f32[144,128]{1,0:T(8,128)S(1)}, u32[]{:S(2)}, u32[]{:S(2)}) collective-permute-start(f32[144,128]{1,0:T(8,128)S(1)} %get-tuple-element.16.own), channel_id=1, source_target_pairs={{4,1},{6,3},{1,4},{8,5},{3,6},{10,7},{5,8},{12,9},{7,10},{14,11},{... | collective-permute-start | bytes 221192 | tf_op jit(solution)/shard_map/ppermute | solution.py:212
  10.9 2.9 %collective-permute-start.4 = (f32[144,128]{1,0:T(8,128)S(1)}, f32[144,128]{1,0:T(8,128)S(1)}, u32[]{:S(2)}, u32[]{:S(2)}) collective-permute-start(f32[144,128]{1,0:T(8,128)S(1)} %get-tuple-element.16.own), channel_id=1, source_target_pairs={{1,0},{0,1},{3,2},{2,3},{5,4},{4,5},{7,6},{6,7},{9,8},{8,9},{11,10... | collective-permute-start | bytes 221192 | tf_op jit(solution)/shard_map/ppermute | solution.py:212
  12.4 1.7 %copy-start.6 = (s32[8,8]{1,0:T(8,128)S(1)}, s32[8,8]{1,0:T(8,128)}, u32[]{:S(2)}) copy-start(s32[8,8]{1,0:T(8,128)} %far_index.1) | copy-start | bytes 772
  12.4 1.7 %copy-start.8 = (s32[1,8]{1,0:T(1,128)S(1)}, s32[1,8]{1,0:T(1,128)}, u32[]{:S(2)}) copy-start(s32[1,8]{1,0:T(1,128)} %up_index.1) | copy-start | bytes 100
  12.4 1.3 %collective-permute-start.5 = (f32[144,128]{1,0:T(8,128)S(1)}, f32[144,128]{1,0:T(8,128)S(1)}, u32[]{:S(2)}, u32[]{:S(2)}) collective-permute-start(f32[144,128]{1,0:T(8,128)S(1)} %collective-permute-done.3.pair), channel_id=1, source_target_pairs={{1,0},{0,1},{3,2},{2,3},{5,4},{4,5},{7,6},{6,7},{9,8},{8,9},{11,10... | collective-permute-start | bytes 221192 | tf_op jit(solution)/shard_map/ppermute | solution.py:212
  12.8 1.3 %collective-permute-start.6 = (f32[144,128]{1,0:T(8,128)S(1)}, f32[144,128]{1,0:T(8,128)S(1)}, u32[]{:S(2)}, u32[]{:S(2)}) collective-permute-start(f32[144,128]{1,0:T(8,128)S(1)} %collective-permute-done.2.side), channel_id=1, source_target_pairs={{1,0},{0,1},{3,2},{2,3},{5,4},{4,5},{7,6},{6,7},{9,8},{8,9},{11,10... | collective-permute-start | bytes 221192 | tf_op jit(solution)/shard_map/ppermute | solution.py:212

commit v5 on v4

--- a/solution.py
+++ b/solution.py
@@ -191,11 +191,10 @@
     opposite = everywhere([((i + count // 2) % count, i) for i in range(count)])
     third = everywhere(mirrored(3))
     across = everywhere(mirrored(1))
-    side = everywhere([(other_side(i), i) for i in range(count) if i not in ends])
+    side = everywhere([(i ^ 1 if i in ends else other_side(i), i) for i in range(count)])
     if groups > 1:
         across += [(g * count + i, (g + 1) % groups * count + i) for g in range(groups) for i in (0, last)]
         third += [(g * count + i, (g + 1) % groups * count + i) for g in range(groups) for i in (0, 2, last - 2, last)]
-        side += [(g * count + i, (g + 1) % groups * count + i) for g in range(groups) for i in ends]
     return beside, across, pair, side, third, opposite
 
 
@@ -235,6 +234,9 @@
     beside = send(own, beside_to)
     whole = jax.ShapeDtypeStruct(vectors.shape, F32)
     parts = jax.ShapeDtypeStruct((leaves, 2 * rank, points), jnp.bfloat16)
+    vectors_across, side, pair = lax.optimization_barrier((vectors_across, side, pair))
+    pair_beside = send(pair, beside_to)
+    side_beside = send(side, beside_to)
     near = pl.pallas_call(
         near_kernel,
         out_shape=whole,
@@ -244,9 +246,6 @@
         compiler_params=room(8),
         cost_estimate=cost(0),
     )(near_index, near_block, vectors, vectors_beside, vectors_across)
-    near, side, pair = lax.optimization_barrier((near, side, pair))
-    pair_beside = send(pair, beside_to)
-    side_beside = send(side, beside_to)
     high, low = pl.pallas_call(
         partner_matrices_kernel,
         out_shape=(parts, parts),

time: 16.2 us -> 16 us (0.988)
  waiting for transfers between devices: 0.47 us -> 0.19 us
    ppermute x9, waiting for transfers between devices: 0.47 us -> 0.19 us  [send(): return lax.ppermute(x, ('groups', 'leaf'), to)]
  transfers between devices with their start and end apart: 9 -> 9, of which waited for: 2 -> 1; matrix products, arithmetic and copies ran while one was open for 0% -> 0% of each run, Pallas kernels for 29% -> 30%
where the time goes in v5:
time: 16 us; the launch traced here: 15.8 us
  starting transfers between devices  9.74 us (61%)
  Pallas kernels  5.71 us (36%)
  waiting for transfers between devices  0.19 us (1%)
    ppermute x9, starting transfers between devices, send(): return lax.ppermute(x, ('groups', 'leaf'), to)  9.74 us
    pallas_call x1, Pallas kernels, per_device(): pl.pallas_call(coeffs_kernel, out_shape=tuple((jax.ShapeDtypeStruct((pack...  1.76 us
    pallas_call x1, Pallas kernels, per_device(): pl.pallas_call(near_kernel, out_shape=whole, in_specs=[VMEM] * 5, out_spe...  1.3 us
    pallas_call x1, Pallas kernels, per_device(): pl.pallas_call(far_kernel, out_shape=whole, in_specs=[VMEM] * 14, out_spe...  1.08 us
    pallas_call x1, Pallas kernels, per_device(): pl.pallas_call(partner_kernel, out_shape=whole, in_specs=[VMEM] * 4, out_...  0.98 us
    pallas_call x1, Pallas kernels, per_device(): pl.pallas_call(partner_matrices_kernel, out_shape=(parts, parts), in_spec...  0.59 us
  transfers between devices with their start and end apart: 9, of which 1 were waited for; matrix products, arithmetic and copies ran while one was open for 0% of the time, Pallas kernels for 30%

profile of v5, /device:TPU:0, one launch (start us, length us, event | category | flops | bytes accessed | tf_op | source)
XLA Modules:
  0.0 15.8 jit_solution(5037227593869687510)
XLA Ops:
  0.0 0.5 %collective-permute-start = (f32[8,32,128]{2,1,0:T(8,128)}, f32[8,32,128]{2,1,0:T(8,128)S(1)}, u32[]{:S(2)}, u32[]{:S(2)}) collective-permute-start(f32[8,32,128]{2,1,0:T(8,128)} %own.1), channel_id=1, source_target_pairs={{1,0},{0,1},{3,2},{2,3},{5,4},{4,5},{7,6},{6,7},{9,8},{8,9},{11,10... | collective-permute-start | bytes 393224 | tf_op jit(solution)/shard_map/ppermute | solution.py:211
  0.5 2.5 %collective-permute-start.1 = (f32[8,32,128]{2,1,0:T(8,128)}, f32[8,32,128]{2,1,0:T(8,128)S(1)}, u32[]{:S(2)}, u32[]{:S(2)}) collective-permute-start(f32[8,32,128]{2,1,0:T(8,128)} %own.1), channel_id=1, source_target_pairs={{2,1},{1,2},{4,3},{3,4},{6,5},{5,6},{8,7},{7,8},{10,9},{9,10},{12,... | collective-permute-start | bytes 393224 | tf_op jit(solution)/shard_map/ppermute | solution.py:211
  3.0 1.8 %shard_map.91 = (f32[144,128]{1,0:T(8,128)S(1)}, f32[152,128]{1,0:T(8,128)S(1)}) custom-call(f32[8,32,128]{2,1,0:T(8,128)} %own.1, f32[8,64,128]{2,1,0:T(8,128)} %bitcast.1, f32[8,64,64]{2,1,0:T(8,128)} %transfer.3), custom_call_target="tpu_custom_call" | custom-call | flops 2500000000 | tf_op jit(solution)/shard_map/pallas_call | solution.py:215
  4.7 0.0 copy-start
  4.7 0.0 copy-start.5
  4.8 0.0 copy-start.7
  4.8 0.0 collective-permute-done.beside
  4.8 0.1 collective-permute-start.3
  4.9 1.3 %collective-permute-start.2 = (f32[144,128]{1,0:T(8,128)S(1)}, f32[144,128]{1,0:T(8,128)S(1)}, u32[]{:S(2)}, u32[]{:S(2)}) collective-permute-start(f32[144,128]{1,0:T(8,128)S(1)} %get-tuple-element.16.own), channel_id=1, source_target_pairs={{1,0},{0,1},{4,2},{5,3},{2,4},{3,5},{8,6},{9,7},{6,8},{7,9},{12,10... | collective-permute-start | bytes 221192 | tf_op jit(solution)/shard_map/ppermute | solution.py:211
  6.2 3.1 %collective-permute-start.8 = (f32[152,128]{1,0:T(8,128)S(1)}, f32[152,128]{1,0:T(8,128)S(1)}, u32[]{:S(2)}, u32[]{:S(2)}) collective-permute-start(f32[152,128]{1,0:T(8,128)S(1)} %get-tuple-element.20), channel_id=1, source_target_pairs={{8,0},{9,1},{10,2},{11,3},{12,4},{13,5},{14,6},{15,7},{0,8},{1,9},... | collective-permute-start | bytes 233480 | tf_op jit(solution)/shard_map/ppermute | solution.py:211
  9.4 1.5 %collective-permute-start.7 = (f32[144,128]{1,0:T(8,128)S(1)}, f32[144,128]{1,0:T(8,128)S(1)}, u32[]{:S(2)}, u32[]{:S(2)}) collective-permute-start(f32[144,128]{1,0:T(8,128)S(1)} %get-tuple-element.16.own), channel_id=1, source_target_pairs={{4,1},{6,3},{1,4},{8,5},{3,6},{10,7},{5,8},{12,9},{7,10},{14,11},{... | collective-permute-start | bytes 221192 | tf_op jit(solution)/shard_map/ppermute | solution.py:211
  10.9 0.0 collective-permute-done.1.across
  10.9 0.2 %collective-permute-start.4 = (f32[144,128]{1,0:T(8,128)S(1)}, f32[144,128]{1,0:T(8,128)S(1)}, u32[]{:S(2)}, u32[]{:S(2)}) collective-permute-start(f32[144,128]{1,0:T(8,128)S(1)} %get-tuple-element.16.own), channel_id=1, source_target_pairs={{1,0},{0,1},{3,2},{2,3},{5,4},{4,5},{7,6},{6,7},{9,8},{8,9},{11,10... | collective-permute-start | bytes 221192 | tf_op jit(solution)/shard_map/ppermute | solution.py:211
  11.1 0.0 collective-permute-done.3.pair
  11.1 0.0 collective-permute-done.2.side
  11.1 0.3 %collective-permute-start.5 = (f32[144,128]{1,0:T(8,128)S(1)}, f32[144,128]{1,0:T(8,128)S(1)}, u32[]{:S(2)}, u32[]{:S(2)}) collective-permute-start(f32[144,128]{1,0:T(8,128)S(1)} %collective-permute-done.3.pair), channel_id=1, source_target_pairs={{1,0},{0,1},{3,2},{2,3},{5,4},{4,5},{7,6},{6,7},{9,8},{8,9},{11,10... | collective-permute-start | bytes 221192 | tf_op jit(solution)/shard_map/ppermute | solution.py:211
  11.4 0.2 %collective-permute-start.6 = (f32[144,128]{1,0:T(8,128)S(1)}, f32[144,128]{1,0:T(8,128)S(1)}, u32[]{:S(2)}, u32[]{:S(2)}) collective-permute-start(f32[144,128]{1,0:T(8,128)S(1)} %collective-permute-done.2.side), channel_id=1, source_target_pairs={{1,0},{0,1},{3,2},{2,3},{5,4},{4,5},{7,6},{6,7},{9,8},{8,9},{11,10... | collective-permute-start | bytes 221192 | tf_op jit(solution)/shard_map/ppermute | solution.py:211
  11.6 0.0 copy-done.1
  11.6 0.0 copy-done.2
  11.6 0.0 copy-done.3
  11.6 0.0 copy-done.4
  11.6 0.6 %shard_map.94 = (bf16[8,128,128]{2,1,0:T(8,128)(2,1)S(1)}, bf16[8,128,128]{2,1,0:T(8,128)(2,1)S(1)}) custom-call(f32[8,8,64,64]{3,2,1,0:T(8,128)S(1)} %copy-done.1, f32[1,8,64,64]{3,2,1,0:T(8,128)S(1)} %copy-done.4, f32[8,64,64]{2,1,0:T(8,128)S(1)} %copy-done.3, f32[8,64,128]{2,1,0:T(8,128)S(1)} %bitcast.2), custom_call_target="tpu_custom_call" | custom-call | flops 1500000000 | tf_op jit(solution)/shard_map/pallas_call | solution.py:249
  12.2 0.0 copy-start.6
  12.2 0.0 copy-start.8
  12.3 1.3 %shard_map.92.near = f32[8,32,128]{2,1,0:T(8,128)S(1)} custom-call(s32[8,6]{1,0:T(8,128)S(1)} %copy-done.7, f32[8,6,128,128]{3,2,1,0:T(8,128)S(1)} %copy-done, f32[8,32,128]{2,1,0:T(8,128)S(1)} %copy-done.5, f32[8,32,128]{2,1,0:T(8,128)S(1)} %collective-permute-done.beside, f32[8,32,128]{2,1,0:T(8,128)S(1)} %collective-permute-done.1.across), custom_call_target="tpu_custom_call" | custom-call | tf_op jit(solution)/shard_map/pallas_call | solution.py:240
  13.6 0.2 %collective-permute-done.7.third = f32[144,128]{1,0:T(8,128)S(1)} collective-permute-done((f32[144,128]{1,0:T(8,128)S(1)}, f32[144,128]{1,0:T(8,128)S(1)}, u32[]{:S(2)}, u32[]{:S(2)}) %collective-permute-start.7) | collective-permute-done | bytes 73760 | tf_op jit(solution)/shard_map/ppermute | solution.py:211
  13.7 0.0 collective-permute-done.4.beside
  13.7 0.0 collective-permute-done.5.pair_beside
  13.7 0.0 collective-permute-done.6.side_beside
  13.8 1.1 %shard_map.93.base = f32[8,32,128]{2,1,0:T(8,128)S(1)} custom-call(s32[8,8]{1,0:T(8,128)S(1)} %copy-done.6, s32[1,8]{1,0:T(1,128)S(1)} %copy-done.8, f32[8,32,128]{2,1,0:T(8,128)S(1)} %shard_map.92.near, f32[144,128]{1,0:T(8,128)S(1)} %get-tuple-element.16.own, f32[144,128]{1,0:T(8,128)S(1)} %collective-permute-done.4.beside, ...), custom_call_target="tpu_custom_call" | custom-call | tf_op jit(solution)/shard_map/pallas_call | solution.py:257
  14.8 0.0 collective-permute-done.8.opposite
  14.8 1.0 %shard_map.95 = f32[8,32,128]{2,1,0:T(8,128)} custom-call(f32[8,32,128]{2,1,0:T(8,128)S(1)} %shard_map.93.base, f32[152,128]{1,0:T(8,128)S(1)} %collective-permute-done.8.opposite, bf16[8,128,128]{2,1,0:T(8,128)(2,1)S(1)} %get-tuple-element.21.high, bf16[8,128,128]{2,1,0:T(8,128)(2,1)S(1)} %get-tuple-element.22.low), custom_call_target="tpu_custom_call" | custom-call | tf_op jit(solution)/shard_map/pallas_call | solution.py:269
  (9 shorter events, 0.0 us)
Async XLA Ops:
  0.0 4.8 %collective-permute-start = (f32[8,32,128]{2,1,0:T(8,128)}, f32[8,32,128]{2,1,0:T(8,128)S(1)}, u32[]{:S(2)}, u32[]{:S(2)}) collective-permute-start(f32[8,32,128]{2,1,0:T(8,128)} %own.1), channel_id=1, source_target_pairs={{1,0},{0,1},{3,2},{2,3},{5,4},{4,5},{7,6},{6,7},{9,8},{8,9},{11,10... | collective-permute-start | bytes 393224 | tf_op jit(solution)/shard_map/ppermute | solution.py:211
  0.5 10.4 %collective-permute-start.1 = (f32[8,32,128]{2,1,0:T(8,128)}, f32[8,32,128]{2,1,0:T(8,128)S(1)}, u32[]{:S(2)}, u32[]{:S(2)}) collective-permute-start(f32[8,32,128]{2,1,0:T(8,128)} %own.1), channel_id=1, source_target_pairs={{2,1},{1,2},{4,3},{3,4},{6,5},{5,6},{8,7},{7,8},{10,9},{9,10},{12,... | collective-permute-start | bytes 393224 | tf_op jit(solution)/shard_map/ppermute | solution.py:211
  2.9 8.6 %copy-start.1 = (f32[8,8,64,64]{3,2,1,0:T(8,128)S(1)}, f32[8,8,64,64]{3,2,1,0:T(8,128)}, u32[]{:S(2)}) copy-start(f32[8,8,64,64]{3,2,1,0:T(8,128)} %far_coupling.3) | copy-start | bytes 3145732
  2.9 8.6 %copy-start.2 = (f32[8,128,64]{1,2,0:T(8,128)S(1)}, f32[8,128,64]{1,2,0:T(8,128)}, u32[]{:S(2)}) copy-start(f32[8,128,64]{1,2,0:T(8,128)} %param.12) | copy-start | bytes 786436
  2.9 8.6 %copy-start.3 = (f32[8,64,64]{2,1,0:T(8,128)S(1)}, f32[8,64,64]{2,1,0:T(8,128)}, u32[]{:S(2)}) copy-start(f32[8,64,64]{2,1,0:T(8,128)} %transfer.3) | copy-start | bytes 393220
  2.9 8.6 %copy-start.4 = (f32[1,8,64,64]{3,2,1,0:T(8,128)S(1)}, f32[1,8,64,64]{3,2,1,0:T(8,128)}, u32[]{:S(2)}) copy-start(f32[1,8,64,64]{3,2,1,0:T(8,128)} %up_coupling.3) | copy-start | bytes 393220
  4.7 7.5 %copy-start = (f32[8,6,128,128]{3,2,1,0:T(8,128)S(1)}, f32[8,6,128,128]{3,2,1,0:T(8,128)}, u32[]{:S(2)}) copy-start(f32[8,6,128,128]{3,2,1,0:T(8,128)} %near_block.1) | copy-start | bytes 9437188
  4.7 7.5 %copy-start.5 = (f32[8,32,128]{2,1,0:T(8,128)S(1)}, f32[8,32,128]{2,1,0:T(8,128)}, u32[]{:S(2)}) copy-start(f32[8,32,128]{2,1,0:T(8,128)} %own.1) | copy-start | bytes 393220
  4.8 7.5 %copy-start.7 = (s32[8,6]{1,0:T(8,128)S(1)}, s32[8,6]{1,0:T(8,128)}, u32[]{:S(2)}) copy-start(s32[8,6]{1,0:T(8,128)} %near_index.1) | copy-start | bytes 580
  4.8 6.3 %collective-permute-start.3 = (f32[144,128]{1,0:T(8,128)S(1)}, f32[144,128]{1,0:T(8,128)S(1)}, u32[]{:S(2)}, u32[]{:S(2)}) collective-permute-start(f32[144,128]{1,0:T(8,128)S(1)} %get-tuple-element.16.own), channel_id=1, source_target_pairs={{2,0},{3,1},{0,2},{1,3},{6,4},{7,5},{4,6},{5,7},{10,8},{11,9},{8,1... | collective-permute-start | bytes 221192 | tf_op jit(solution)/shard_map/ppermute | solution.py:211
  4.9 6.2 %collective-permute-start.2 = (f32[144,128]{1,0:T(8,128)S(1)}, f32[144,128]{1,0:T(8,128)S(1)}, u32[]{:S(2)}, u32[]{:S(2)}) collective-permute-start(f32[144,128]{1,0:T(8,128)S(1)} %get-tuple-element.16.own), channel_id=1, source_target_pairs={{1,0},{0,1},{4,2},{5,3},{2,4},{3,5},{8,6},{9,7},{6,8},{7,9},{12,10... | collective-permute-start | bytes 221192 | tf_op jit(solution)/shard_map/ppermute | solution.py:211
  6.2 8.6 %collective-permute-start.8 = (f32[152,128]{1,0:T(8,128)S(1)}, f32[152,128]{1,0:T(8,128)S(1)}, u32[]{:S(2)}, u32[]{:S(2)}) collective-permute-start(f32[152,128]{1,0:T(8,128)S(1)} %get-tuple-element.20), channel_id=1, source_target_pairs={{8,0},{9,1},{10,2},{11,3},{12,4},{13,5},{14,6},{15,7},{0,8},{1,9},... | collective-permute-start | bytes 233480 | tf_op jit(solution)/shard_map/ppermute | solution.py:211
  9.4 4.4 %collective-permute-start.7 = (f32[144,128]{1,0:T(8,128)S(1)}, f32[144,128]{1,0:T(8,128)S(1)}, u32[]{:S(2)}, u32[]{:S(2)}) collective-permute-start(f32[144,128]{1,0:T(8,128)S(1)} %get-tuple-element.16.own), channel_id=1, source_target_pairs={{4,1},{6,3},{1,4},{8,5},{3,6},{10,7},{5,8},{12,9},{7,10},{14,11},{... | collective-permute-start | bytes 221192 | tf_op jit(solution)/shard_map/ppermute | solution.py:211
  10.9 2.9 %collective-permute-start.4 = (f32[144,128]{1,0:T(8,128)S(1)}, f32[144,128]{1,0:T(8,128)S(1)}, u32[]{:S(2)}, u32[]{:S(2)}) collective-permute-start(f32[144,128]{1,0:T(8,128)S(1)} %get-tuple-element.16.own), channel_id=1, source_target_pairs={{1,0},{0,1},{3,2},{2,3},{5,4},{4,5},{7,6},{6,7},{9,8},{8,9},{11,10... | collective-permute-start | bytes 221192 | tf_op jit(solution)/shard_map/ppermute | solution.py:211
  11.1 2.7 %collective-permute-start.5 = (f32[144,128]{1,0:T(8,128)S(1)}, f32[144,128]{1,0:T(8,128)S(1)}, u32[]{:S(2)}, u32[]{:S(2)}) collective-permute-start(f32[144,128]{1,0:T(8,128)S(1)} %collective-permute-done.3.pair), channel_id=1, source_target_pairs={{1,0},{0,1},{3,2},{2,3},{5,4},{4,5},{7,6},{6,7},{9,8},{8,9},{11,10... | collective-permute-start | bytes 221192 | tf_op jit(solution)/shard_map/ppermute | solution.py:211
  11.4 2.3 %collective-permute-start.6 = (f32[144,128]{1,0:T(8,128)S(1)}, f32[144,128]{1,0:T(8,128)S(1)}, u32[]{:S(2)}, u32[]{:S(2)}) collective-permute-start(f32[144,128]{1,0:T(8,128)S(1)} %collective-permute-done.2.side), channel_id=1, source_target_pairs={{1,0},{0,1},{3,2},{2,3},{5,4},{4,5},{7,6},{6,7},{9,8},{8,9},{11,10... | collective-permute-start | bytes 221192 | tf_op jit(solution)/shard_map/ppermute | solution.py:211
  12.2 1.5 %copy-start.6 = (s32[8,8]{1,0:T(8,128)S(1)}, s32[8,8]{1,0:T(8,128)}, u32[]{:S(2)}) copy-start(s32[8,8]{1,0:T(8,128)} %far_index.1) | copy-start | bytes 772
  12.2 1.5 %copy-start.8 = (s32[1,8]{1,0:T(1,128)S(1)}, s32[1,8]{1,0:T(1,128)}, u32[]{:S(2)}) copy-start(s32[1,8]{1,0:T(1,128)} %up_index.1) | copy-start | bytes 100

commit v6 on v5

--- a/solution.py
+++ b/solution.py
@@ -53,23 +53,14 @@
     return jnp.concatenate([x[:half], x[half:]], axis=1)
 
 
-def coeffs_kernel(vectors_in, basis_in, transfer_in, coeffs, longer, vectors, basis, transfer, arrived):
+def coeffs_kernel(vectors, basis, transfer, coeffs, longer):
     leaves, rows, points = vectors.shape
-    copies = [
-        pltpu.make_async_copy(there, here, arrived.at[i])
-        for i, (there, here) in enumerate(((vectors_in, vectors), (basis_in, basis), (transfer_in, transfer)))
-    ]
-    for copy in copies:
-        copy.start()
-    copies[0].wait()
-    copies[1].wait()
     rank = basis.shape[1]
     half = rows // 2
     parts = []
     for l in range(leaves):
         parts.append(dot(vectors[l], basis[l], NT))
     whole = jnp.concatenate(parts, axis=1)
-    copies[2].wait()
     parts.append(dot(whole, transfer[...].reshape(leaves * rank, rank), NN))
     for i, part in enumerate(parts):
         packed = pack(part)
@@ -183,18 +174,17 @@
         return [(g * count + j, g * count + i) for g in range(groups) for j, i in pairs]
 
     def mirrored(step):
-        wanted = [(i - step, i) if i % 2 == 0 else (i + step, i) for i in range(count)]
-        return [(j, i) for j, i in wanted if 0 <= j <= last]
+        sources = [i - step if i % 2 == 0 else i + step for i in range(count)]
+        return [(j if 0 <= j <= last else i ^ 1, i) for i, j in enumerate(sources)]
 
     beside = everywhere([(i ^ 1, i) for i in range(count)])
     pair = everywhere([(i ^ 2, i) for i in range(count)])
-    opposite = everywhere([((i + count // 2) % count, i) for i in range(count)])
-    third = everywhere(mirrored(3))
-    across = everywhere(mirrored(1))
+    opposite = everywhere([((i + count // 2) % count ^ 1, i) for i in range(count)])
+    third = everywhere(mirrored(4))
+    across = everywhere([(i - 1 if i % 2 == 0 else i + 1, i) for i in range(count) if i not in (0, last)])
     side = everywhere([(i ^ 1 if i in ends else other_side(i), i) for i in range(count)])
     if groups > 1:
         across += [(g * count + i, (g + 1) % groups * count + i) for g in range(groups) for i in (0, last)]
-        third += [(g * count + i, (g + 1) % groups * count + i) for g in range(groups) for i in (0, 2, last - 2, last)]
     return beside, across, pair, side, third, opposite
 
 
@@ -210,31 +200,26 @@
     def send(x, to):
         return lax.ppermute(x, ("groups", "leaf"), to)
 
+    basis_beside = send(basis, beside_to)
+    transfer_beside = send(transfer, beside_to)
+    vectors_beside = send(vectors, beside_to)
     vectors_across = send(vectors, across_to)
-    vectors_beside = send(vectors, beside_to)
-    own, own_longer = pl.pallas_call(
+    theirs, theirs_longer = pl.pallas_call(
         coeffs_kernel,
         out_shape=tuple(jax.ShapeDtypeStruct((packed + extra, points), F32) for extra in (0, 8)),
-        in_specs=[HBM] * 3,
+        in_specs=[VMEM] * 3,
         out_specs=(VMEM, VMEM),
-        scratch_shapes=[
-            pltpu.VMEM(vectors.shape, F32),
-            pltpu.VMEM(basis.shape, F32),
-            pltpu.VMEM(transfer.shape, F32),
-            pltpu.SemaphoreType.DMA((3,)),
-        ],
         compiler_params=room(4),
         cost_estimate=cost(5),
-    )(*(pltpu.with_memory_space_constraint(x, pltpu.HBM) for x in (vectors, basis, transfer)))
-    own, vectors_beside = lax.optimization_barrier((own, vectors_beside))
-    pair = send(own, pair_to)
-    side = send(own, side_to)
-    opposite = send(own_longer, opposite_to)
-    third = send(own, third_to)
-    beside = send(own, beside_to)
+    )(vectors_beside, basis_beside, transfer_beside)
+    pair = send(theirs, pair_to)
+    side = send(theirs, side_to)
+    opposite = send(theirs_longer, opposite_to)
+    third = send(theirs, third_to)
+    own = send(theirs, beside_to)
     whole = jax.ShapeDtypeStruct(vectors.shape, F32)
     parts = jax.ShapeDtypeStruct((leaves, 2 * rank, points), jnp.bfloat16)
-    vectors_across, side, pair = lax.optimization_barrier((vectors_across, side, pair))
+    vectors_across, pair, side = lax.optimization_barrier((vectors_across, pair, side))
     pair_beside = send(pair, beside_to)
     side_beside = send(side, beside_to)
     near = pl.pallas_call(
@@ -252,7 +237,7 @@
         in_specs=[VMEM] * 4,
         out_specs=(VMEM, VMEM),
         compiler_params=room(4),
-        cost_estimate=cost(3),
+        cost_estimate=cost(0),
     )(far_coupling, up_coupling, transfer, basis)
     base = pl.pallas_call(
         far_kernel,
@@ -263,7 +248,7 @@
         compiler_params=room(10),
         cost_estimate=cost(0),
     )(
-        far_index, up_index, near, own, beside, pair, pair_beside, side, side_beside, third,
+        far_index, up_index, near, own, theirs, pair_beside, pair, side_beside, side, third,
         far_coupling, up_coupling, transfer, basis,
     )
     return pl.pallas_call(

time: 16 us -> 15.6 us (0.975)
  the two profiles are of different devices: /device:TPU:0 before, /device:TPU:27 now
where the time goes in v6:
time: 15.6 us; the launch traced here: 15.5 us
  starting transfers between devices  6.97 us (45%)
  Pallas kernels  4.5 us (29%)
  waiting for transfers between devices  3.84 us (25%)
    ppermute x11, starting transfers between devices, send(): return lax.ppermute(x, ('groups', 'leaf'), to)  6.97 us
    ppermute x11, waiting for transfers between devices, send(): return lax.ppermute(x, ('groups', 'leaf'), to)  3.84 us
    pallas_call x1, Pallas kernels, per_device(): pl.pallas_call(near_kernel, out_shape=whole, in_specs=[VMEM] * 5, out_spe...  1.3 us
    pallas_call x1, Pallas kernels, per_device(): pl.pallas_call(far_kernel, out_shape=whole, in_specs=[VMEM] * 14, out_spe...  1.08 us
    pallas_call x1, Pallas kernels, per_device(): pl.pallas_call(partner_kernel, out_shape=whole, in_specs=[VMEM] * 4, out_...  0.98 us
    pallas_call x1, Pallas kernels, per_device(): pl.pallas_call(partner_matrices_kernel, out_shape=(parts, parts), in_spec...  0.59 us
    pallas_call x1, Pallas kernels, per_device(): pl.pallas_call(coeffs_kernel, out_shape=tuple((jax.ShapeDtypeStruct((pack...  0.55 us
  transfers between devices with their start and end apart: 11, of which 2 were waited for; matrix products, arithmetic and copies ran while one was open for 0% of the time, Pallas kernels for 23%

profile of v6, /device:TPU:27, one launch (start us, length us, event | category | flops | bytes accessed | tf_op | source)
XLA Modules:
  0.0 15.5 jit_solution(16511424746362152311)
XLA Ops:
  0.0 0.0 copy-start.4
  0.0 0.0 copy-start.5
  0.0 0.7 %collective-permute-start.2 = (f32[8,64,128]{2,1,0:T(8,128)}, f32[8,64,128]{2,1,0:T(8,128)S(1)}, u32[]{:S(2)}, u32[]{:S(2)}) collective-permute-start(f32[8,64,128]{2,1,0:T(8,128)} %bitcast.1), channel_id=1, source_target_pairs={{1,0},{0,1},{3,2},{2,3},{5,4},{4,5},{7,6},{6,7},{9,8},{8,9},{11,10... | collective-permute-start | bytes 786440 | tf_op jit(solution)/shard_map/ppermute | solution.py:201
  0.8 0.1 collective-permute-start
  0.9 0.4 %collective-permute-start.3 = (f32[8,64,64]{2,1,0:T(8,128)}, f32[8,64,64]{2,1,0:T(8,128)S(1)}, u32[]{:S(2)}, u32[]{:S(2)}) collective-permute-start(f32[8,64,64]{2,1,0:T(8,128)} %transfer.3), channel_id=1, source_target_pairs={{1,0},{0,1},{3,2},{2,3},{5,4},{4,5},{7,6},{6,7},{9,8},{8,9},{11,10... | collective-permute-start | bytes 393224 | tf_op jit(solution)/shard_map/ppermute | solution.py:201
  1.3 1.2 %collective-permute-start.1 = (f32[8,32,128]{2,1,0:T(8,128)}, f32[8,32,128]{2,1,0:T(8,128)S(1)}, u32[]{:S(2)}, u32[]{:S(2)}) collective-permute-start(f32[8,32,128]{2,1,0:T(8,128)} %own.1), channel_id=1, source_target_pairs={{2,1},{1,2},{4,3},{3,4},{6,5},{5,6},{8,7},{7,8},{10,9},{9,10},{12,... | collective-permute-start | bytes 393224 | tf_op jit(solution)/shard_map/ppermute | solution.py:201
  2.5 0.0 collective-permute-done.vectors.beside
  2.5 0.2 %collective-permute-done.3.transfer = f32[8,64,64]{2,1,0:T(8,128)S(1)} collective-permute-done((f32[8,64,64]{2,1,0:T(8,128)}, f32[8,64,64]{2,1,0:T(8,128)S(1)}, u32[]{:S(2)}, u32[]{:S(2)}) %collective-permute-start.3) | collective-permute-done | bytes 131104 | tf_op jit(solution)/shard_map/ppermute | solution.py:201
  2.7 0.0 collective-permute-done.2.basis
  2.7 0.5 %shard_map.91 = (f32[144,128]{1,0:T(8,128)S(1)}, f32[152,128]{1,0:T(8,128)S(1)}) custom-call(f32[8,32,128]{2,1,0:T(8,128)S(1)} %collective-permute-done.vectors.beside, f32[8,64,128]{2,1,0:T(8,128)S(1)} %collective-permute-done.2.basis, f32[8,64,64]{2,1,0:T(8,128)S(1)} %collective-permute-done.3.transfer), custom_call_target="tpu_custom_call" | custom-call | flops 2500000000 | tf_op jit(solution)/shard_map/pallas_call | solution.py:207
  3.3 1.2 %collective-permute-start.4 = (f32[144,128]{1,0:T(8,128)S(1)}, f32[144,128]{1,0:T(8,128)S(1)}, u32[]{:S(2)}, u32[]{:S(2)}) collective-permute-start(f32[144,128]{1,0:T(8,128)S(1)} %get-tuple-element.12.beside), channel_id=1, source_target_pairs={{2,0},{3,1},{0,2},{1,3},{6,4},{7,5},{4,6},{5,7},{10,8},{11,9},{8,1... | collective-permute-start | bytes 221192 | tf_op jit(solution)/shard_map/ppermute | solution.py:201
  4.5 0.1 collective-permute-start.5
  4.6 0.9 %collective-permute-start.10 = (f32[152,128]{1,0:T(8,128)S(1)}, f32[152,128]{1,0:T(8,128)S(1)}, u32[]{:S(2)}, u32[]{:S(2)}) collective-permute-start(f32[152,128]{1,0:T(8,128)S(1)} %get-tuple-element.16), channel_id=1, source_target_pairs={{9,0},{8,1},{11,2},{10,3},{13,4},{12,5},{15,6},{14,7},{1,8},{0,9},... | collective-permute-start | bytes 233480 | tf_op jit(solution)/shard_map/ppermute | solution.py:201
  5.5 0.1 collective-permute-start.6
  5.6 3.6 %collective-permute-done.1.across = f32[8,32,128]{2,1,0:T(8,128)S(1)} collective-permute-done((f32[8,32,128]{2,1,0:T(8,128)}, f32[8,32,128]{2,1,0:T(8,128)S(1)}, u32[]{:S(2)}, u32[]{:S(2)}) %collective-permute-start.1) | collective-permute-done | bytes 131104 | tf_op jit(solution)/shard_map/ppermute | solution.py:201
  9.2 0.2 %collective-permute-start.9 = (f32[144,128]{1,0:T(8,128)S(1)}, f32[144,128]{1,0:T(8,128)S(1)}, u32[]{:S(2)}, u32[]{:S(2)}) collective-permute-start(f32[144,128]{1,0:T(8,128)S(1)} %get-tuple-element.12.beside), channel_id=1, source_target_pairs={{1,0},{5,1},{3,2},{7,3},{0,4},{9,5},{2,6},{11,7},{4,8},{13,9},{6,1... | collective-permute-start | bytes 221192 | tf_op jit(solution)/shard_map/ppermute | solution.py:201
  9.3 0.0 collective-permute-done.4.pair_beside
  9.3 0.0 collective-permute-done.5.side_beside
  9.4 2.0 %collective-permute-start.7 = (f32[144,128]{1,0:T(8,128)S(1)}, f32[144,128]{1,0:T(8,128)S(1)}, u32[]{:S(2)}, u32[]{:S(2)}) collective-permute-start(f32[144,128]{1,0:T(8,128)S(1)} %collective-permute-done.4.pair_beside), channel_id=1, source_target_pairs={{1,0},{0,1},{3,2},{2,3},{5,4},{4,5},{7,6},{6,7},{9,8},{8,9},{11,10... | collective-permute-start | bytes 221192 | tf_op jit(solution)/shard_map/ppermute | solution.py:201
  11.4 0.0 collective-permute-start.8
  11.4 0.6 %shard_map.94 = (bf16[8,128,128]{2,1,0:T(8,128)(2,1)S(1)}, bf16[8,128,128]{2,1,0:T(8,128)(2,1)S(1)}) custom-call(f32[8,8,64,64]{3,2,1,0:T(8,128)S(1)} %copy-done, f32[1,8,64,64]{3,2,1,0:T(8,128)S(1)} %copy-done.4, f32[8,64,64]{2,1,0:T(8,128)S(1)} %copy-done.3, f32[8,64,128]{2,1,0:T(8,128)S(1)} %bitcast.2), custom_call_target="tpu_custom_call" | custom-call | tf_op jit(solution)/shard_map/pallas_call | solution.py:234
  12.0 0.0 copy-done.5
  12.0 0.0 copy-done.7
  12.0 0.0 copy-done.1
  12.1 1.3 %shard_map.92.near = f32[8,32,128]{2,1,0:T(8,128)S(1)} custom-call(s32[8,6]{1,0:T(8,128)S(1)} %copy-done.7, f32[8,6,128,128]{3,2,1,0:T(8,128)S(1)} %copy-done.1, f32[8,32,128]{2,1,0:T(8,128)S(1)} %copy-done.5, f32[8,32,128]{2,1,0:T(8,128)S(1)} %collective-permute-done.vectors.beside, f32[8,32,128]{2,1,0:T(8,128)S(1)} %collective-permute-done.1.across), custom_call_target="tpu_custom_call" | custom-call | tf_op jit(solution)/shard_map/pallas_call | solution.py:225
  13.4 0.0 collective-permute-done.6.own
  13.4 0.0 collective-permute-done.9.third
  13.4 0.0 collective-permute-done.7.pair
  13.4 0.0 collective-permute-done.8.side
  13.4 1.1 %shard_map.93.base = f32[8,32,128]{2,1,0:T(8,128)S(1)} custom-call(s32[8,8]{1,0:T(8,128)S(1)} %copy-done.6, s32[1,8]{1,0:T(1,128)S(1)} %copy-done.8, f32[8,32,128]{2,1,0:T(8,128)S(1)} %shard_map.92.near, f32[144,128]{1,0:T(8,128)S(1)} %collective-permute-done.6.own, f32[144,128]{1,0:T(8,128)S(1)} %get-tuple-element.12.beside, ...), custom_call_target="tpu_custom_call" | custom-call | tf_op jit(solution)/shard_map/pallas_call | solution.py:242
  14.5 0.0 collective-permute-done.10.opposite
  14.5 1.0 %shard_map.95 = f32[8,32,128]{2,1,0:T(8,128)} custom-call(f32[8,32,128]{2,1,0:T(8,128)S(1)} %shard_map.93.base, f32[152,128]{1,0:T(8,128)S(1)} %collective-permute-done.10.opposite, bf16[8,128,128]{2,1,0:T(8,128)(2,1)S(1)} %get-tuple-element.17.high, bf16[8,128,128]{2,1,0:T(8,128)(2,1)S(1)} %get-tuple-element.18.low), custom_call_target="tpu_custom_call" | custom-call | tf_op jit(solution)/shard_map/pallas_call | solution.py:254
  (13 shorter events, 0.0 us)
Async XLA Ops:
  0.0 11.4 %copy-start = (f32[8,8,64,64]{3,2,1,0:T(8,128)S(1)}, f32[8,8,64,64]{3,2,1,0:T(8,128)}, u32[]{:S(2)}) copy-start(f32[8,8,64,64]{3,2,1,0:T(8,128)} %far_coupling.3) | copy-start | bytes 3145732
  0.0 11.4 %copy-start.2 = (f32[8,128,64]{1,2,0:T(8,128)S(1)}, f32[8,128,64]{1,2,0:T(8,128)}, u32[]{:S(2)}) copy-start(f32[8,128,64]{1,2,0:T(8,128)} %param.12) | copy-start | bytes 786436
  0.0 11.4 %copy-start.3 = (f32[8,64,64]{2,1,0:T(8,128)S(1)}, f32[8,64,64]{2,1,0:T(8,128)}, u32[]{:S(2)}) copy-start(f32[8,64,64]{2,1,0:T(8,128)} %transfer.3) | copy-start | bytes 393220
  0.0 11.4 %copy-start.4 = (f32[1,8,64,64]{3,2,1,0:T(8,128)S(1)}, f32[1,8,64,64]{3,2,1,0:T(8,128)}, u32[]{:S(2)}) copy-start(f32[1,8,64,64]{3,2,1,0:T(8,128)} %up_coupling.3) | copy-start | bytes 393220
  0.0 12.0 %copy-start.5 = (f32[8,32,128]{2,1,0:T(8,128)S(1)}, f32[8,32,128]{2,1,0:T(8,128)}, u32[]{:S(2)}) copy-start(f32[8,32,128]{2,1,0:T(8,128)} %own.1) | copy-start | bytes 393220
  0.0 12.0 %copy-start.7 = (s32[8,6]{1,0:T(8,128)S(1)}, s32[8,6]{1,0:T(8,128)}, u32[]{:S(2)}) copy-start(s32[8,6]{1,0:T(8,128)} %near_index.1) | copy-start | bytes 580
  0.0 2.7 %collective-permute-start.2 = (f32[8,64,128]{2,1,0:T(8,128)}, f32[8,64,128]{2,1,0:T(8,128)S(1)}, u32[]{:S(2)}, u32[]{:S(2)}) collective-permute-start(f32[8,64,128]{2,1,0:T(8,128)} %bitcast.1), channel_id=1, source_target_pairs={{1,0},{0,1},{3,2},{2,3},{5,4},{4,5},{7,6},{6,7},{9,8},{8,9},{11,10... | collective-permute-start | bytes 786440 | tf_op jit(solution)/shard_map/ppermute | solution.py:201
  0.8 1.7 %collective-permute-start = (f32[8,32,128]{2,1,0:T(8,128)}, f32[8,32,128]{2,1,0:T(8,128)S(1)}, u32[]{:S(2)}, u32[]{:S(2)}) collective-permute-start(f32[8,32,128]{2,1,0:T(8,128)} %own.1), channel_id=1, source_target_pairs={{1,0},{0,1},{3,2},{2,3},{5,4},{4,5},{7,6},{6,7},{9,8},{8,9},{11,10... | collective-permute-start | bytes 393224 | tf_op jit(solution)/shard_map/ppermute | solution.py:201
  0.9 1.9 %collective-permute-start.3 = (f32[8,64,64]{2,1,0:T(8,128)}, f32[8,64,64]{2,1,0:T(8,128)S(1)}, u32[]{:S(2)}, u32[]{:S(2)}) collective-permute-start(f32[8,64,64]{2,1,0:T(8,128)} %transfer.3), channel_id=1, source_target_pairs={{1,0},{0,1},{3,2},{2,3},{5,4},{4,5},{7,6},{6,7},{9,8},{8,9},{11,10... | collective-permute-start | bytes 393224 | tf_op jit(solution)/shard_map/ppermute | solution.py:201
  1.3 7.9 %collective-permute-start.1 = (f32[8,32,128]{2,1,0:T(8,128)}, f32[8,32,128]{2,1,0:T(8,128)S(1)}, u32[]{:S(2)}, u32[]{:S(2)}) collective-permute-start(f32[8,32,128]{2,1,0:T(8,128)} %own.1), channel_id=1, source_target_pairs={{2,1},{1,2},{4,3},{3,4},{6,5},{5,6},{8,7},{7,8},{10,9},{9,10},{12,... | collective-permute-start | bytes 393224 | tf_op jit(solution)/shard_map/ppermute | solution.py:201
  2.7 9.3 %copy-start.1 = (f32[8,6,128,128]{3,2,1,0:T(8,128)S(1)}, f32[8,6,128,128]{3,2,1,0:T(8,128)}, u32[]{:S(2)}) copy-start(f32[8,6,128,128]{3,2,1,0:T(8,128)} %near_block.1) | copy-start | bytes 9437188
  3.3 6.1 %collective-permute-start.4 = (f32[144,128]{1,0:T(8,128)S(1)}, f32[144,128]{1,0:T(8,128)S(1)}, u32[]{:S(2)}, u32[]{:S(2)}) collective-permute-start(f32[144,128]{1,0:T(8,128)S(1)} %get-tuple-element.12.beside), channel_id=1, source_target_pairs={{2,0},{3,1},{0,2},{1,3},{6,4},{7,5},{4,6},{5,7},{10,8},{11,9},{8,1... | collective-permute-start | bytes 221192 | tf_op jit(solution)/shard_map/ppermute | solution.py:201
  4.5 4.8 %collective-permute-start.5 = (f32[144,128]{1,0:T(8,128)S(1)}, f32[144,128]{1,0:T(8,128)S(1)}, u32[]{:S(2)}, u32[]{:S(2)}) collective-permute-start(f32[144,128]{1,0:T(8,128)S(1)} %get-tuple-element.12.beside), channel_id=1, source_target_pairs={{1,0},{0,1},{4,2},{5,3},{2,4},{3,5},{8,6},{9,7},{6,8},{7,9},{12,10... | collective-permute-start | bytes 221192 | tf_op jit(solution)/shard_map/ppermute | solution.py:201
  4.6 8.8 %copy-start.6 = (s32[8,8]{1,0:T(8,128)S(1)}, s32[8,8]{1,0:T(8,128)}, u32[]{:S(2)}) copy-start(s32[8,8]{1,0:T(8,128)} %far_index.1) | copy-start | bytes 772
  4.6 8.8 %copy-start.8 = (s32[1,8]{1,0:T(1,128)S(1)}, s32[1,8]{1,0:T(1,128)}, u32[]{:S(2)}) copy-start(s32[1,8]{1,0:T(1,128)} %up_index.1) | copy-start | bytes 100
  4.6 9.9 %collective-permute-start.10 = (f32[152,128]{1,0:T(8,128)S(1)}, f32[152,128]{1,0:T(8,128)S(1)}, u32[]{:S(2)}, u32[]{:S(2)}) collective-permute-start(f32[152,128]{1,0:T(8,128)S(1)} %get-tuple-element.16), channel_id=1, source_target_pairs={{9,0},{8,1},{11,2},{10,3},{13,4},{12,5},{15,6},{14,7},{1,8},{0,9},... | collective-permute-start | bytes 233480 | tf_op jit(solution)/shard_map/ppermute | solution.py:201
  5.5 7.9 %collective-permute-start.6 = (f32[144,128]{1,0:T(8,128)S(1)}, f32[144,128]{1,0:T(8,128)S(1)}, u32[]{:S(2)}, u32[]{:S(2)}) collective-permute-start(f32[144,128]{1,0:T(8,128)S(1)} %get-tuple-element.12.beside), channel_id=1, source_target_pairs={{1,0},{0,1},{3,2},{2,3},{5,4},{4,5},{7,6},{6,7},{9,8},{8,9},{11,10... | collective-permute-start | bytes 221192 | tf_op jit(solution)/shard_map/ppermute | solution.py:201
  9.2 4.2 %collective-permute-start.9 = (f32[144,128]{1,0:T(8,128)S(1)}, f32[144,128]{1,0:T(8,128)S(1)}, u32[]{:S(2)}, u32[]{:S(2)}) collective-permute-start(f32[144,128]{1,0:T(8,128)S(1)} %get-tuple-element.12.beside), channel_id=1, source_target_pairs={{1,0},{5,1},{3,2},{7,3},{0,4},{9,5},{2,6},{11,7},{4,8},{13,9},{6,1... | collective-permute-start | bytes 221192 | tf_op jit(solution)/shard_map/ppermute | solution.py:201
  9.4 4.0 %collective-permute-start.7 = (f32[144,128]{1,0:T(8,128)S(1)}, f32[144,128]{1,0:T(8,128)S(1)}, u32[]{:S(2)}, u32[]{:S(2)}) collective-permute-start(f32[144,128]{1,0:T(8,128)S(1)} %collective-permute-done.4.pair_beside), channel_id=1, source_target_pairs={{1,0},{0,1},{3,2},{2,3},{5,4},{4,5},{7,6},{6,7},{9,8},{8,9},{11,10... | collective-permute-start | bytes 221192 | tf_op jit(solution)/shard_map/ppermute | solution.py:201
  11.4 2.0 %collective-permute-start.8 = (f32[144,128]{1,0:T(8,128)S(1)}, f32[144,128]{1,0:T(8,128)S(1)}, u32[]{:S(2)}, u32[]{:S(2)}) collective-permute-start(f32[144,128]{1,0:T(8,128)S(1)} %collective-permute-done.5.side_beside), channel_id=1, source_target_pairs={{1,0},{0,1},{3,2},{2,3},{5,4},{4,5},{7,6},{6,7},{9,8},{8,9},{11,10... | collective-permute-start | bytes 221192 | tf_op jit(solution)/shard_map/ppermute | solution.py:201

commit v7 on v6

--- a/solution.py
+++ b/solution.py
@@ -216,10 +216,18 @@
     side = send(theirs, side_to)
     opposite = send(theirs_longer, opposite_to)
     third = send(theirs, third_to)
-    own = send(theirs, beside_to)
+    own = send(theirs_longer, beside_to)
     whole = jax.ShapeDtypeStruct(vectors.shape, F32)
     parts = jax.ShapeDtypeStruct((leaves, 2 * rank, points), jnp.bfloat16)
-    vectors_across, pair, side = lax.optimization_barrier((vectors_across, pair, side))
+    high, low = pl.pallas_call(
+        partner_matrices_kernel,
+        out_shape=(parts, parts),
+        in_specs=[VMEM] * 4,
+        out_specs=(VMEM, VMEM),
+        compiler_params=room(4),
+        cost_estimate=cost(0),
+    )(far_coupling, up_coupling, transfer, basis)
+    vectors_across, side, pair, high, low = lax.optimization_barrier((vectors_across, side, pair, high, low))
     pair_beside = send(pair, beside_to)
     side_beside = send(side, beside_to)
     near = pl.pallas_call(
@@ -231,14 +239,6 @@
         compiler_params=room(8),
         cost_estimate=cost(0),
     )(near_index, near_block, vectors, vectors_beside, vectors_across)
-    high, low = pl.pallas_call(
-        partner_matrices_kernel,
-        out_shape=(parts, parts),
-        in_specs=[VMEM] * 4,
-        out_specs=(VMEM, VMEM),
-        compiler_params=room(4),
-        cost_estimate=cost(0),
-    )(far_coupling, up_coupling, transfer, basis)
     base = pl.pallas_call(
         far_kernel,
         out_shape=whole,

time: 15.6 us -> 15.5 us (level)
  the two profiles are of different devices: /device:TPU:27 before, /device:TPU:0 now
where the time goes in v7:
time: 15.5 us; the launch traced here: 15.4 us
  starting transfers between devices  10.5 us (68%)
  Pallas kernels  4.51 us (29%)
  waiting for transfers between devices  0.19 us (1%)
    ppermute x11, starting transfers between devices, send(): return lax.ppermute(x, ('groups', 'leaf'), to)  10.5 us
    pallas_call x1, Pallas kernels, per_device(): pl.pallas_call(near_kernel, out_shape=whole, in_specs=[VMEM] * 5, out_spe...  1.3 us
    pallas_call x1, Pallas kernels, per_device(): pl.pallas_call(far_kernel, out_shape=whole, in_specs=[VMEM] * 14, out_spe...  1.09 us
    pallas_call x1, Pallas kernels, per_device(): pl.pallas_call(partner_kernel, out_shape=whole, in_specs=[VMEM] * 4, out_...  0.98 us
    pallas_call x1, Pallas kernels, per_device(): pl.pallas_call(partner_matrices_kernel, out_shape=(parts, parts), in_spec...  0.59 us
    pallas_call x1, Pallas kernels, per_device(): pl.pallas_call(coeffs_kernel, out_shape=tuple((jax.ShapeDtypeStruct((pack...  0.55 us
  transfers between devices with their start and end apart: 11, of which 1 were waited for; matrix products, arithmetic and copies ran while one was open for 0% of the time, Pallas kernels for 23%

profile of v7, /device:TPU:0, one launch (start us, length us, event | category | flops | bytes accessed | tf_op | source)
XLA Modules:
  0.0 15.4 jit_solution(6503567807581068435)
XLA Ops:
  0.0 0.0 copy-start.6
  0.0 0.5 %collective-permute-start.2 = (f32[8,64,128]{2,1,0:T(8,128)}, f32[8,64,128]{2,1,0:T(8,128)S(1)}, u32[]{:S(2)}, u32[]{:S(2)}) collective-permute-start(f32[8,64,128]{2,1,0:T(8,128)} %bitcast.1), channel_id=1, source_target_pairs={{1,0},{0,1},{3,2},{2,3},{5,4},{4,5},{7,6},{6,7},{9,8},{8,9},{11,10... | collective-permute-start | bytes 786440 | tf_op jit(solution)/shard_map/ppermute | solution.py:201
  0.6 0.1 collective-permute-start
  0.6 0.4 %collective-permute-start.3 = (f32[8,64,64]{2,1,0:T(8,128)}, f32[8,64,64]{2,1,0:T(8,128)S(1)}, u32[]{:S(2)}, u32[]{:S(2)}) collective-permute-start(f32[8,64,64]{2,1,0:T(8,128)} %transfer.3), channel_id=1, source_target_pairs={{1,0},{0,1},{3,2},{2,3},{5,4},{4,5},{7,6},{6,7},{9,8},{8,9},{11,10... | collective-permute-start | bytes 393224 | tf_op jit(solution)/shard_map/ppermute | solution.py:201
  1.1 2.6 %collective-permute-start.1 = (f32[8,32,128]{2,1,0:T(8,128)}, f32[8,32,128]{2,1,0:T(8,128)S(1)}, u32[]{:S(2)}, u32[]{:S(2)}) collective-permute-start(f32[8,32,128]{2,1,0:T(8,128)} %own.1), channel_id=1, source_target_pairs={{2,1},{1,2},{4,3},{3,4},{6,5},{5,6},{8,7},{7,8},{10,9},{9,10},{12,... | collective-permute-start | bytes 393224 | tf_op jit(solution)/shard_map/ppermute | solution.py:201
  3.6 0.0 collective-permute-done.vectors.beside
  3.6 0.0 collective-permute-done.3.transfer
  3.6 0.0 collective-permute-done.2.basis
  3.7 0.5 %shard_map.91 = (f32[144,128]{1,0:T(8,128)S(1)}, f32[152,128]{1,0:T(8,128)S(1)}) custom-call(f32[8,32,128]{2,1,0:T(8,128)S(1)} %collective-permute-done.vectors.beside, f32[8,64,128]{2,1,0:T(8,128)S(1)} %collective-permute-done.2.basis, f32[8,64,64]{2,1,0:T(8,128)S(1)} %collective-permute-done.3.transfer), custom_call_target="tpu_custom_call" | custom-call | flops 2500000000 | tf_op jit(solution)/shard_map/pallas_call | solution.py:207
  4.2 1.7 %collective-permute-start.5 = (f32[144,128]{1,0:T(8,128)S(1)}, f32[144,128]{1,0:T(8,128)S(1)}, u32[]{:S(2)}, u32[]{:S(2)}) collective-permute-start(f32[144,128]{1,0:T(8,128)S(1)} %get-tuple-element.14.beside), channel_id=1, source_target_pairs={{2,0},{3,1},{0,2},{1,3},{6,4},{7,5},{4,6},{5,7},{10,8},{11,9},{8,1... | collective-permute-start | bytes 221192 | tf_op jit(solution)/shard_map/ppermute | solution.py:201
  5.9 0.0 collective-permute-start.4
  5.9 0.5 %collective-permute-start.6 = (f32[152,128]{1,0:T(8,128)S(1)}, f32[152,128]{1,0:T(8,128)S(1)}, u32[]{:S(2)}, u32[]{:S(2)}) collective-permute-start(f32[152,128]{1,0:T(8,128)S(1)} %get-tuple-element.18), channel_id=1, source_target_pairs={{1,0},{0,1},{3,2},{2,3},{5,4},{4,5},{7,6},{6,7},{9,8},{8,9},{11,10... | collective-permute-start | bytes 233480 | tf_op jit(solution)/shard_map/ppermute | solution.py:201
  6.5 2.6 %collective-permute-start.10 = (f32[152,128]{1,0:T(8,128)S(1)}, f32[152,128]{1,0:T(8,128)S(1)}, u32[]{:S(2)}, u32[]{:S(2)}) collective-permute-start(f32[152,128]{1,0:T(8,128)S(1)} %get-tuple-element.18), channel_id=1, source_target_pairs={{9,0},{8,1},{11,2},{10,3},{13,4},{12,5},{15,6},{14,7},{1,8},{0,9},... | collective-permute-start | bytes 233480 | tf_op jit(solution)/shard_map/ppermute | solution.py:201
  9.0 0.0 copy-done.4
  9.1 0.6 %shard_map.92 = (bf16[8,128,128]{2,1,0:T(8,128)(2,1)S(1)}, bf16[8,128,128]{2,1,0:T(8,128)(2,1)S(1)}) custom-call(f32[8,8,64,64]{3,2,1,0:T(8,128)S(1)} %copy-done, f32[1,8,64,64]{3,2,1,0:T(8,128)S(1)} %copy-done.4, f32[8,64,64]{2,1,0:T(8,128)S(1)} %copy-done.3, f32[8,64,128]{2,1,0:T(8,128)S(1)} %bitcast.2), custom_call_target="tpu_custom_call" | custom-call | tf_op jit(solution)/shard_map/pallas_call | solution.py:222
  9.7 0.0 collective-permute-done.1.across
  9.7 1.6 %collective-permute-start.9 = (f32[144,128]{1,0:T(8,128)S(1)}, f32[144,128]{1,0:T(8,128)S(1)}, u32[]{:S(2)}, u32[]{:S(2)}) collective-permute-start(f32[144,128]{1,0:T(8,128)S(1)} %get-tuple-element.14.beside), channel_id=1, source_target_pairs={{1,0},{5,1},{3,2},{7,3},{0,4},{9,5},{2,6},{11,7},{4,8},{13,9},{6,1... | collective-permute-start | bytes 221192 | tf_op jit(solution)/shard_map/ppermute | solution.py:201
  11.3 0.0 collective-permute-done.5.pair_beside
  11.3 0.0 collective-permute-done.4.side_beside
  11.3 0.0 collective-permute-start.7
  11.3 0.5 %collective-permute-start.8 = (f32[144,128]{1,0:T(8,128)S(1)}, f32[144,128]{1,0:T(8,128)S(1)}, u32[]{:S(2)}, u32[]{:S(2)}) collective-permute-start(f32[144,128]{1,0:T(8,128)S(1)} %collective-permute-done.4.side_beside), channel_id=1, source_target_pairs={{1,0},{0,1},{3,2},{2,3},{5,4},{4,5},{7,6},{6,7},{9,8},{8,9},{11,10... | collective-permute-start | bytes 221192 | tf_op jit(solution)/shard_map/ppermute | solution.py:201
  11.8 0.0 copy-done.6
  11.8 1.3 %shard_map.93.near = f32[8,32,128]{2,1,0:T(8,128)S(1)} custom-call(s32[8,6]{1,0:T(8,128)S(1)} %copy-done.6, f32[8,6,128,128]{3,2,1,0:T(8,128)S(1)} %copy-done.1, f32[8,32,128]{2,1,0:T(8,128)S(1)} %copy-done.5, f32[8,32,128]{2,1,0:T(8,128)S(1)} %collective-permute-done.vectors.beside, f32[8,32,128]{2,1,0:T(8,128)S(1)} %collective-permute-done.1.across), custom_call_target="tpu_custom_call" | custom-call | tf_op jit(solution)/shard_map/pallas_call | solution.py:233
  13.1 0.2 %collective-permute-done.9.third = f32[144,128]{1,0:T(8,128)S(1)} collective-permute-done((f32[144,128]{1,0:T(8,128)S(1)}, f32[144,128]{1,0:T(8,128)S(1)}, u32[]{:S(2)}, u32[]{:S(2)}) %collective-permute-start.9) | collective-permute-done | bytes 73760 | tf_op jit(solution)/shard_map/ppermute | solution.py:201
  13.2 0.0 collective-permute-done.6.own
  13.2 0.0 collective-permute-done.7.pair
  13.2 0.0 collective-permute-done.8.side
  13.3 0.0 copy-done.7
  13.3 0.0 copy-done.8
  13.3 1.1 %shard_map.94.base = f32[8,32,128]{2,1,0:T(8,128)S(1)} custom-call(s32[8,8]{1,0:T(8,128)S(1)} %copy-done.7, s32[1,8]{1,0:T(1,128)S(1)} %copy-done.8, f32[8,32,128]{2,1,0:T(8,128)S(1)} %shard_map.93.near, f32[152,128]{1,0:T(8,128)S(1)} %collective-permute-done.6.own, f32[144,128]{1,0:T(8,128)S(1)} %get-tuple-element.14.beside, ...), custom_call_target="tpu_custom_call" | custom-call | tf_op jit(solution)/shard_map/pallas_call | solution.py:242
  14.4 0.0 collective-permute-done.10.opposite
  14.4 1.0 %shard_map.95 = f32[8,32,128]{2,1,0:T(8,128)} custom-call(f32[8,32,128]{2,1,0:T(8,128)S(1)} %shard_map.94.base, f32[152,128]{1,0:T(8,128)S(1)} %collective-permute-done.10.opposite, bf16[8,128,128]{2,1,0:T(8,128)(2,1)S(1)} %get-tuple-element.21.high, bf16[8,128,128]{2,1,0:T(8,128)(2,1)S(1)} %get-tuple-element.22.low), custom_call_target="tpu_custom_call" | custom-call | tf_op jit(solution)/shard_map/pallas_call | solution.py:254
  (13 shorter events, 0.0 us)
Async XLA Ops:
  0.0 9.0 %copy-start = (f32[8,8,64,64]{3,2,1,0:T(8,128)S(1)}, f32[8,8,64,64]{3,2,1,0:T(8,128)}, u32[]{:S(2)}) copy-start(f32[8,8,64,64]{3,2,1,0:T(8,128)} %far_coupling.3) | copy-start | bytes 3145732
  0.0 9.0 %copy-start.2 = (f32[8,128,64]{1,2,0:T(8,128)S(1)}, f32[8,128,64]{1,2,0:T(8,128)}, u32[]{:S(2)}) copy-start(f32[8,128,64]{1,2,0:T(8,128)} %param.12) | copy-start | bytes 786436
  0.0 9.0 %copy-start.3 = (f32[8,64,64]{2,1,0:T(8,128)S(1)}, f32[8,64,64]{2,1,0:T(8,128)}, u32[]{:S(2)}) copy-start(f32[8,64,64]{2,1,0:T(8,128)} %transfer.3) | copy-start | bytes 393220
  0.0 9.0 %copy-start.4 = (f32[1,8,64,64]{3,2,1,0:T(8,128)S(1)}, f32[1,8,64,64]{3,2,1,0:T(8,128)}, u32[]{:S(2)}) copy-start(f32[1,8,64,64]{3,2,1,0:T(8,128)} %up_coupling.3) | copy-start | bytes 393220
  0.0 11.8 %copy-start.5 = (f32[8,32,128]{2,1,0:T(8,128)S(1)}, f32[8,32,128]{2,1,0:T(8,128)}, u32[]{:S(2)}) copy-start(f32[8,32,128]{2,1,0:T(8,128)} %own.1) | copy-start | bytes 393220
  0.0 11.8 %copy-start.6 = (s32[8,6]{1,0:T(8,128)S(1)}, s32[8,6]{1,0:T(8,128)}, u32[]{:S(2)}) copy-start(s32[8,6]{1,0:T(8,128)} %near_index.1) | copy-start | bytes 580
  0.0 3.6 %collective-permute-start.2 = (f32[8,64,128]{2,1,0:T(8,128)}, f32[8,64,128]{2,1,0:T(8,128)S(1)}, u32[]{:S(2)}, u32[]{:S(2)}) collective-permute-start(f32[8,64,128]{2,1,0:T(8,128)} %bitcast.1), channel_id=1, source_target_pairs={{1,0},{0,1},{3,2},{2,3},{5,4},{4,5},{7,6},{6,7},{9,8},{8,9},{11,10... | collective-permute-start | bytes 786440 | tf_op jit(solution)/shard_map/ppermute | solution.py:201
  0.6 3.1 %collective-permute-start = (f32[8,32,128]{2,1,0:T(8,128)}, f32[8,32,128]{2,1,0:T(8,128)S(1)}, u32[]{:S(2)}, u32[]{:S(2)}) collective-permute-start(f32[8,32,128]{2,1,0:T(8,128)} %own.1), channel_id=1, source_target_pairs={{1,0},{0,1},{3,2},{2,3},{5,4},{4,5},{7,6},{6,7},{9,8},{8,9},{11,10... | collective-permute-start | bytes 393224 | tf_op jit(solution)/shard_map/ppermute | solution.py:201
  0.6 3.0 %collective-permute-start.3 = (f32[8,64,64]{2,1,0:T(8,128)}, f32[8,64,64]{2,1,0:T(8,128)S(1)}, u32[]{:S(2)}, u32[]{:S(2)}) collective-permute-start(f32[8,64,64]{2,1,0:T(8,128)} %transfer.3), channel_id=1, source_target_pairs={{1,0},{0,1},{3,2},{2,3},{5,4},{4,5},{7,6},{6,7},{9,8},{8,9},{11,10... | collective-permute-start | bytes 393224 | tf_op jit(solution)/shard_map/ppermute | solution.py:201
  1.1 8.6 %collective-permute-start.1 = (f32[8,32,128]{2,1,0:T(8,128)}, f32[8,32,128]{2,1,0:T(8,128)S(1)}, u32[]{:S(2)}, u32[]{:S(2)}) collective-permute-start(f32[8,32,128]{2,1,0:T(8,128)} %own.1), channel_id=1, source_target_pairs={{2,1},{1,2},{4,3},{3,4},{6,5},{5,6},{8,7},{7,8},{10,9},{9,10},{12,... | collective-permute-start | bytes 393224 | tf_op jit(solution)/shard_map/ppermute | solution.py:201
  3.6 8.1 %copy-start.1 = (f32[8,6,128,128]{3,2,1,0:T(8,128)S(1)}, f32[8,6,128,128]{3,2,1,0:T(8,128)}, u32[]{:S(2)}) copy-start(f32[8,6,128,128]{3,2,1,0:T(8,128)} %near_block.1) | copy-start | bytes 9437188
  4.2 7.1 %collective-permute-start.5 = (f32[144,128]{1,0:T(8,128)S(1)}, f32[144,128]{1,0:T(8,128)S(1)}, u32[]{:S(2)}, u32[]{:S(2)}) collective-permute-start(f32[144,128]{1,0:T(8,128)S(1)} %get-tuple-element.14.beside), channel_id=1, source_target_pairs={{2,0},{3,1},{0,2},{1,3},{6,4},{7,5},{4,6},{5,7},{10,8},{11,9},{8,1... | collective-permute-start | bytes 221192 | tf_op jit(solution)/shard_map/ppermute | solution.py:201
  5.9 5.3 %collective-permute-start.4 = (f32[144,128]{1,0:T(8,128)S(1)}, f32[144,128]{1,0:T(8,128)S(1)}, u32[]{:S(2)}, u32[]{:S(2)}) collective-permute-start(f32[144,128]{1,0:T(8,128)S(1)} %get-tuple-element.14.beside), channel_id=1, source_target_pairs={{1,0},{0,1},{4,2},{5,3},{2,4},{3,5},{8,6},{9,7},{6,8},{7,9},{12,10... | collective-permute-start | bytes 221192 | tf_op jit(solution)/shard_map/ppermute | solution.py:201
  5.9 7.3 %copy-start.7 = (s32[8,8]{1,0:T(8,128)S(1)}, s32[8,8]{1,0:T(8,128)}, u32[]{:S(2)}) copy-start(s32[8,8]{1,0:T(8,128)} %far_index.1) | copy-start | bytes 772
  5.9 7.3 %copy-start.8 = (s32[1,8]{1,0:T(1,128)S(1)}, s32[1,8]{1,0:T(1,128)}, u32[]{:S(2)}) copy-start(s32[1,8]{1,0:T(1,128)} %up_index.1) | copy-start | bytes 100
  5.9 7.3 %collective-permute-start.6 = (f32[152,128]{1,0:T(8,128)S(1)}, f32[152,128]{1,0:T(8,128)S(1)}, u32[]{:S(2)}, u32[]{:S(2)}) collective-permute-start(f32[152,128]{1,0:T(8,128)S(1)} %get-tuple-element.18), channel_id=1, source_target_pairs={{1,0},{0,1},{3,2},{2,3},{5,4},{4,5},{7,6},{6,7},{9,8},{8,9},{11,10... | collective-permute-start | bytes 233480 | tf_op jit(solution)/shard_map/ppermute | solution.py:201
  6.5 7.9 %collective-permute-start.10 = (f32[152,128]{1,0:T(8,128)S(1)}, f32[152,128]{1,0:T(8,128)S(1)}, u32[]{:S(2)}, u32[]{:S(2)}) collective-permute-start(f32[152,128]{1,0:T(8,128)S(1)} %get-tuple-element.18), channel_id=1, source_target_pairs={{9,0},{8,1},{11,2},{10,3},{13,4},{12,5},{15,6},{14,7},{1,8},{0,9},... | collective-permute-start | bytes 233480 | tf_op jit(solution)/shard_map/ppermute | solution.py:201
  9.7 3.6 %collective-permute-start.9 = (f32[144,128]{1,0:T(8,128)S(1)}, f32[144,128]{1,0:T(8,128)S(1)}, u32[]{:S(2)}, u32[]{:S(2)}) collective-permute-start(f32[144,128]{1,0:T(8,128)S(1)} %get-tuple-element.14.beside), channel_id=1, source_target_pairs={{1,0},{5,1},{3,2},{7,3},{0,4},{9,5},{2,6},{11,7},{4,8},{13,9},{6,1... | collective-permute-start | bytes 221192 | tf_op jit(solution)/shard_map/ppermute | solution.py:201
  11.3 2.0 %collective-permute-start.7 = (f32[144,128]{1,0:T(8,128)S(1)}, f32[144,128]{1,0:T(8,128)S(1)}, u32[]{:S(2)}, u32[]{:S(2)}) collective-permute-start(f32[144,128]{1,0:T(8,128)S(1)} %collective-permute-done.5.pair_beside), channel_id=1, source_target_pairs={{1,0},{0,1},{3,2},{2,3},{5,4},{4,5},{7,6},{6,7},{9,8},{8,9},{11,10... | collective-permute-start | bytes 221192 | tf_op jit(solution)/shard_map/ppermute | solution.py:201
  11.3 2.0 %collective-permute-start.8 = (f32[144,128]{1,0:T(8,128)S(1)}, f32[144,128]{1,0:T(8,128)S(1)}, u32[]{:S(2)}, u32[]{:S(2)}) collective-permute-start(f32[144,128]{1,0:T(8,128)S(1)} %collective-permute-done.4.side_beside), channel_id=1, source_target_pairs={{1,0},{0,1},{3,2},{2,3},{5,4},{4,5},{7,6},{6,7},{9,8},{8,9},{11,10... | collective-permute-start | bytes 221192 | tf_op jit(solution)/shard_map/ppermute | solution.py:201

commit v8 on v7

--- a/solution.py
+++ b/solution.py
@@ -53,7 +53,7 @@
     return jnp.concatenate([x[:half], x[half:]], axis=1)
 
 
-def coeffs_kernel(vectors, basis, transfer, coeffs, longer):
+def coeffs_kernel(vectors, basis, transfer, coeffs, *longer):
     leaves, rows, points = vectors.shape
     rank = basis.shape[1]
     half = rows // 2
@@ -65,14 +65,16 @@
     for i, part in enumerate(parts):
         packed = pack(part)
         coeffs[i * half : (i + 1) * half] = packed
-        longer[i * half : (i + 1) * half] = packed
-    longer[len(parts) * half :] = jnp.zeros_like(longer[len(parts) * half :])
+        for out in longer:
+            out[i * half : (i + 1) * half] = packed
+    for out in longer:
+        out[len(parts) * half :] = jnp.zeros_like(out[len(parts) * half :])
 
 
 def place(index, here):
     differ = index ^ here
     side = (index ^ other_side_of(here)) & -2 == 0
-    return jnp.where(differ & -4 == 0, differ, jnp.where(side, 4 + (differ & 1), 6))
+    return jnp.where(differ & -4 == 0, jnp.maximum(differ - 1, 0), jnp.where(side, 3 + (differ & 1), 5))
 
 
 def other_side_of(core):
@@ -112,7 +114,7 @@
 
 
 def far_kernel(
-    far_index, up_index, near, own, beside, pair, pair_beside, side, side_beside, third,
+    far_index, up_index, near, beside, pair, pair_beside, side, side_beside, third,
     far_coupling, up_coupling, transfer, basis, base, held,
 ):
     leaves, rows, points = near.shape
@@ -122,7 +124,7 @@
     here = lax.axis_index("leaf")
     left = lax.broadcasted_iota(jnp.int32, (half, 2 * rank), 1) < rank
     left_all = lax.broadcasted_iota(jnp.int32, (rows, 2 * rank), 1) < rank
-    sources = (own, beside, pair, pair_beside, side, side_beside, third)
+    sources = (beside, pair, pair_beside, side, side_beside, third)
     for k, source in enumerate(sources):
         for i in range(leaves + 1):
             block = k * (leaves + 1) + i
@@ -204,19 +206,18 @@
     transfer_beside = send(transfer, beside_to)
     vectors_beside = send(vectors, beside_to)
     vectors_across = send(vectors, across_to)
-    theirs, theirs_longer = pl.pallas_call(
+    theirs, theirs_longer, theirs_longest = pl.pallas_call(
         coeffs_kernel,
-        out_shape=tuple(jax.ShapeDtypeStruct((packed + extra, points), F32) for extra in (0, 8)),
+        out_shape=tuple(jax.ShapeDtypeStruct((packed + extra, points), F32) for extra in (0, 8, 16)),
         in_specs=[VMEM] * 3,
-        out_specs=(VMEM, VMEM),
+        out_specs=(VMEM,) * 3,
         compiler_params=room(4),
         cost_estimate=cost(5),
     )(vectors_beside, basis_beside, transfer_beside)
     pair = send(theirs, pair_to)
     side = send(theirs, side_to)
-    opposite = send(theirs_longer, opposite_to)
-    third = send(theirs, third_to)
-    own = send(theirs_longer, beside_to)
+    opposite = send(theirs_longest, opposite_to)
+    third = send(theirs_longer, third_to)
     whole = jax.ShapeDtypeStruct(vectors.shape, F32)
     parts = jax.ShapeDtypeStruct((leaves, 2 * rank, points), jnp.bfloat16)
     high, low = pl.pallas_call(
@@ -242,13 +243,13 @@
     base = pl.pallas_call(
         far_kernel,
         out_shape=whole,
-        in_specs=[VMEM] * 14,
+        in_specs=[VMEM] * 13,
         out_specs=VMEM,
-        scratch_shapes=[pltpu.VMEM((7 * (leaves + 1), rows, points), F32)],
+        scratch_shapes=[pltpu.VMEM((6 * (leaves + 1), rows, points), F32)],
         compiler_params=room(10),
         cost_estimate=cost(0),
     )(
-        far_index, up_index, near, own, theirs, pair_beside, pair, side_beside, side, third,
+        far_index, up_index, near, theirs, pair_beside, pair, side_beside, side, third,
         far_coupling, up_coupling, transfer, basis,
     )
     return pl.pallas_call(

time: 15.5 us -> 15.8 us (1.019)
  the two profiles are of different devices: /device:TPU:0 before, /device:TPU:1 now
where the time goes in v8:
time: 15.8 us; the launch traced here: 15.6 us
  starting transfers between devices  8.49 us (54%)
  Pallas kernels  4.48 us (28%)
  waiting for transfers between devices  2.52 us (16%)
    ppermute x10, starting transfers between devices, send(): return lax.ppermute(x, ('groups', 'leaf'), to)  8.49 us
    ppermute x10, waiting for transfers between devices, send(): return lax.ppermute(x, ('groups', 'leaf'), to)  2.52 us
    pallas_call x1, Pallas kernels, per_device(): pl.pallas_call(near_kernel, out_shape=whole, in_specs=[VMEM] * 5, out_spe...  1.3 us
    pallas_call x1, Pallas kernels, per_device(): pl.pallas_call(far_kernel, out_shape=whole, in_specs=[VMEM] * 13, out_spe...  1.07 us
    pallas_call x1, Pallas kernels, per_device(): pl.pallas_call(partner_kernel, out_shape=whole, in_specs=[VMEM] * 4, out_...  0.97 us
    pallas_call x1, Pallas kernels, per_device(): pl.pallas_call(partner_matrices_kernel, out_shape=(parts, parts), in_spec...  0.59 us
    pallas_call x1, Pallas kernels, per_device(): pl.pallas_call(coeffs_kernel, out_shape=tuple((jax.ShapeDtypeStruct((pack...  0.55 us
  transfers between devices with their start and end apart: 10, of which 3 were waited for; matrix products, arithmetic and copies ran while one was open for 0% of the time, Pallas kernels for 23%

profile of v8, /device:TPU:1, one launch (start us, length us, event | category | flops | bytes accessed | tf_op | source)
XLA Modules:
  0.0 15.6 jit_solution(16143098128668528449)
XLA Ops:
  0.0 0.0 copy-start.4
  0.0 0.0 copy-start.5
  0.0 0.0 copy-start.6
  0.0 0.1 collective-permute-start.2
  0.1 0.5 %collective-permute-start = (f32[8,32,128]{2,1,0:T(8,128)}, f32[8,32,128]{2,1,0:T(8,128)S(1)}, u32[]{:S(2)}, u32[]{:S(2)}) collective-permute-start(f32[8,32,128]{2,1,0:T(8,128)} %own.1), channel_id=1, source_target_pairs={{1,0},{0,1},{3,2},{2,3},{5,4},{4,5},{7,6},{6,7},{9,8},{8,9},{11,10... | collective-permute-start | bytes 393224 | tf_op jit(solution)/shard_map/ppermute | solution.py:203
  0.6 0.1 collective-permute-start.3
  0.7 2.6 %collective-permute-start.1 = (f32[8,32,128]{2,1,0:T(8,128)}, f32[8,32,128]{2,1,0:T(8,128)S(1)}, u32[]{:S(2)}, u32[]{:S(2)}) collective-permute-start(f32[8,32,128]{2,1,0:T(8,128)} %own.1), channel_id=1, source_target_pairs={{2,1},{1,2},{4,3},{3,4},{6,5},{5,6},{8,7},{7,8},{10,9},{9,10},{12,... | collective-permute-start | bytes 393224 | tf_op jit(solution)/shard_map/ppermute | solution.py:203
  3.3 0.0 collective-permute-done.vectors.beside
  3.3 0.0 collective-permute-done.3.transfer
  3.3 0.0 collective-permute-done.2.basis
  3.3 0.0 copy-start.1
  3.3 0.5 %shard_map.91 = (f32[144,128]{1,0:T(8,128)S(1)}, f32[152,128]{1,0:T(8,128)S(1)}, f32[160,128]{1,0:T(8,128)S(1)}) custom-call(f32[8,32,128]{2,1,0:T(8,128)S(1)} %collective-permute-done.vectors.beside, f32[8,64,128]{2,1,0:T(8,128)S(1)} %collective-permute-done.2.basis, f32[8,64,64]{2,1,0:T(8,128)S(1)} %collective-permute-done.3.transfer), custom_call_target="tpu_custom_call" | custom-call | flops 2500000000 | tf_op jit(solution)/shard_map/pallas_call | solution.py:209
  3.9 1.5 %collective-permute-start.5 = (f32[144,128]{1,0:T(8,128)S(1)}, f32[144,128]{1,0:T(8,128)S(1)}, u32[]{:S(2)}, u32[]{:S(2)}) collective-permute-start(f32[144,128]{1,0:T(8,128)S(1)} %get-tuple-element.15.beside), channel_id=1, source_target_pairs={{2,0},{3,1},{0,2},{1,3},{6,4},{7,5},{4,6},{5,7},{10,8},{11,9},{8,1... | collective-permute-start | bytes 221192 | tf_op jit(solution)/shard_map/ppermute | solution.py:203
  5.3 0.7 %collective-permute-start.4 = (f32[144,128]{1,0:T(8,128)S(1)}, f32[144,128]{1,0:T(8,128)S(1)}, u32[]{:S(2)}, u32[]{:S(2)}) collective-permute-start(f32[144,128]{1,0:T(8,128)S(1)} %get-tuple-element.15.beside), channel_id=1, source_target_pairs={{1,0},{0,1},{4,2},{5,3},{2,4},{3,5},{8,6},{9,7},{6,8},{7,9},{12,10... | collective-permute-start | bytes 221192 | tf_op jit(solution)/shard_map/ppermute | solution.py:203
  6.0 2.6 %collective-permute-start.9 = (f32[160,128]{1,0:T(8,128)S(1)}, f32[160,128]{1,0:T(8,128)S(1)}, u32[]{:S(2)}, u32[]{:S(2)}) collective-permute-start(f32[160,128]{1,0:T(8,128)S(1)} %get-tuple-element.22), channel_id=1, source_target_pairs={{9,0},{8,1},{11,2},{10,3},{13,4},{12,5},{15,6},{14,7},{1,8},{0,9},... | collective-permute-start | bytes 245768 | tf_op jit(solution)/shard_map/ppermute | solution.py:203
  8.6 0.0 collective-permute-start.8
  8.6 0.0 copy-done.2
  8.6 0.0 copy-done.3
  8.6 0.0 copy-done.4
  8.6 0.6 %shard_map.92 = (bf16[8,128,128]{2,1,0:T(8,128)(2,1)S(1)}, bf16[8,128,128]{2,1,0:T(8,128)(2,1)S(1)}) custom-call(f32[8,8,64,64]{3,2,1,0:T(8,128)S(1)} %copy-done, f32[1,8,64,64]{3,2,1,0:T(8,128)S(1)} %copy-done.4, f32[8,64,64]{2,1,0:T(8,128)S(1)} %copy-done.3, f32[8,64,128]{2,1,0:T(8,128)S(1)} %bitcast.2), custom_call_target="tpu_custom_call" | custom-call | tf_op jit(solution)/shard_map/pallas_call | solution.py:223
  9.2 0.0 collective-permute-done.1.across
  9.2 0.8 %collective-permute-done.5.pair_beside = f32[144,128]{1,0:T(8,128)S(1)} collective-permute-done((f32[144,128]{1,0:T(8,128)S(1)}, f32[144,128]{1,0:T(8,128)S(1)}, u32[]{:S(2)}, u32[]{:S(2)}) %collective-permute-start.5) | collective-permute-done | bytes 73760 | tf_op jit(solution)/shard_map/ppermute | solution.py:203
  10.0 0.0 collective-permute-done.4.side_beside
  10.0 0.5 %collective-permute-start.6 = (f32[144,128]{1,0:T(8,128)S(1)}, f32[144,128]{1,0:T(8,128)S(1)}, u32[]{:S(2)}, u32[]{:S(2)}) collective-permute-start(f32[144,128]{1,0:T(8,128)S(1)} %collective-permute-done.5.pair_beside), channel_id=1, source_target_pairs={{1,0},{0,1},{3,2},{2,3},{5,4},{4,5},{7,6},{6,7},{9,8},{8,9},{11,10... | collective-permute-start | bytes 221192 | tf_op jit(solution)/shard_map/ppermute | solution.py:203
  10.5 0.0 collective-permute-start.7
  10.6 1.3 %shard_map.93.near = f32[8,32,128]{2,1,0:T(8,128)S(1)} custom-call(s32[8,6]{1,0:T(8,128)S(1)} %copy-done.6, f32[8,6,128,128]{3,2,1,0:T(8,128)S(1)} %copy-done.1, f32[8,32,128]{2,1,0:T(8,128)S(1)} %copy-done.5, f32[8,32,128]{2,1,0:T(8,128)S(1)} %collective-permute-done.vectors.beside, f32[8,32,128]{2,1,0:T(8,128)S(1)} %collective-permute-done.1.across), custom_call_target="tpu_custom_call" | custom-call | tf_op jit(solution)/shard_map/pallas_call | solution.py:234
  11.9 0.1 collective-permute-done.8.third
  12.0 0.0 collective-permute-done.6.pair
  12.0 0.0 collective-permute-done.7.side
  12.0 1.1 %shard_map.94.base = f32[8,32,128]{2,1,0:T(8,128)S(1)} custom-call(s32[8,8]{1,0:T(8,128)S(1)} %copy-done.7, s32[1,8]{1,0:T(1,128)S(1)} %copy-done.8, f32[8,32,128]{2,1,0:T(8,128)S(1)} %shard_map.93.near, f32[144,128]{1,0:T(8,128)S(1)} %get-tuple-element.15.beside, f32[144,128]{1,0:T(8,128)S(1)} %collective-permute-done.6.pair, ...), custom_call_target="tpu_custom_call" | custom-call | tf_op jit(solution)/shard_map/pallas_call | solution.py:243
  13.1 1.6 %collective-permute-done.9.opposite = f32[160,128]{1,0:T(8,128)S(1)} collective-permute-done((f32[160,128]{1,0:T(8,128)S(1)}, f32[160,128]{1,0:T(8,128)S(1)}, u32[]{:S(2)}, u32[]{:S(2)}) %collective-permute-start.9) | collective-permute-done | bytes 81952 | tf_op jit(solution)/shard_map/ppermute | solution.py:203
  14.7 1.0 %shard_map.95 = f32[8,32,128]{2,1,0:T(8,128)} custom-call(f32[8,32,128]{2,1,0:T(8,128)S(1)} %shard_map.94.base, f32[160,128]{1,0:T(8,128)S(1)} %collective-permute-done.9.opposite, bf16[8,128,128]{2,1,0:T(8,128)(2,1)S(1)} %get-tuple-element.23.high, bf16[8,128,128]{2,1,0:T(8,128)(2,1)S(1)} %get-tuple-element.24.low), custom_call_target="tpu_custom_call" | custom-call | tf_op jit(solution)/shard_map/pallas_call | solution.py:255
  (11 shorter events, 0.0 us)
Async XLA Ops:
  0.0 8.6 %copy-start = (f32[8,8,64,64]{3,2,1,0:T(8,128)S(1)}, f32[8,8,64,64]{3,2,1,0:T(8,128)}, u32[]{:S(2)}) copy-start(f32[8,8,64,64]{3,2,1,0:T(8,128)} %far_coupling.3) | copy-start | bytes 3145732
  0.0 8.6 %copy-start.2 = (f32[8,128,64]{1,2,0:T(8,128)S(1)}, f32[8,128,64]{1,2,0:T(8,128)}, u32[]{:S(2)}) copy-start(f32[8,128,64]{1,2,0:T(8,128)} %param.12) | copy-start | bytes 786436
  0.0 8.6 %copy-start.3 = (f32[8,64,64]{2,1,0:T(8,128)S(1)}, f32[8,64,64]{2,1,0:T(8,128)}, u32[]{:S(2)}) copy-start(f32[8,64,64]{2,1,0:T(8,128)} %transfer.3) | copy-start | bytes 393220
  0.0 8.6 %copy-start.4 = (f32[1,8,64,64]{3,2,1,0:T(8,128)S(1)}, f32[1,8,64,64]{3,2,1,0:T(8,128)}, u32[]{:S(2)}) copy-start(f32[1,8,64,64]{3,2,1,0:T(8,128)} %up_coupling.3) | copy-start | bytes 393220
  0.0 10.5 %copy-start.5 = (f32[8,32,128]{2,1,0:T(8,128)S(1)}, f32[8,32,128]{2,1,0:T(8,128)}, u32[]{:S(2)}) copy-start(f32[8,32,128]{2,1,0:T(8,128)} %own.1) | copy-start | bytes 393220
  0.0 10.5 %copy-start.6 = (s32[8,6]{1,0:T(8,128)S(1)}, s32[8,6]{1,0:T(8,128)}, u32[]{:S(2)}) copy-start(s32[8,6]{1,0:T(8,128)} %near_index.1) | copy-start | bytes 580
  0.0 3.3 %collective-permute-start.2 = (f32[8,64,128]{2,1,0:T(8,128)}, f32[8,64,128]{2,1,0:T(8,128)S(1)}, u32[]{:S(2)}, u32[]{:S(2)}) collective-permute-start(f32[8,64,128]{2,1,0:T(8,128)} %bitcast.1), channel_id=1, source_target_pairs={{1,0},{0,1},{3,2},{2,3},{5,4},{4,5},{7,6},{6,7},{9,8},{8,9},{11,10... | collective-permute-start | bytes 786440 | tf_op jit(solution)/shard_map/ppermute | solution.py:203
  0.1 3.2 %collective-permute-start = (f32[8,32,128]{2,1,0:T(8,128)}, f32[8,32,128]{2,1,0:T(8,128)S(1)}, u32[]{:S(2)}, u32[]{:S(2)}) collective-permute-start(f32[8,32,128]{2,1,0:T(8,128)} %own.1), channel_id=1, source_target_pairs={{1,0},{0,1},{3,2},{2,3},{5,4},{4,5},{7,6},{6,7},{9,8},{8,9},{11,10... | collective-permute-start | bytes 393224 | tf_op jit(solution)/shard_map/ppermute | solution.py:203
  0.6 2.7 %collective-permute-start.3 = (f32[8,64,64]{2,1,0:T(8,128)}, f32[8,64,64]{2,1,0:T(8,128)S(1)}, u32[]{:S(2)}, u32[]{:S(2)}) collective-permute-start(f32[8,64,64]{2,1,0:T(8,128)} %transfer.3), channel_id=1, source_target_pairs={{1,0},{0,1},{3,2},{2,3},{5,4},{4,5},{7,6},{6,7},{9,8},{8,9},{11,10... | collective-permute-start | bytes 393224 | tf_op jit(solution)/shard_map/ppermute | solution.py:203
  0.7 8.5 %collective-permute-start.1 = (f32[8,32,128]{2,1,0:T(8,128)}, f32[8,32,128]{2,1,0:T(8,128)S(1)}, u32[]{:S(2)}, u32[]{:S(2)}) collective-permute-start(f32[8,32,128]{2,1,0:T(8,128)} %own.1), channel_id=1, source_target_pairs={{2,1},{1,2},{4,3},{3,4},{6,5},{5,6},{8,7},{7,8},{10,9},{9,10},{12,... | collective-permute-start | bytes 393224 | tf_op jit(solution)/shard_map/ppermute | solution.py:203
  3.3 7.2 %copy-start.1 = (f32[8,6,128,128]{3,2,1,0:T(8,128)S(1)}, f32[8,6,128,128]{3,2,1,0:T(8,128)}, u32[]{:S(2)}) copy-start(f32[8,6,128,128]{3,2,1,0:T(8,128)} %near_block.1) | copy-start | bytes 9437188
  3.9 6.1 %collective-permute-start.5 = (f32[144,128]{1,0:T(8,128)S(1)}, f32[144,128]{1,0:T(8,128)S(1)}, u32[]{:S(2)}, u32[]{:S(2)}) collective-permute-start(f32[144,128]{1,0:T(8,128)S(1)} %get-tuple-element.15.beside), channel_id=1, source_target_pairs={{2,0},{3,1},{0,2},{1,3},{6,4},{7,5},{4,6},{5,7},{10,8},{11,9},{8,1... | collective-permute-start | bytes 221192 | tf_op jit(solution)/shard_map/ppermute | solution.py:203
  5.3 4.7 %collective-permute-start.4 = (f32[144,128]{1,0:T(8,128)S(1)}, f32[144,128]{1,0:T(8,128)S(1)}, u32[]{:S(2)}, u32[]{:S(2)}) collective-permute-start(f32[144,128]{1,0:T(8,128)S(1)} %get-tuple-element.15.beside), channel_id=1, source_target_pairs={{1,0},{0,1},{4,2},{5,3},{2,4},{3,5},{8,6},{9,7},{6,8},{7,9},{12,10... | collective-permute-start | bytes 221192 | tf_op jit(solution)/shard_map/ppermute | solution.py:203
  6.0 8.7 %collective-permute-start.9 = (f32[160,128]{1,0:T(8,128)S(1)}, f32[160,128]{1,0:T(8,128)S(1)}, u32[]{:S(2)}, u32[]{:S(2)}) collective-permute-start(f32[160,128]{1,0:T(8,128)S(1)} %get-tuple-element.22), channel_id=1, source_target_pairs={{9,0},{8,1},{11,2},{10,3},{13,4},{12,5},{15,6},{14,7},{1,8},{0,9},... | collective-permute-start | bytes 245768 | tf_op jit(solution)/shard_map/ppermute | solution.py:203
  8.6 3.4 %copy-start.7 = (s32[8,8]{1,0:T(8,128)S(1)}, s32[8,8]{1,0:T(8,128)}, u32[]{:S(2)}) copy-start(s32[8,8]{1,0:T(8,128)} %far_index.1) | copy-start | bytes 772
  8.6 3.4 %copy-start.8 = (s32[1,8]{1,0:T(1,128)S(1)}, s32[1,8]{1,0:T(1,128)}, u32[]{:S(2)}) copy-start(s32[1,8]{1,0:T(1,128)} %up_index.1) | copy-start | bytes 100
  8.6 3.4 %collective-permute-start.8 = (f32[152,128]{1,0:T(8,128)S(1)}, f32[152,128]{1,0:T(8,128)S(1)}, u32[]{:S(2)}, u32[]{:S(2)}) collective-permute-start(f32[152,128]{1,0:T(8,128)S(1)} %get-tuple-element.21), channel_id=1, source_target_pairs={{1,0},{5,1},{3,2},{7,3},{0,4},{9,5},{2,6},{11,7},{4,8},{13,9},{6,1... | collective-permute-start | bytes 233480 | tf_op jit(solution)/shard_map/ppermute | solution.py:203
  10.0 2.0 %collective-permute-start.6 = (f32[144,128]{1,0:T(8,128)S(1)}, f32[144,128]{1,0:T(8,128)S(1)}, u32[]{:S(2)}, u32[]{:S(2)}) collective-permute-start(f32[144,128]{1,0:T(8,128)S(1)} %collective-permute-done.5.pair_beside), channel_id=1, source_target_pairs={{1,0},{0,1},{3,2},{2,3},{5,4},{4,5},{7,6},{6,7},{9,8},{8,9},{11,10... | collective-permute-start | bytes 221192 | tf_op jit(solution)/shard_map/ppermute | solution.py:203
  10.5 1.5 %collective-permute-start.7 = (f32[144,128]{1,0:T(8,128)S(1)}, f32[144,128]{1,0:T(8,128)S(1)}, u32[]{:S(2)}, u32[]{:S(2)}) collective-permute-start(f32[144,128]{1,0:T(8,128)S(1)} %collective-permute-done.4.side_beside), channel_id=1, source_target_pairs={{1,0},{0,1},{3,2},{2,3},{5,4},{4,5},{7,6},{6,7},{9,8},{8,9},{11,10... | collective-permute-start | bytes 221192 | tf_op jit(solution)/shard_map/ppermute | solution.py:203

commit v9 on v8

--- a/solution.py
+++ b/solution.py
@@ -74,7 +74,7 @@
 def place(index, here):
     differ = index ^ here
     side = (index ^ other_side_of(here)) & -2 == 0
-    return jnp.where(differ & -4 == 0, jnp.maximum(differ - 1, 0), jnp.where(side, 3 + (differ & 1), 5))
+    return jnp.where(differ & -4 == 0, differ, jnp.where(side, 4 + (differ & 1), 6))
 
 
 def other_side_of(core):
@@ -114,7 +114,7 @@
 
 
 def far_kernel(
-    far_index, up_index, near, beside, pair, pair_beside, side, side_beside, third,
+    far_index, up_index, near, own, beside, pair, pair_beside, side, side_beside, third,
     far_coupling, up_coupling, transfer, basis, base, held,
 ):
     leaves, rows, points = near.shape
@@ -124,7 +124,7 @@
     here = lax.axis_index("leaf")
     left = lax.broadcasted_iota(jnp.int32, (half, 2 * rank), 1) < rank
     left_all = lax.broadcasted_iota(jnp.int32, (rows, 2 * rank), 1) < rank
-    sources = (beside, pair, pair_beside, side, side_beside, third)
+    sources = (own, beside, pair, pair_beside, side, side_beside, third)
     for k, source in enumerate(sources):
         for i in range(leaves + 1):
             block = k * (leaves + 1) + i
@@ -206,11 +206,11 @@
     transfer_beside = send(transfer, beside_to)
     vectors_beside = send(vectors, beside_to)
     vectors_across = send(vectors, across_to)
-    theirs, theirs_longer, theirs_longest = pl.pallas_call(
+    theirs, theirs_longer, theirs_longest, theirs_most = pl.pallas_call(
         coeffs_kernel,
-        out_shape=tuple(jax.ShapeDtypeStruct((packed + extra, points), F32) for extra in (0, 8, 16)),
+        out_shape=tuple(jax.ShapeDtypeStruct((packed + extra, points), F32) for extra in (0, 8, 16, 24)),
         in_specs=[VMEM] * 3,
-        out_specs=(VMEM,) * 3,
+        out_specs=(VMEM,) * 4,
         compiler_params=room(4),
         cost_estimate=cost(5),
     )(vectors_beside, basis_beside, transfer_beside)
@@ -218,6 +218,7 @@
     side = send(theirs, side_to)
     opposite = send(theirs_longest, opposite_to)
     third = send(theirs_longer, third_to)
+    own = send(theirs_most, beside_to)
     whole = jax.ShapeDtypeStruct(vectors.shape, F32)
     parts = jax.ShapeDtypeStruct((leaves, 2 * rank, points), jnp.bfloat16)
     high, low = pl.pallas_call(
@@ -243,13 +244,13 @@
     base = pl.pallas_call(
         far_kernel,
         out_shape=whole,
-        in_specs=[VMEM] * 13,
+        in_specs=[VMEM] * 14,
         out_specs=VMEM,
-        scratch_shapes=[pltpu.VMEM((6 * (leaves + 1), rows, points), F32)],
+        scratch_shapes=[pltpu.VMEM((7 * (leaves + 1), rows, points), F32)],
         compiler_params=room(10),
         cost_estimate=cost(0),
     )(
-        far_index, up_index, near, theirs, pair_beside, pair, side_beside, side, third,
+        far_index, up_index, near, own, theirs, pair_beside, pair, side_beside, side, third,
         far_coupling, up_coupling, transfer, basis,
     )
     return pl.pallas_call(

time: 15.8 us -> 15.6 us (0.987)
  waiting for transfers between devices: 2.52 us -> 0.98 us
  starting transfers between devices: 8.49 us -> 9.91 us
    ppermute x10 -> x11, waiting for transfers between devices: 2.52 us -> 0.98 us  [send(): return lax.ppermute(x, ('groups', 'leaf'), to)]
    ppermute x10 -> x11, starting transfers between devices: 8.49 us -> 9.91 us  [send(): return lax.ppermute(x, ('groups', 'leaf'), to)]
  transfers between devices with their start and end apart: 10 -> 11, of which waited for: 3 -> 3; matrix products, arithmetic and copies ran while one was open for 0% -> 0% of each run, Pallas kernels for 23% -> 23%
where the time goes in v9:
time: 15.6 us; the launch traced here: 15.5 us
  starting transfers between devices  9.91 us (64%)
  Pallas kernels  4.49 us (29%)
  waiting for transfers between devices  0.98 us (6%)
    ppermute x11, starting transfers between devices, send(): return lax.ppermute(x, ('groups', 'leaf'), to)  9.91 us
    pallas_call x1, Pallas kernels, per_device(): pl.pallas_call(near_kernel, out_shape=whole, in_specs=[VMEM] * 5, out_spe...  1.3 us
    pallas_call x1, Pallas kernels, per_device(): pl.pallas_call(far_kernel, out_shape=whole, in_specs=[VMEM] * 14, out_spe...  1.08 us
    ppermute x11, waiting for transfers between devices, send(): return lax.ppermute(x, ('groups', 'leaf'), to)  0.98 us
    pallas_call x1, Pallas kernels, per_device(): pl.pallas_call(partner_kernel, out_shape=whole, in_specs=[VMEM] * 4, out_...  0.97 us
    pallas_call x1, Pallas kernels, per_device(): pl.pallas_call(partner_matrices_kernel, out_shape=(parts, parts), in_spec...  0.59 us
    pallas_call x1, Pallas kernels, per_device(): pl.pallas_call(coeffs_kernel, out_shape=tuple((jax.ShapeDtypeStruct((pack...  0.55 us
  transfers between devices with their start and end apart: 11, of which 3 were waited for; matrix products, arithmetic and copies ran while one was open for 0% of the time, Pallas kernels for 23%

profile of v9, /device:TPU:1, one launch (start us, length us, event | category | flops | bytes accessed | tf_op | source)
XLA Modules:
  0.0 15.5 jit_solution(10916056095712150502)
XLA Ops:
  0.0 0.0 copy-start.4
  0.0 0.1 collective-permute-start.2
  0.1 0.5 %collective-permute-start = (f32[8,32,128]{2,1,0:T(8,128)}, f32[8,32,128]{2,1,0:T(8,128)S(1)}, u32[]{:S(2)}, u32[]{:S(2)}) collective-permute-start(f32[8,32,128]{2,1,0:T(8,128)} %own.1), channel_id=1, source_target_pairs={{1,0},{0,1},{3,2},{2,3},{5,4},{4,5},{7,6},{6,7},{9,8},{8,9},{11,10... | collective-permute-start | bytes 393224 | tf_op jit(solution)/shard_map/ppermute | solution.py:203
  0.6 0.1 collective-permute-start.3
  0.7 2.6 %collective-permute-start.1 = (f32[8,32,128]{2,1,0:T(8,128)}, f32[8,32,128]{2,1,0:T(8,128)S(1)}, u32[]{:S(2)}, u32[]{:S(2)}) collective-permute-start(f32[8,32,128]{2,1,0:T(8,128)} %own.1), channel_id=1, source_target_pairs={{2,1},{1,2},{4,3},{3,4},{6,5},{5,6},{8,7},{7,8},{10,9},{9,10},{12,... | collective-permute-start | bytes 393224 | tf_op jit(solution)/shard_map/ppermute | solution.py:203
  3.3 0.0 collective-permute-done.vectors.beside
  3.3 0.0 collective-permute-done.3.transfer
  3.3 0.0 collective-permute-done.2.basis
  3.3 0.5 %shard_map.91 = (f32[144,128]{1,0:T(8,128)S(1)}, f32[152,128]{1,0:T(8,128)S(1)}, f32[160,128]{1,0:T(8,128)S(1)}, f32[168,128]{1,0:T(8,128)S(1)}) custom-call(f32[8,32,128]{2,1,0:T(8,128)S(1)} %collective-permute-done.vectors.beside, f32[8,64,128]{2,1,0:T(8,128)S(1)} %collective-permute-done.2.basis, f32[8,64,64]{2,1,0:T(8,128)S(1)} %collective-permute-done.3.transfer), custom_call_target="tpu_custom_call" | custom-call | flops 2500000000 | tf_op jit(solution)/shard_map/pallas_call | solution.py:209
  3.9 1.5 %collective-permute-start.5 = (f32[144,128]{1,0:T(8,128)S(1)}, f32[144,128]{1,0:T(8,128)S(1)}, u32[]{:S(2)}, u32[]{:S(2)}) collective-permute-start(f32[144,128]{1,0:T(8,128)S(1)} %get-tuple-element.16.beside), channel_id=1, source_target_pairs={{2,0},{3,1},{0,2},{1,3},{6,4},{7,5},{4,6},{5,7},{10,8},{11,9},{8,1... | collective-permute-start | bytes 221192 | tf_op jit(solution)/shard_map/ppermute | solution.py:203
  5.3 0.7 %collective-permute-start.4 = (f32[144,128]{1,0:T(8,128)S(1)}, f32[144,128]{1,0:T(8,128)S(1)}, u32[]{:S(2)}, u32[]{:S(2)}) collective-permute-start(f32[144,128]{1,0:T(8,128)S(1)} %get-tuple-element.16.beside), channel_id=1, source_target_pairs={{1,0},{0,1},{4,2},{5,3},{2,4},{3,5},{8,6},{9,7},{6,8},{7,9},{12,10... | collective-permute-start | bytes 221192 | tf_op jit(solution)/shard_map/ppermute | solution.py:203
  6.0 0.0 collective-permute-start.6
  6.0 2.6 %collective-permute-start.10 = (f32[160,128]{1,0:T(8,128)S(1)}, f32[160,128]{1,0:T(8,128)S(1)}, u32[]{:S(2)}, u32[]{:S(2)}) collective-permute-start(f32[160,128]{1,0:T(8,128)S(1)} %get-tuple-element.24), channel_id=1, source_target_pairs={{9,0},{8,1},{11,2},{10,3},{13,4},{12,5},{15,6},{14,7},{1,8},{0,9},... | collective-permute-start | bytes 245768 | tf_op jit(solution)/shard_map/ppermute | solution.py:203
  8.6 0.0 collective-permute-done.1.across
  8.6 0.5 %collective-permute-start.9 = (f32[152,128]{1,0:T(8,128)S(1)}, f32[152,128]{1,0:T(8,128)S(1)}, u32[]{:S(2)}, u32[]{:S(2)}) collective-permute-start(f32[152,128]{1,0:T(8,128)S(1)} %get-tuple-element.23), channel_id=1, source_target_pairs={{1,0},{5,1},{3,2},{7,3},{0,4},{9,5},{2,6},{11,7},{4,8},{13,9},{6,1... | collective-permute-start | bytes 233480 | tf_op jit(solution)/shard_map/ppermute | solution.py:203
  9.1 0.0 copy-done.4
  9.1 0.6 %shard_map.92 = (bf16[8,128,128]{2,1,0:T(8,128)(2,1)S(1)}, bf16[8,128,128]{2,1,0:T(8,128)(2,1)S(1)}) custom-call(f32[8,8,64,64]{3,2,1,0:T(8,128)S(1)} %copy-done, f32[1,8,64,64]{3,2,1,0:T(8,128)S(1)} %copy-done.4, f32[8,64,64]{2,1,0:T(8,128)S(1)} %copy-done.3, f32[8,64,128]{2,1,0:T(8,128)S(1)} %bitcast.2), custom_call_target="tpu_custom_call" | custom-call | tf_op jit(solution)/shard_map/pallas_call | solution.py:224
  9.7 0.3 %collective-permute-done.5.pair_beside = f32[144,128]{1,0:T(8,128)S(1)} collective-permute-done((f32[144,128]{1,0:T(8,128)S(1)}, f32[144,128]{1,0:T(8,128)S(1)}, u32[]{:S(2)}, u32[]{:S(2)}) %collective-permute-start.5) | collective-permute-done | bytes 73760 | tf_op jit(solution)/shard_map/ppermute | solution.py:203
  10.0 0.0 collective-permute-done.4.side_beside
  10.0 1.3 %collective-permute-start.7 = (f32[144,128]{1,0:T(8,128)S(1)}, f32[144,128]{1,0:T(8,128)S(1)}, u32[]{:S(2)}, u32[]{:S(2)}) collective-permute-start(f32[144,128]{1,0:T(8,128)S(1)} %collective-permute-done.5.pair_beside), channel_id=1, source_target_pairs={{1,0},{0,1},{3,2},{2,3},{5,4},{4,5},{7,6},{6,7},{9,8},{8,9},{11,10... | collective-permute-start | bytes 221192 | tf_op jit(solution)/shard_map/ppermute | solution.py:203
  11.4 0.1 collective-permute-start.8
  11.5 0.0 copy-done.5
  11.5 1.3 %shard_map.93.near = f32[8,32,128]{2,1,0:T(8,128)S(1)} custom-call(s32[8,6]{1,0:T(8,128)S(1)} %copy-done.7, f32[8,6,128,128]{3,2,1,0:T(8,128)S(1)} %copy-done.1, f32[8,32,128]{2,1,0:T(8,128)S(1)} %copy-done.5, f32[8,32,128]{2,1,0:T(8,128)S(1)} %collective-permute-done.vectors.beside, f32[8,32,128]{2,1,0:T(8,128)S(1)} %collective-permute-done.1.across), custom_call_target="tpu_custom_call" | custom-call | tf_op jit(solution)/shard_map/pallas_call | solution.py:235
  12.8 0.4 %collective-permute-done.9.third = f32[152,128]{1,0:T(8,128)S(1)} collective-permute-done((f32[152,128]{1,0:T(8,128)S(1)}, f32[152,128]{1,0:T(8,128)S(1)}, u32[]{:S(2)}, u32[]{:S(2)}) %collective-permute-start.9) | collective-permute-done | bytes 77856 | tf_op jit(solution)/shard_map/ppermute | solution.py:203
  13.2 0.0 collective-permute-done.6.own
  13.2 0.0 collective-permute-done.7.pair
  13.2 0.0 collective-permute-done.8.side
  13.2 0.0 copy-done.6
  13.2 0.0 copy-done.8
  13.2 1.1 %shard_map.94.base = f32[8,32,128]{2,1,0:T(8,128)S(1)} custom-call(s32[8,8]{1,0:T(8,128)S(1)} %copy-done.6, s32[1,8]{1,0:T(1,128)S(1)} %copy-done.8, f32[8,32,128]{2,1,0:T(8,128)S(1)} %shard_map.93.near, f32[168,128]{1,0:T(8,128)S(1)} %collective-permute-done.6.own, f32[144,128]{1,0:T(8,128)S(1)} %get-tuple-element.16.beside, ...), custom_call_target="tpu_custom_call" | custom-call | tf_op jit(solution)/shard_map/pallas_call | solution.py:244
  14.3 0.2 %collective-permute-done.10.opposite = f32[160,128]{1,0:T(8,128)S(1)} collective-permute-done((f32[160,128]{1,0:T(8,128)S(1)}, f32[160,128]{1,0:T(8,128)S(1)}, u32[]{:S(2)}, u32[]{:S(2)}) %collective-permute-start.10) | collective-permute-done | bytes 81952 | tf_op jit(solution)/shard_map/ppermute | solution.py:203
  14.5 1.0 %shard_map.95 = f32[8,32,128]{2,1,0:T(8,128)} custom-call(f32[8,32,128]{2,1,0:T(8,128)S(1)} %shard_map.94.base, f32[160,128]{1,0:T(8,128)S(1)} %collective-permute-done.10.opposite, bf16[8,128,128]{2,1,0:T(8,128)(2,1)S(1)} %get-tuple-element.25.high, bf16[8,128,128]{2,1,0:T(8,128)(2,1)S(1)} %get-tuple-element.26.low), custom_call_target="tpu_custom_call" | custom-call | tf_op jit(solution)/shard_map/pallas_call | solution.py:256
  (13 shorter events, 0.0 us)
Async XLA Ops:
  0.0 9.1 %copy-start = (f32[8,8,64,64]{3,2,1,0:T(8,128)S(1)}, f32[8,8,64,64]{3,2,1,0:T(8,128)}, u32[]{:S(2)}) copy-start(f32[8,8,64,64]{3,2,1,0:T(8,128)} %far_coupling.3) | copy-start | bytes 3145732
  0.0 9.1 %copy-start.2 = (f32[8,128,64]{1,2,0:T(8,128)S(1)}, f32[8,128,64]{1,2,0:T(8,128)}, u32[]{:S(2)}) copy-start(f32[8,128,64]{1,2,0:T(8,128)} %param.12) | copy-start | bytes 786436
  0.0 9.1 %copy-start.3 = (f32[8,64,64]{2,1,0:T(8,128)S(1)}, f32[8,64,64]{2,1,0:T(8,128)}, u32[]{:S(2)}) copy-start(f32[8,64,64]{2,1,0:T(8,128)} %transfer.3) | copy-start | bytes 393220
  0.0 9.1 %copy-start.4 = (f32[1,8,64,64]{3,2,1,0:T(8,128)S(1)}, f32[1,8,64,64]{3,2,1,0:T(8,128)}, u32[]{:S(2)}) copy-start(f32[1,8,64,64]{3,2,1,0:T(8,128)} %up_coupling.3) | copy-start | bytes 393220
  0.0 11.4 %copy-start.5 = (f32[8,32,128]{2,1,0:T(8,128)S(1)}, f32[8,32,128]{2,1,0:T(8,128)}, u32[]{:S(2)}) copy-start(f32[8,32,128]{2,1,0:T(8,128)} %own.1) | copy-start | bytes 393220
  0.0 11.4 %copy-start.7 = (s32[8,6]{1,0:T(8,128)S(1)}, s32[8,6]{1,0:T(8,128)}, u32[]{:S(2)}) copy-start(s32[8,6]{1,0:T(8,128)} %near_index.1) | copy-start | bytes 580
  0.0 3.3 %collective-permute-start.2 = (f32[8,64,128]{2,1,0:T(8,128)}, f32[8,64,128]{2,1,0:T(8,128)S(1)}, u32[]{:S(2)}, u32[]{:S(2)}) collective-permute-start(f32[8,64,128]{2,1,0:T(8,128)} %bitcast.1), channel_id=1, source_target_pairs={{1,0},{0,1},{3,2},{2,3},{5,4},{4,5},{7,6},{6,7},{9,8},{8,9},{11,10... | collective-permute-start | bytes 786440 | tf_op jit(solution)/shard_map/ppermute | solution.py:203
  0.1 3.2 %collective-permute-start = (f32[8,32,128]{2,1,0:T(8,128)}, f32[8,32,128]{2,1,0:T(8,128)S(1)}, u32[]{:S(2)}, u32[]{:S(2)}) collective-permute-start(f32[8,32,128]{2,1,0:T(8,128)} %own.1), channel_id=1, source_target_pairs={{1,0},{0,1},{3,2},{2,3},{5,4},{4,5},{7,6},{6,7},{9,8},{8,9},{11,10... | collective-permute-start | bytes 393224 | tf_op jit(solution)/shard_map/ppermute | solution.py:203
  0.6 2.7 %collective-permute-start.3 = (f32[8,64,64]{2,1,0:T(8,128)}, f32[8,64,64]{2,1,0:T(8,128)S(1)}, u32[]{:S(2)}, u32[]{:S(2)}) collective-permute-start(f32[8,64,64]{2,1,0:T(8,128)} %transfer.3), channel_id=1, source_target_pairs={{1,0},{0,1},{3,2},{2,3},{5,4},{4,5},{7,6},{6,7},{9,8},{8,9},{11,10... | collective-permute-start | bytes 393224 | tf_op jit(solution)/shard_map/ppermute | solution.py:203
  0.7 7.9 %collective-permute-start.1 = (f32[8,32,128]{2,1,0:T(8,128)}, f32[8,32,128]{2,1,0:T(8,128)S(1)}, u32[]{:S(2)}, u32[]{:S(2)}) collective-permute-start(f32[8,32,128]{2,1,0:T(8,128)} %own.1), channel_id=1, source_target_pairs={{2,1},{1,2},{4,3},{3,4},{6,5},{5,6},{8,7},{7,8},{10,9},{9,10},{12,... | collective-permute-start | bytes 393224 | tf_op jit(solution)/shard_map/ppermute | solution.py:203
  3.3 8.1 %copy-start.1 = (f32[8,6,128,128]{3,2,1,0:T(8,128)S(1)}, f32[8,6,128,128]{3,2,1,0:T(8,128)}, u32[]{:S(2)}) copy-start(f32[8,6,128,128]{3,2,1,0:T(8,128)} %near_block.1) | copy-start | bytes 9437188
  3.9 6.1 %collective-permute-start.5 = (f32[144,128]{1,0:T(8,128)S(1)}, f32[144,128]{1,0:T(8,128)S(1)}, u32[]{:S(2)}, u32[]{:S(2)}) collective-permute-start(f32[144,128]{1,0:T(8,128)S(1)} %get-tuple-element.16.beside), channel_id=1, source_target_pairs={{2,0},{3,1},{0,2},{1,3},{6,4},{7,5},{4,6},{5,7},{10,8},{11,9},{8,1... | collective-permute-start | bytes 221192 | tf_op jit(solution)/shard_map/ppermute | solution.py:203
  5.3 4.7 %collective-permute-start.4 = (f32[144,128]{1,0:T(8,128)S(1)}, f32[144,128]{1,0:T(8,128)S(1)}, u32[]{:S(2)}, u32[]{:S(2)}) collective-permute-start(f32[144,128]{1,0:T(8,128)S(1)} %get-tuple-element.16.beside), channel_id=1, source_target_pairs={{1,0},{0,1},{4,2},{5,3},{2,4},{3,5},{8,6},{9,7},{6,8},{7,9},{12,10... | collective-permute-start | bytes 221192 | tf_op jit(solution)/shard_map/ppermute | solution.py:203
  6.0 7.2 %collective-permute-start.6 = (f32[168,128]{1,0:T(8,128)S(1)}, f32[168,128]{1,0:T(8,128)S(1)}, u32[]{:S(2)}, u32[]{:S(2)}) collective-permute-start(f32[168,128]{1,0:T(8,128)S(1)} %get-tuple-element.20), channel_id=1, source_target_pairs={{1,0},{0,1},{3,2},{2,3},{5,4},{4,5},{7,6},{6,7},{9,8},{8,9},{11,10... | collective-permute-start | bytes 258056 | tf_op jit(solution)/shard_map/ppermute | solution.py:203
  6.0 8.5 %collective-permute-start.10 = (f32[160,128]{1,0:T(8,128)S(1)}, f32[160,128]{1,0:T(8,128)S(1)}, u32[]{:S(2)}, u32[]{:S(2)}) collective-permute-start(f32[160,128]{1,0:T(8,128)S(1)} %get-tuple-element.24), channel_id=1, source_target_pairs={{9,0},{8,1},{11,2},{10,3},{13,4},{12,5},{15,6},{14,7},{1,8},{0,9},... | collective-permute-start | bytes 245768 | tf_op jit(solution)/shard_map/ppermute | solution.py:203
  8.6 4.6 %copy-start.6 = (s32[8,8]{1,0:T(8,128)S(1)}, s32[8,8]{1,0:T(8,128)}, u32[]{:S(2)}) copy-start(s32[8,8]{1,0:T(8,128)} %far_index.1) | copy-start | bytes 772
  8.6 4.6 %copy-start.8 = (s32[1,8]{1,0:T(1,128)S(1)}, s32[1,8]{1,0:T(1,128)}, u32[]{:S(2)}) copy-start(s32[1,8]{1,0:T(1,128)} %up_index.1) | copy-start | bytes 100
  8.6 4.6 %collective-permute-start.9 = (f32[152,128]{1,0:T(8,128)S(1)}, f32[152,128]{1,0:T(8,128)S(1)}, u32[]{:S(2)}, u32[]{:S(2)}) collective-permute-start(f32[152,128]{1,0:T(8,128)S(1)} %get-tuple-element.23), channel_id=1, source_target_pairs={{1,0},{5,1},{3,2},{7,3},{0,4},{9,5},{2,6},{11,7},{4,8},{13,9},{6,1... | collective-permute-start | bytes 233480 | tf_op jit(solution)/shard_map/ppermute | solution.py:203
  10.0 3.1 %collective-permute-start.7 = (f32[144,128]{1,0:T(8,128)S(1)}, f32[144,128]{1,0:T(8,128)S(1)}, u32[]{:S(2)}, u32[]{:S(2)}) collective-permute-start(f32[144,128]{1,0:T(8,128)S(1)} %collective-permute-done.5.pair_beside), channel_id=1, source_target_pairs={{1,0},{0,1},{3,2},{2,3},{5,4},{4,5},{7,6},{6,7},{9,8},{8,9},{11,10... | collective-permute-start | bytes 221192 | tf_op jit(solution)/shard_map/ppermute | solution.py:203
  11.4 1.8 %collective-permute-start.8 = (f32[144,128]{1,0:T(8,128)S(1)}, f32[144,128]{1,0:T(8,128)S(1)}, u32[]{:S(2)}, u32[]{:S(2)}) collective-permute-start(f32[144,128]{1,0:T(8,128)S(1)} %collective-permute-done.4.side_beside), channel_id=1, source_target_pairs={{1,0},{0,1},{3,2},{2,3},{5,4},{4,5},{7,6},{6,7},{9,8},{8,9},{11,10... | collective-permute-start | bytes 221192 | tf_op jit(solution)/shard_map/ppermute | solution.py:203
